TPU v7x, 128 devices: a whole 4x4x4 slice. The times are simulated.
128 devices in a mesh: fsdp: 4 (over z), dp: 4 (over y_hi, core), outer: 8 (over x, y_lo).
Axes of the slice: x: 4, y: 4 (y_hi: 2, y_lo: 2; y = y_hi * 2 + y_lo), z: 4, core: 2. Of those that a mesh axis runs over, the one named last changes fastest.
Arguments:
- grad_parts: bfloat16 [8, 4, 4, 8192, 512], P('outer', 'fsdp', 'dp'), may hold values from -6 to 6
- momentum: float32 [8, 8192, 512], P('outer', ('fsdp', 'dp')), may hold values from -6 to 6
- params: float32 [8192, 512], P(('fsdp', 'dp')), may hold values from -6 to 6
- band: int32 [256], replicated, may hold values from 0 to 4095, as said below
Outputs:
- new_momentum: float32 [8, 8192, 512], P('outer', ('fsdp', 'dp'))
- new_params: float32 [8192, 512], P('fsdp')
Inputs may be any that keep to these rules, and one draw needn't show every extreme that they name: `band`: 256 distinct positions, each vertical frequency times 64 plus horizontal frequency.
All inputs are finite; a program needn't handle non-finite values.
Results may differ from a plain program's by a relative error of at most 0.0003.
Values sent between devices are 32-bit elements; how exact they have to be, the bound alone decides.
No kernel may reach another device: no remote copies, remote signals or barrier semaphores. Data moves between devices by JAX's collectives and lax.ppermute only.
A program may use at most 192 MiB of HBM per device.

v0:
```python
import jax
import jax.numpy as jnp
from jax import lax
from jax.sharding import PartitionSpec as P

GROUP = 64


beta = 0.9


def dct_table():
    freq = jnp.arange(GROUP, dtype=jnp.float32)[:, None]
    place = jnp.arange(GROUP, dtype=jnp.float32)[None, :]
    scale = jnp.where(freq == 0, jnp.sqrt(1.0 / GROUP), jnp.sqrt(2.0 / GROUP)).astype(jnp.float32)
    return scale * jnp.cos(jnp.pi * (2.0 * place + 1.0) * freq / (2.0 * GROUP))


def encode(field, table):
    rows, cols = field.shape
    blocks = field.reshape(rows // GROUP, GROUP, cols // GROUP, GROUP)
    half = jnp.einsum("km,ambn->akbn", table, blocks, precision=lax.Precision.HIGHEST)
    coeff = jnp.einsum("akbn,ln->abkl", half, table, precision=lax.Precision.HIGHEST)
    return coeff.reshape(rows // GROUP, cols // GROUP, GROUP * GROUP)


def decode(shared, band, table):
    nrow, ncol = (shared.shape[0], shared.shape[1])
    placed = jnp.zeros((nrow, ncol, GROUP * GROUP), jnp.float32).at[:, :, band].set(shared)
    placed = placed.reshape(nrow, ncol, GROUP, GROUP)
    half = jnp.einsum("km,abkl->ambl", table, placed, precision=lax.Precision.HIGHEST)
    field = jnp.einsum("ambl,ln->ambn", half, table, precision=lax.Precision.HIGHEST)
    return field.reshape(nrow * GROUP, ncol * GROUP)


def local(grad_parts, momentum, params, band):
    table = dct_table()
    partial_value = grad_parts.reshape(grad_parts.shape[3], grad_parts.shape[4]).astype(jnp.float32)
    summed = lax.psum_scatter(partial_value, ("fsdp", "dp"), scatter_dimension=0, tiled=True)
    grad = summed * (1.0 / (lax.axis_size("fsdp") * lax.axis_size("dp")))
    mom = beta * momentum[0] + grad
    coeff = encode(mom, table)
    shared = coeff[:, :, band]
    total = lax.psum(shared, "outer")
    new_momentum = mom - decode(shared, band, table)
    updated = params - decode(total * (1.0 / lax.axis_size("outer")), band, table)
    new_params = lax.all_gather(updated, "dp", axis=0, tiled=True)
    return (new_momentum[None], new_params)


def solution(mesh):
    return jax.shard_map(
        local,
        mesh=mesh,
        in_specs=(
            P("outer", "fsdp", "dp", None, None),
            P("outer", ("fsdp", "dp"), None),
            P(("fsdp", "dp"), None),
            P(),
        ),
        out_specs=(P("outer", ("fsdp", "dp"), None), P("fsdp", None)),
        check_vma=False,
    )
```

profile of v0, /device:TPU:1, one launch (start us, length us, event | category | flops | bytes accessed | tf_op | source)
XLA Modules:
  0.0 415.6 jit_solution(6368548868409508349)
XLA Ops:
  7.2 11.5 %bitcast_convert_fusion = f32[8192,512]{1,0:T(8,128)} fusion(bf16[1,1,1,8192,512]{4,3,2,1,0:T(8,128)(2,1)} %param.4), kind=kLoop, calls=%fused_computation.3 | loop fusion | flops 4194304 | bytes 25165824 | tf_op jit(solution)/shard_map/convert_element_type | solution.py:38
  19.4 149.0 %reduce-scatter.2.cloned.1.call-done = f32[512,512]{1,0:T(8,128)} async-done(((f32[8192,512]{1,0:T(8,128)}), f32[512,512]{1,0:T(8,128)}) %reduce-scatter.2.cloned.1.call-update) | async-done | bytes 1048592 | tf_op jit(solution)/shard_map/reduce_scatter | solution.py:39
  168.5 1.5 bitcast_add_fusion
  170.4 2.3 fusion.6
  172.7 6.1 %fusion.8 = f32[8,8,64,64]{2,3,1,0:T(8,128)S(1)} fusion(f32[8,8,64,64]{2,3,1,0:T(8,128)S(1)} %fusion.6, f32[64]{0:T(128)S(1)} %get-tuple-element.3, f32[64]{0:T(128)S(1)} %get-tuple-element.2), kind=kOutput, calls=%fused_computation.12 | convolution fusion | flops 201338880 | bytes 2097664 | tf_op jit(solution)/shard_map/akbn,ln->abkl/dot_general | solution.py:23
  178.8 13.6 %copy.14 = f32[8,8,64,64]{1,0,3,2:T(8,128)} copy(f32[8,8,64,64]{2,3,1,0:T(8,128)S(1)} %fusion.8) | data formatting | bytes 2097152 | tf_op jit(solution)/shard_map/reshape | solution.py:24
  192.4 6.5 %gather_fusion = f32[256,8,8]{2,1,0:T(8,128)S(1)} fusion(f32[8,8,4096]{1,0,2:T(8,128)} %bitcast.51, s32[1024]{0:T(1024)S(1)} %pad_clamp_fusion), kind=kCustom, calls=%fused_computation | custom fusion | bytes 132096 | tf_op jit(solution)/shard_map/gather | solution.py:43
  198.9 6.2 %broadcast.42.clone = f32[8,8,4096]{1,0,2:T(8,128)} broadcast(f32[]{:T(128)} %constant.1.clone.1), dimensions={} | broadcast | bytes 1048580 | tf_op jit(solution)/shard_map/broadcast.3
  205.1 24.0 %scatter_fusion = f32[8,8,4096]{1,0,2:T(8,128)} fusion(f32[8,8,4096]{1,0,2:T(8,128)} %broadcast.42.clone, s32[256]{0:T(256)S(1)} %compare_select_fusion, f32[256,8,8]{2,1,0:T(8,128)S(1)} %gather_fusion), kind=kCustom, calls=%fused_computation.1 | custom fusion | bytes 197632 | tf_op jit(solution)/shard_map/scatter | solution.py:29
  230.0 74.5 %all-reduce.2.cloned.1.call-done = f32[8,8,256]{1,0,2:T(8,128)} async-done(((f32[8,8,256]{1,0,2:T(8,128)}), f32[8,8,256]{1,0,2:T(8,128)}) %all-reduce.2.cloned.1.call-update) | async-done | bytes 65552 | tf_op jit(solution)/shard_map/psum | solution.py:44
  305.9 6.0 %broadcast.42 = f32[8,8,4096]{1,0,2:T(8,128)} broadcast(f32[]{:T(128)} %constant.1.clone.1), dimensions={} | broadcast | bytes 1048580 | tf_op jit(solution)/shard_map/broadcast.3
  311.8 23.8 %scatter_fusion.1 = f32[8,8,4096]{1,0,2:T(8,128)} fusion(f32[8,8,4096]{1,0,2:T(8,128)} %broadcast.42, s32[256]{0:T(256)S(1)} %compare_select_fusion, f32[256,8,8]{2,1,0:T(8,128)S(1)} %multiply_bitcast_fusion), kind=kCustom, calls=%fused_computation.2 | custom fusion | bytes 197632 | tf_op jit(solution)/shard_map/scatter | solution.py:29
  335.7 12.0 %copy.13 = f32[8,8,64,64]{2,3,1,0:T(8,128)S(1)} copy(f32[8,8,64,64]{1,0,3,2:T(8,128)} %bitcast.49) | data formatting | bytes 2097152 | tf_op jit(solution)/shard_map/reshape | solution.py:30
  347.7 6.2 %fusion.12 = f32[8,8,64,64]{2,3,1,0:T(8,128)S(1)} fusion(f32[8,8,64,64]{2,3,1,0:T(8,128)S(1)} %copy.13, f32[64]{0:T(128)S(1)} %get-tuple-element.3, f32[64]{0:T(128)S(1)} %get-tuple-element.2), kind=kOutput, calls=%fused_computation.17 | convolution fusion | flops 201338880 | bytes 2097664 | tf_op jit(solution)/shard_map/km,abkl->ambl/dot_general | solution.py:31
  353.9 2.0 fusion
  357.1 1.5 reshape.48
  358.6 2.7 sub.7
  361.3 12.2 %copy.12 = f32[8,8,64,64]{2,3,1,0:T(8,128)S(1)} copy(f32[8,8,64,64]{1,0,3,2:T(8,128)} %bitcast.50) | data formatting | bytes 2097152 | tf_op jit(solution)/shard_map/reshape | solution.py:30
  373.6 6.2 %fusion.15 = f32[8,8,64,64]{2,3,1,0:T(8,128)S(1)} fusion(f32[8,8,64,64]{2,3,1,0:T(8,128)S(1)} %copy.12, f32[64]{0:T(128)S(1)} %get-tuple-element.3, f32[64]{0:T(128)S(1)} %get-tuple-element.2), kind=kOutput, calls=%fused_computation.20 | convolution fusion | flops 201338880 | bytes 2097664 | tf_op jit(solution)/shard_map/km,abkl->ambl/dot_general | solution.py:31
  379.8 2.0 fusion.2
  383.0 1.5 reshape.46
  384.4 2.4 subtract_bitcast_fusion
  386.8 17.6 %all-gather.2.cloned.1.call-done = f32[2048,512]{1,0:T(8,128)} async-done(((f32[512,512]{1,0:T(8,128)}), f32[2048,512]{1,0:T(8,128)}) %all-gather.2.cloned.1.call-update) | async-done | bytes 4194320 | tf_op jit(solution)/shard_map/all_gather | solution.py:47
  404.4 4.6 %copy.22 = f32[2048,512]{1,0:T(8,128)} copy(f32[2048,512]{1,0:T(8,128)} %all-gather.2.cloned.1.call-done) | data formatting | bytes 8388608
  (19 shorter events, 5.8 us)
Async XLA Ops:
  7.2 161.3 %reduce-scatter.2.cloned.1.call-start = ((), (), s32[]{:S(2)}) async-start(), calls=%async_computation.1 | async-start | bytes 17825792 | tf_op jit(solution)/shard_map/reduce_scatter | solution.py:39
  18.7 0.7 copy-start.2
  18.7 149.7 %copy-start.1 = (f32[1,512,512]{2,1,0:T(8,128)S(1)}, f32[1,512,512]{2,1,0:T(8,128)}, u32[]{:S(2)}) copy-start(f32[1,512,512]{2,1,0:T(8,128)} %param.5) | copy-start | bytes 3145732
  198.9 6.2 %copy-start = (f32[256,8,8]{2,1,0:T(8,128)}, f32[256,8,8]{2,1,0:T(8,128)S(1)}, u32[]{:S(2)}) copy-start(f32[256,8,8]{2,1,0:T(8,128)S(1)} %gather_fusion) | copy-start | bytes 196612
  229.1 75.5 %all-reduce.2.cloned.1.call-start = ((), (), s32[]{:S(2)}) async-start(), calls=%async_computation.2 | async-start | bytes 2097152 | tf_op jit(solution)/shard_map/psum | solution.py:44
  229.8 174.6 %all-gather.2.cloned.1.call-start = ((), (), s32[]{:S(2)}) async-start(), calls=%async_computation.3 | async-start | bytes 5242880 | tf_op jit(solution)/shard_map/all_gather | solution.py:47
Sparse Core Ops, SparseCore 0:
  18.9 149.5 reduce-scatter.1
  233.0 71.5 all-reduce.1
  361.4 42.9 all-gather.1
where the time goes:
time: 417 us; the launch traced here: 416 us
  waiting for transfers between devices  242 us (58%)
  local copies, waits for them, and re-layouts  115 us (28%)
  matrix products  24.8 us (6%)
  other arithmetic  19.4 us (5%)
  between operations  13.8 us (3%)
    reduce_scatter x1, waiting for transfers between devices, local(): lax.psum_scatter(partial_value, ('fsdp', 'dp'), scatter_dimension=0, tile...  149 us
    psum x1, waiting for transfers between devices, local(): total = lax.psum(shared, 'outer')  74.5 us
    scatter x2, local copies, waits for them, and re-layouts, decode(): jnp.zeros((nrow, ncol, GROUP * GROUP), jnp.float32).at[:, :, band]  47.8 us
    reshape x2, local copies, waits for them, and re-layouts, decode(): placed = placed.reshape(nrow, ncol, GROUP, GROUP)  24.3 us
    all_gather x1, waiting for transfers between devices, local(): new_params = lax.all_gather(updated, 'dp', axis=0, tiled=True)  17.6 us
    reshape x1, local copies, waits for them, and re-layouts, encode(): return coeff.reshape(rows // GROUP, cols // GROUP, GROUP * GROUP)  13.6 us
    dot_general x2, matrix products, decode(): jnp.einsum('km,abkl->ambl', table, placed, precision=lax.Precision.HIGHEST)  12.4 us
    another operation x2, local copies, waits for them, and re-layouts  12.2 us
  transfers between devices with their start and end apart: 3, of which 3 were waited for; matrix products, arithmetic and copies ran while one was open for 6% of the time, Pallas kernels for 0%

commit v1 on v0

v1 whole, which is shorter than its diff:
```python
import jax
import jax.numpy as jnp
from jax import lax
from jax.experimental import pallas as pl
from jax.experimental.pallas import tpu as pltpu
from jax.sharding import PartitionSpec as P

GROUP = 64
BAND = 256
COLS = 512
NB = COLS // GROUP
OWN = 512
AXES = ("fsdp", "dp", "outer")
beta = 0.9

F32 = jnp.float32
BF16 = jnp.bfloat16


def place(x, y, z, core):
    return z * 32 + ((y // 2) * 2 + core) * 8 + x * 2 + y % 2


def swap(value, x=0, y=0, z=0, core=0):
    pairs = []
    for px in range(4):
        for py in range(4):
            for pz in range(4):
                for pc in range(2):
                    pairs.append((place(px, py, pz, pc), place(px ^ x, py ^ y, (pz + z) % 4, pc ^ core)))
    return lax.ppermute(value, AXES, pairs)


def cosine_columns(freq):
    freq = freq.astype(F32)[None, :]
    pos = jnp.arange(GROUP, dtype=F32)[:, None]
    scale = jnp.where(freq == 0, jnp.sqrt(1.0 / GROUP), jnp.sqrt(2.0 / GROUP)).astype(F32)
    return scale * jnp.cos(jnp.pi * (2.0 * pos + 1.0) * freq / (2.0 * GROUP))


def split(value):
    high = value.astype(BF16)
    return high, (value - high.astype(F32)).astype(BF16)


def dot(a, b):
    return jnp.dot(a, b, preferred_element_type=F32)


def mom_kernel(grad_ref, momentum_ref, vert_ref, horiz_ref, mom_ref, shared_ref):
    rows = grad_ref.shape[0]
    mom = beta * momentum_ref[...] + grad_ref[...] * (1.0 / 16.0)
    mom_ref[...] = mom
    vert = vert_ref[...][None]
    w_high, w_low = split(horiz_ref[...])
    x_high, x_low = split(mom)
    for b in range(NB):
        cut = slice(b * GROUP, (b + 1) * GROUP)
        half = dot(x_high[:, cut], w_high) + dot(x_low[:, cut], w_high) + dot(x_high[:, cut], w_low)
        half = half.reshape(rows // GROUP, GROUP, BAND)
        shared_ref[:, b, :] = jnp.sum(half * vert, axis=1)


def take_out(field, coeff, vert, w_both):
    rows = field.shape[0]
    out = []
    for b in range(NB):
        wide = coeff[:, b, :][:, None, :] * vert[None]
        high, low = split(wide.reshape(rows, BAND))
        both = dot(high, w_both)
        out.append(both[:, :GROUP] + both[:, GROUP:] + dot(low, w_both[:, :GROUP]))
    return field - jnp.concatenate(out, axis=1)


def residual_kernel(mom_ref, shared_ref, vert_ref, horiz_t_ref, out_ref):
    high, low = split(horiz_t_ref[...])
    w_both = jnp.concatenate([high, low], axis=1)
    out_ref[...] = take_out(mom_ref[...], shared_ref[...], vert_ref[...], w_both)


def update_kernel(at_ref, params_ref, total_ref, vert_ref, horiz_t_ref, out_ref):
    high, low = split(horiz_t_ref[...])
    w_both = jnp.concatenate([high, low], axis=1)
    out_ref[...] = take_out(params_ref[...], total_ref[0] * (1.0 / 8.0), vert_ref[...], w_both)


def full(shape):
    return pl.BlockSpec(shape, lambda *_: (0,) * len(shape))


def mom_call(grad, momentum, vert, horiz):
    rows = 128
    return pl.pallas_call(
        mom_kernel,
        grid=(OWN // rows,),
        in_specs=[
            pl.BlockSpec((rows, COLS), lambda i: (i, 0)),
            pl.BlockSpec((rows, COLS), lambda i: (i, 0)),
            full((GROUP, BAND)),
            full((GROUP, BAND)),
        ],
        out_specs=[
            pl.BlockSpec((rows, COLS), lambda i: (i, 0)),
            pl.BlockSpec((rows // GROUP, NB, BAND), lambda i: (i, 0, 0)),
        ],
        out_shape=[
            jax.ShapeDtypeStruct((OWN, COLS), F32),
            jax.ShapeDtypeStruct((OWN // GROUP, NB, BAND), F32),
        ],
        name="momentum_encode",
    )(grad, momentum, vert, horiz)


def residual_call(mom, shared, vert, horiz_t):
    rows = 128
    return pl.pallas_call(
        residual_kernel,
        grid=(OWN // rows,),
        in_specs=[
            pl.BlockSpec((rows, COLS), lambda i: (i, 0)),
            pl.BlockSpec((rows // GROUP, NB, BAND), lambda i: (i, 0, 0)),
            full((GROUP, BAND)),
            full((BAND, GROUP)),
        ],
        out_specs=pl.BlockSpec((rows, COLS), lambda i: (i, 0)),
        out_shape=jax.ShapeDtypeStruct((OWN, COLS), F32),
        cost_estimate=pl.CostEstimate(flops=2 * 10**9, bytes_accessed=2 * 2**20, transcendentals=0),
        name="momentum_residual",
    )(mom, shared, vert, horiz_t)


def update_call(which, params, total, vert, horiz_t):
    rows = 256
    per = OWN // rows
    return pl.pallas_call(
        update_kernel,
        grid_spec=pltpu.PrefetchScalarGridSpec(
            num_scalar_prefetch=1,
            grid=(4, per),
            in_specs=[
                pl.BlockSpec((rows, COLS), lambda i, r, at: (i * per + r, 0)),
                pl.BlockSpec((1, rows // GROUP, NB, BAND), lambda i, r, at: (i, r, 0, 0)),
                full((GROUP, BAND)),
                full((BAND, GROUP)),
            ],
            out_specs=pl.BlockSpec((rows, COLS), lambda i, r, at: (at[i] * per + r, 0)),
        ),
        out_shape=jax.ShapeDtypeStruct((4 * OWN, COLS), F32),
        name="parameter_update",
    )(which, params, total, vert, horiz_t)


def local(grad_parts, momentum, params, band):
    dp = lax.axis_index("dp")
    band = band.astype(jnp.int32)
    vert = cosine_columns(band // GROUP)
    horiz = cosine_columns(band % GROUP)
    horiz_t = horiz.T

    partial_value = grad_parts.reshape(grad_parts.shape[3], grad_parts.shape[4]).astype(F32)
    summed = lax.psum_scatter(partial_value, ("fsdp", "dp"), scatter_dimension=0, tiled=True)

    far = swap(params, y=3)
    both = jnp.concatenate([params, far], axis=0)
    near = swap(both, core=1)
    every = jnp.concatenate([params, near[:OWN], far, near[OWN:]], axis=0)

    mom, shared = mom_call(summed, momentum[0], vert, horiz)
    new_momentum = residual_call(mom, shared, vert, horiz_t)

    total = (shared + swap(shared, x=1)) + (swap(shared, x=2) + swap(shared, x=3))
    here = total + swap(total, y=1)
    there = swap(total, y=2) + swap(total, y=3)
    pair = jnp.stack([here, there])
    other = swap(pair, core=1)
    totals = jnp.stack([pair[0], other[0], pair[1], other[1]])
    which = dp ^ jnp.arange(4, dtype=jnp.int32)
    new_params = update_call(which, every, totals, vert, horiz_t)
    return (new_momentum[None], new_params)


def solution(mesh):
    return jax.shard_map(
        local,
        mesh=mesh,
        in_specs=(
            P("outer", "fsdp", "dp", None, None),
            P("outer", ("fsdp", "dp"), None),
            P(("fsdp", "dp"), None),
            P(),
        ),
        out_specs=(P("outer", ("fsdp", "dp"), None), P("fsdp", None)),
        check_vma=False,
    )
```

time: 417 us -> 220 us (0.53)
  local copies, waits for them, and re-layouts: 115 us -> 2.93 us
  waiting for transfers between devices: 242 us -> 146 us
  matrix products: 24.8 us -> 0 us
  Pallas kernels: 0 us -> 20.5 us
  starting transfers between devices: 0.26 us -> 17 us
    psum x1 -> x0, waiting for transfers between devices: 74.5 us -> none  [local(): total = lax.psum(shared, 'outer')]
    scatter x2 -> x0, local copies, waits for them, and re-layouts: 47.8 us -> none  [decode(): jnp.zeros((nrow, ncol, GROUP * GROUP), jnp.float32).at[:, :, band]]
    reshape x6 -> x0, local copies, waits for them, and re-layouts: 41.2 us -> none  [the longest x2 24.3 us: decode(): placed = placed.reshape(nrow, ncol, GROUP, GROUP)]
    reduce_scatter x1, waiting for transfers between devices: 149 us -> 119 us  [local(): lax.psum_scatter(partial_value, ('fsdp', 'dp'), scatter_dimension=0, tile...]
    ppermute x0 -> x9, waiting for transfers between devices: none -> 27.2 us  [swap(): return lax.ppermute(value, AXES, pairs)]
    dot_general x6 -> x0, matrix products: 24.8 us -> none  [the longest x2 12.4 us: decode(): jnp.einsum('km,abkl->ambl', table, placed, precision=lax.Precision.HIGHEST)]
    pallas_call x0 -> x3, Pallas kernels: none -> 20.5 us  [the longest x1 11.1 us: update_call(): pl.pallas_call(update_kernel, grid_spec=pltpu.PrefetchScalarGridSpec(num_...]
    all_gather x1 -> x0, waiting for transfers between devices: 17.6 us -> none  [local(): new_params = lax.all_gather(updated, 'dp', axis=0, tiled=True)]
  transfers between devices with their start and end apart: 3 -> 10, of which waited for: 3 -> 5; matrix products, arithmetic and copies ran while one was open for 6% -> 4% of each run, Pallas kernels for 0% -> 4%
where the time goes in v1:
time: 220 us
  waiting for transfers between devices  146 us (66%)
  Pallas kernels  20.5 us (9%)
  other arithmetic  19.1 us (9%)
  starting transfers between devices  17 us (8%)
  between operations  14.1 us (6%)
  local copies, waits for them, and re-layouts  2.93 us (1%)
    reduce_scatter x1, waiting for transfers between devices, local(): lax.psum_scatter(partial_value, ('fsdp', 'dp'), scatter_dimension=0, tile...  119 us
    ppermute x9, waiting for transfers between devices, swap(): return lax.ppermute(value, AXES, pairs)  27.2 us
    ppermute x9, starting transfers between devices, swap(): return lax.ppermute(value, AXES, pairs)  17 us
    convert_element_type x1, other arithmetic, local(): grad_parts.reshape(grad_parts.shape[3], grad_parts.shape[4]).astype(F32)  11.5 us
    pallas_call x1, Pallas kernels, update_call(): pl.pallas_call(update_kernel, grid_spec=pltpu.PrefetchScalarGridSpec(num_...  11.1 us
    pallas_call x1, Pallas kernels, residual_call(): pl.pallas_call(residual_kernel, grid=(OWN // rows,), in_specs=[pl.BlockSp...  4.78 us
    pallas_call x1, Pallas kernels, mom_call(): pl.pallas_call(mom_kernel, grid=(OWN // rows,), in_specs=[pl.BlockSpec((r...  4.6 us
  transfers between devices with their start and end apart: 10, of which 5 were waited for; matrix products, arithmetic and copies ran while one was open for 4% of the time, Pallas kernels for 4%

profile of v1, /device:TPU:1, one launch (start us, length us, event | category | flops | bytes accessed | tf_op | source)
XLA Modules:
  0.0 219.9 jit_solution(9948113979269837030)
XLA Ops:
  7.2 11.5 %bitcast_convert_fusion = f32[8192,512]{1,0:T(8,128)} fusion(bf16[1,1,1,8192,512]{4,3,2,1,0:T(8,128)(2,1)} %param.4), kind=kLoop, calls=%fused_computation | loop fusion | flops 4194304 | bytes 25165824 | tf_op jit(solution)/shard_map/convert_element_type | solution.py:160
  18.8 1.2 copy-done
  20.0 3.6 %collective-permute-start = (f32[512,512]{1,0:T(8,128)S(1)}, f32[512,512]{1,0:T(8,128)S(1)}, u32[]{:S(2)}, u32[]{:S(2)}) collective-permute-start(f32[512,512]{1,0:T(8,128)S(1)} %copy-done), channel_id=1, source_target_pairs={{0,17},{8,25},{32,49},{40,57},{64,81},{72,89},{96,113},{104,121},{... | collective-permute-start | bytes 3145736 | tf_op jit(solution)/shard_map/ppermute | solution.py:31
  23.5 22.7 %collective-permute-done = f32[512,512]{1,0:T(8,128)S(1)} collective-permute-done((f32[512,512]{1,0:T(8,128)S(1)}, f32[512,512]{1,0:T(8,128)S(1)}, u32[]{:S(2)}, u32[]{:S(2)}) %collective-permute-start) | collective-permute-done | bytes 1048608 | tf_op jit(solution)/shard_map/ppermute | solution.py:31
  46.3 1.5 pad_maximum_fusion.1
  47.8 1.4 collective-permute-start.1
  49.2 0.6 iota_xor_fusion.at_ref
  49.8 1.2 cosine_multiply_fusion.horiz_t_ref
  50.9 1.1 cosine_multiply_fusion.1
  52.1 119.1 %reduce-scatter.2.cloned.1.call-done.grad_ref = f32[512,512]{1,0:T(8,128)} async-done(((f32[8192,512]{1,0:T(8,128)}), f32[512,512]{1,0:T(8,128)}) %reduce-scatter.2.cloned.1.call-update) | async-done | bytes 1048592 | tf_op jit(solution)/shard_map/reduce_scatter | solution.py:161
  171.1 4.6 %momentum_encode.1 = (f32[512,512]{1,0:T(8,128)}, f32[8,8,256]{2,1,0:T(8,128)}) custom-call(f32[512,512]{1,0:T(8,128)} %reduce-scatter.2.cloned.1.call-done.grad_ref, f32[512,512]{1,0:T(8,128)} %bitcast.9, f32[64,256]{1,0:T(8,128)} %get-tuple-element.17.vert_ref, f32[64,256]{1,0:T(8,128)} %get-tuple-element.16.horiz_ref), custom_call_target="tpu_custom_call" | custom-call | tf_op jit(solution)/shard_map/momentum_encode/pallas_call | solution.py:93
  175.7 2.7 %collective-permute-start.3 = (f32[8,8,256]{2,1,0:T(8,128)}, f32[8,8,256]{2,1,0:T(8,128)S(1)}, u32[]{:S(2)}, u32[]{:S(2)}) collective-permute-start(f32[8,8,256]{2,1,0:T(8,128)} %get-tuple-element.5.shared_ref), channel_id=1, source_target_pairs={{0,4},{8,12},{32,36},{40,44},{64,68},{72,76},{96,100},{104,108},{1... | collective-permute-start | bytes 196616 | tf_op jit(solution)/shard_map/ppermute | solution.py:31
  178.5 0.9 collective-permute-start.4
  179.4 1.7 fusion.4
  181.1 1.9 collective-permute-done.4
  183.4 2.4 %pad_maximum_fusion.params_ref = f32[2048,512]{1,0:T(8,128)} fusion(f32[512,512]{1,0:T(8,128)S(1)} %get-tuple-element.11, f32[512,512]{1,0:T(8,128)S(1)} %collective-permute-done, f32[512,512]{1,0:T(8,128)S(1)} %get-tuple-element.10, f32[512,512]{1,0:T(8,128)S(1)} %copy-done), kind=kLoop, calls=%fused_computation.1 | loop fusion | flops 3145728 | bytes 8388608 | tf_op jit(solution)/shard_map/concatenate | solution.py:166
  185.8 1.7 collective-permute-start.6
  187.6 1.8 collective-permute-start.7
  189.4 1.3 collective-permute-done.6
  190.7 1.3 collective-permute-done.7
  192.0 4.5 %collective-permute-start.8 = (f32[2,8,8,256]{3,2,1,0:T(8,128)S(1)}, f32[2,8,8,256]{3,2,1,0:T(8,128)S(1)}, u32[]{:S(2)}, u32[]{:S(2)}) collective-permute-start(f32[2,8,8,256]{3,2,1,0:T(8,128)S(1)} %pad_maximum_fusion.3), channel_id=1, source_target_pairs={{0,8},{8,0},{32,40},{40,32},{64,72},{72,64},{96,104},{104,96},{1,9... | collective-permute-start | bytes 393224 | tf_op jit(solution)/shard_map/ppermute | solution.py:31
  196.4 4.8 %momentum_residual.1 = f32[512,512]{1,0:T(8,128)} custom-call(f32[512,512]{1,0:T(8,128)} %get-tuple-element.4.mom_ref, f32[8,8,256]{2,1,0:T(8,128)} %get-tuple-element.5.shared_ref, f32[64,256]{1,0:T(8,128)} %get-tuple-element.17.vert_ref, f32[256,64]{1,0:T(8,128)} %cosine_multiply_fusion.horiz_t_ref), custom_call_target="tpu_custom_call" | custom-call | flops 2000000000 | bytes 2097152 | tf_op jit(solution)/shard_map/momentum_residual/pallas_call | solution.py:116
  201.2 0.7 pad_maximum_fusion.2.total_ref
  201.9 11.1 %parameter_update.1 = f32[2048,512]{1,0:T(8,128)} custom-call(s32[4]{0:T(128)} %iota_xor_fusion.at_ref, f32[2048,512]{1,0:T(8,128)} %pad_maximum_fusion.params_ref, f32[4,8,8,256]{3,2,1,0:T(8,128)} %pad_maximum_fusion.2.total_ref, f32[64,256]{1,0:T(8,128)} %get-tuple-element.17.vert_ref, f32[256,64]{1,0:T(8,128)} %cosine_multiply_fusion.horiz_t_ref), custom_call_target="tpu_custom_call" | custom-call | tf_op jit(solution)/shard_map/parameter_update/pallas_call | solution.py:135
  (21 shorter events, 0.6 us)
Async XLA Ops:
  7.2 164.0 %reduce-scatter.2.cloned.1.call-start = ((), (), s32[]{:S(2)}) async-start(), calls=%async_computation.1 | async-start | bytes 17825792 | tf_op jit(solution)/shard_map/reduce_scatter | solution.py:161
  18.8 1.2 copy-start
  20.0 29.8 %copy-start.2 = (s32[256]{0:T(256)S(1)}, s32[256]{0:T(256)}, u32[]{:S(2)}) copy-start(s32[256]{0:T(256)} %param.7) | copy-start | bytes 3076
  20.0 26.3 %collective-permute-start = (f32[512,512]{1,0:T(8,128)S(1)}, f32[512,512]{1,0:T(8,128)S(1)}, u32[]{:S(2)}, u32[]{:S(2)}) collective-permute-start(f32[512,512]{1,0:T(8,128)S(1)} %copy-done), channel_id=1, source_target_pairs={{0,17},{8,25},{32,49},{40,57},{64,81},{72,89},{96,113},{104,121},{... | collective-permute-start | bytes 3145736 | tf_op jit(solution)/shard_map/ppermute | solution.py:31
  47.8 131.6 %collective-permute-start.1 = (f32[1024,512]{1,0:T(8,128)}, f32[1024,512]{1,0:T(8,128)}, u32[]{:S(2)}, u32[]{:S(2)}) collective-permute-start(f32[1024,512]{1,0:T(8,128)} %pad_maximum_fusion.1), channel_id=1, source_target_pairs={{0,8},{8,0},{32,40},{40,32},{64,72},{72,64},{96,104},{104,96},{1,9... | collective-permute-start | bytes 6291464 | tf_op jit(solution)/shard_map/ppermute | solution.py:31
  175.7 7.3 %copy-start.1 = (f32[8,8,256]{2,1,0:T(8,128)S(1)}, f32[8,8,256]{2,1,0:T(8,128)}, u32[]{:S(2)}) copy-start(f32[8,8,256]{2,1,0:T(8,128)} %get-tuple-element.5.shared_ref) | copy-start | bytes 196612
  175.7 5.3 %collective-permute-start.3 = (f32[8,8,256]{2,1,0:T(8,128)}, f32[8,8,256]{2,1,0:T(8,128)S(1)}, u32[]{:S(2)}, u32[]{:S(2)}) collective-permute-start(f32[8,8,256]{2,1,0:T(8,128)} %get-tuple-element.5.shared_ref), channel_id=1, source_target_pairs={{0,4},{8,12},{32,36},{40,44},{64,68},{72,76},{96,100},{104,108},{1... | collective-permute-start | bytes 196616 | tf_op jit(solution)/shard_map/ppermute | solution.py:31
  178.5 4.5 %collective-permute-start.4 = (f32[8,8,256]{2,1,0:T(8,128)}, f32[8,8,256]{2,1,0:T(8,128)S(1)}, u32[]{:S(2)}, u32[]{:S(2)}) collective-permute-start(f32[8,8,256]{2,1,0:T(8,128)} %get-tuple-element.5.shared_ref), channel_id=1, source_target_pairs={{0,6},{8,14},{32,38},{40,46},{64,70},{72,78},{96,102},{104,110},{1... | collective-permute-start | bytes 196616 | tf_op jit(solution)/shard_map/ppermute | solution.py:31
  179.4 3.7 %collective-permute-start.2 = (f32[8,8,256]{2,1,0:T(8,128)}, f32[8,8,256]{2,1,0:T(8,128)S(1)}, u32[]{:S(2)}, u32[]{:S(2)}) collective-permute-start(f32[8,8,256]{2,1,0:T(8,128)} %get-tuple-element.5.shared_ref), channel_id=1, source_target_pairs={{0,2},{8,10},{32,34},{40,42},{64,66},{72,74},{96,98},{104,106},{1,... | collective-permute-start | bytes 196616 | tf_op jit(solution)/shard_map/ppermute | solution.py:31
  183.0 6.3 %collective-permute-start.5 = (f32[8,8,256]{2,1,0:T(8,128)S(1)}, f32[8,8,256]{2,1,0:T(8,128)S(1)}, u32[]{:S(2)}, u32[]{:S(2)}) collective-permute-start(f32[8,8,256]{2,1,0:T(8,128)S(1)} %add_add_fusion), channel_id=1, source_target_pairs={{0,1},{8,9},{32,33},{40,41},{64,65},{72,73},{96,97},{104,105},{1,0... | collective-permute-start | bytes 196616 | tf_op jit(solution)/shard_map/ppermute | solution.py:31
  185.8 4.8 %collective-permute-start.6 = (f32[8,8,256]{2,1,0:T(8,128)S(1)}, f32[8,8,256]{2,1,0:T(8,128)S(1)}, u32[]{:S(2)}, u32[]{:S(2)}) collective-permute-start(f32[8,8,256]{2,1,0:T(8,128)S(1)} %add_add_fusion), channel_id=1, source_target_pairs={{0,16},{8,24},{32,48},{40,56},{64,80},{72,88},{96,112},{104,120},{... | collective-permute-start | bytes 196616 | tf_op jit(solution)/shard_map/ppermute | solution.py:31
  187.6 4.3 %collective-permute-start.7 = (f32[8,8,256]{2,1,0:T(8,128)S(1)}, f32[8,8,256]{2,1,0:T(8,128)S(1)}, u32[]{:S(2)}, u32[]{:S(2)}) collective-permute-start(f32[8,8,256]{2,1,0:T(8,128)S(1)} %add_add_fusion), channel_id=1, source_target_pairs={{0,17},{8,25},{32,49},{40,57},{64,81},{72,89},{96,113},{104,121},{... | collective-permute-start | bytes 196616 | tf_op jit(solution)/shard_map/ppermute | solution.py:31
  192.0 9.2 %collective-permute-start.8 = (f32[2,8,8,256]{3,2,1,0:T(8,128)S(1)}, f32[2,8,8,256]{3,2,1,0:T(8,128)S(1)}, u32[]{:S(2)}, u32[]{:S(2)}) collective-permute-start(f32[2,8,8,256]{3,2,1,0:T(8,128)S(1)} %pad_maximum_fusion.3), channel_id=1, source_target_pairs={{0,8},{8,0},{32,40},{40,32},{64,72},{72,64},{96,104},{104,96},{1,9... | collective-permute-start | bytes 393224 | tf_op jit(solution)/shard_map/ppermute | solution.py:31
Sparse Core Ops, SparseCore 0:
  18.9 152.1 reduce-scatter.1

commit v2 on v0

v2 whole, which is shorter than its diff:
```python
import jax
import jax.numpy as jnp
from jax import lax
from jax.experimental import pallas as pl
from jax.experimental.pallas import tpu as pltpu
from jax.sharding import PartitionSpec as P

GROUP = 64
BAND = 256
COLS = 512
NB = COLS // GROUP
OWN = 512
ZROWS = 320
LANES = COLS // 128
AXES = ("fsdp", "dp", "outer")
beta = 0.9

F32 = jnp.float32
BF16 = jnp.bfloat16


def place(x, y, z, core):
    return z * 32 + ((y // 2) * 2 + core) * 8 + x * 2 + y % 2


def swap(value, x=0, y=0, z=0, core=0):
    pairs = []
    for px in range(4):
        for py in range(4):
            for pz in range(4):
                for pc in range(2):
                    pairs.append((place(px, py, pz, pc), place(px ^ x, py ^ y, (pz + z) % 4, pc ^ core)))
    return lax.ppermute(value, AXES, pairs)


def cosine_columns(freq):
    freq = freq.astype(F32)[None, :]
    pos = jnp.arange(GROUP, dtype=F32)[:, None]
    scale = jnp.where(freq == 0, jnp.sqrt(1.0 / GROUP), jnp.sqrt(2.0 / GROUP)).astype(F32)
    return scale * jnp.cos(jnp.pi * (2.0 * pos + 1.0) * freq / (2.0 * GROUP))


def split(value):
    high = value.astype(BF16)
    return high, (value - high.astype(F32)).astype(BF16)


def dot(a, b):
    return jnp.dot(a, b, preferred_element_type=F32)


def piece_shape(step):
    f, _, _, _, rows = step
    return (2, rows, COLS) if isinstance(f, str) else (rows, COLS)


def piece_source(step, z, yh, core, parts_ref):
    f, r, c, top, rows = step
    cut = pl.ds(top, rows)
    r_at, c_at = (yh + r) % 2, (core + c) % 2
    if isinstance(f, str):
        lo = (z + (1 if f == "sides" else 0)) % 2
        return parts_ref.at[:, lo, r_at, c_at, cut, :]
    to = (z + f) % 4
    return parts_ref.at[to // 2, to % 2, r_at, c_at, cut, :]


def mark(z, piece, term, out):
    out[...] = jnp.zeros((8, 128), F32)


def piece_call(name, parts, steps, terms, after, outs, cost=1):
    outs = outs + [((8, 128), mark)]
    outs = [out if len(out) == 3 else out + (F32,) for out in outs]
    terms = [t if isinstance(t, tuple) else (t, t.shape, lambda x, ref: ref) for t in terms]
    n_terms, n_after, n_outs, n_steps = len(terms), len(after), len(outs), len(steps)

    def kernel(parts_ref, *refs):
        refs = list(refs)
        take = lambda n: [refs.pop(0) for _ in range(n)]
        term_refs, _, out_refs = take(n_terms), take(n_after), take(n_outs)
        bufs, held, built = take(n_steps), take(n_terms), take(n_outs)
        load_sems, out_sems = take(n_steps + n_terms), take(n_outs)
        z, dp, x = lax.axis_index("fsdp"), lax.axis_index("dp"), lax.axis_index("outer") // 2
        sources = [piece_source(s, z, dp // 2, dp % 2, parts_ref) for s in steps]
        sources += [pick(x, ref) for (_, _, pick), ref in zip(terms, term_refs)]
        loads = []
        for src, buf, sem in zip(sources, bufs + held, load_sems):
            copy = pltpu.make_async_copy(src, buf, sem)
            copy.start()
            loads.append(copy)
        waiting = set(range(len(loads)))

        def loaded(i):
            if i in waiting:
                waiting.remove(i)
                loads[i].wait()
            return (bufs + held)[i]

        stores = []
        for (_, body, _), ref, buf, sem in zip(outs, out_refs, built, out_sems):
            body(z, loaded, lambda i: loaded(n_steps + i), buf)
            copy = pltpu.make_async_copy(buf, ref, sem)
            copy.start()
            stores.append(copy)
        for i in sorted(waiting):
            loads[i].wait()
        for copy in stores:
            copy.wait()

    anywhere = pl.BlockSpec(memory_space=pl.ANY)
    return pl.pallas_call(
        kernel,
        in_specs=[pl.BlockSpec(memory_space=pltpu.HBM)] + [anywhere] * (n_terms + n_after),
        out_specs=[anywhere] * n_outs,
        out_shape=[jax.ShapeDtypeStruct(s, t) for s, _, t in outs],
        scratch_shapes=[pltpu.VMEM(piece_shape(s), BF16) for s in steps]
        + [pltpu.VMEM(s, F32) for _, s, _ in terms]
        + [pltpu.VMEM(s, t) for s, _, t in outs]
        + [pltpu.SemaphoreType.DMA] * (n_steps + n_terms + n_outs),
        compiler_params=pltpu.CompilerParams(vmem_limit_bytes=40 * 2**20),
        cost_estimate=pl.CostEstimate(flops=1, bytes_accessed=cost, transcendentals=0),
        name=name,
    )(parts, *[t for t, _, _ in terms], *after)


def encode(mom, vert, horiz):
    rows = mom.shape[0]
    w_high, w_low = split(horiz)
    x_high, x_low = split(mom)
    out = []
    for b in range(NB):
        cut = slice(b * GROUP, (b + 1) * GROUP)
        half = dot(x_high[:, cut], w_high) + dot(x_low[:, cut], w_high) + dot(x_high[:, cut], w_low)
        out.append(jnp.sum(half.reshape(rows // GROUP, GROUP, BAND) * vert[None], axis=1))
    return out


def step_rows(grad_parts, momentum, params, vert, horiz):
    parts = pltpu.with_memory_space_constraint(grad_parts.reshape(2, 2, 2, 2, OWN, COLS), pltpu.HBM)
    vert_t, horiz_t = vert.T, horiz.T
    zr, yr, half = ZROWS, OWN - ZROWS, COLS // 2
    zs, ys = (zr, COLS), (yr, COLS)
    zh, yhs = (zr, half), (yr, half)
    left, right = slice(0, half), slice(half, COLS)
    call = lambda name, *rest, **options: piece_call(name, parts, *rest, **options)

    def widen(name, groups, after):
        outs, first = [], 0
        for group in groups:
            counts = [2 * s[4] if isinstance(s[0], str) else s[4] for s in group]

            def body(z, piece, term, out, counts=counts, first=first):
                top = 0
                for i, n in enumerate(counts):
                    out[top:top + n, :] = piece(first + i)[...].reshape(n, COLS).astype(F32)
                    top += n

            outs.append(((sum(counts), COLS), body))
            first += len(group)
        return call(name, [s for group in groups for s in group], [], after, outs)

    def rows_of(ref, top, n, cols=slice(None)):
        return ref[top:top + n, cols]

    def side(ref, top, n, at_f, cols):
        return ref[pl.ds(pl.multiple_of(top + at_f * n, 64), n), cols]

    def hi(z, f):
        return ((z + f) % 4) // 2

    def halves(top):
        def body(cols):
            def run(z, piece, term, out):
                out[...] = rows_of(term(0), top, zr, cols) + piece(0)[:, cols].astype(F32)
            return run
        return [(zh, body(left)), (zh, body(right))]

    quarter = OWN // 4
    far_rows, crossed_rows = 2 * yr, 2 * yr + quarter

    def crossing(i_piece, i_term, top, i_params):
        def run(z, piece, term, out):
            for h in range(2):
                out[h * yr:(h + 1) * yr, :] = rows_of(term(i_term), top + h * yr, yr) + piece(i_piece)[h].astype(F32)
            out[far_rows:, :] = term(i_params)[...]
        return run

    def params_quarter(i):
        def pick(x, ref):
            return ref.at[pl.ds(pl.multiple_of((x % 2) * (2 * quarter) + i * quarter, quarter), quarter), :]
        return (params, (quarter, COLS), pick)

    def sides(i_piece, got, i_add):
        def body(f, h_add, i_add):
            def run(z, piece, term, out):
                k = hi(z, f)
                for h, cols in enumerate((left, right)):
                    value = got(term, f, k, cols) + piece(i_piece)[k, :, cols].astype(F32)
                    out[:, cols] = value + term(i_add)[...] if h == h_add else value
            return run
        return [(zs, body(1, 0, i_add)), (zs, body(3, 1, i_add + 1))]

    up, down = (lambda v: swap(v, z=1)), (lambda v: swap(v, z=3))
    wa, ta = widen("widen_a", [[(2, 1, 1, 0, zr), ("even", 1, 1, zr, yr)]], [])
    ca = swap(wa, core=1)
    wb, tb = widen("widen_b", [[("sides", 1, 1, 0, zr), (2, 0, 1, 0, zr)]], [ta])
    cb = swap(wb, core=1)
    u1, d1, y1, t1 = call("far_opposite", [(2, 1, 0, 0, zr), ("even", 1, 0, zr, yr)], [ca, params_quarter(0)], [tb],
                          halves(0) + [((crossed_rows, COLS), crossing(1, 0, zr, 1))])
    gu1, gd1, gy1 = up(u1), down(d1), swap(y1, y=2)
    *wc, tc = widen("widen_c", [[("sides", 1, 1, zr, yr)], [("even", 0, 1, zr, yr)]], [t1])
    c_cross, c_last = [swap(w, core=1) for w in wc]
    u2, d2, t2 = call("near_opposite", [(2, 0, 0, 0, zr)], [cb], [tc], halves(2 * zr))
    gu2, gd2 = up(u2), down(d2)
    u3, d3, y2, t3 = call("far_sides", [("sides", 1, 0, 0, zr), ("sides", 1, 0, zr, yr)],
                          [cb, gu1, gd1, c_cross, params_quarter(1)], [t2],
                          sides(0, lambda term, f, k, cols: side(term(0), 0, zr, k, cols), 1)
                          + [((crossed_rows, COLS), crossing(1, 3, 0, 4))])
    gu3, gd3, gy2 = up(u3), down(d3), swap(y2, y=2)
    *wd, td = widen("widen_d", [[(1, 0, 1, 0, zr)], [(3, 0, 1, 0, zr)], [(0, 1, 1, 0, zr)], [(0, 0, 1, 0, zr)],
                                [("sides", 0, 1, zr, yr)]], [t3, gu2, gd2])
    c_up, c_down, c_far, c_near, c_sides = [swap(w, core=1) for w in wd]
    table_high, table_low, tt = call("band_table", [], [vert_t, horiz_t], [td], band_table())

    def last_half(cols):
        def run(z, piece, term, out):
            k = hi(z, 2)
            out[...] = side(term(0), 0, yr, k, cols) + side(term(1), 0, yr, k, cols) + piece(0)[k, :, cols].astype(F32)
        return run

    def last_own_body(z, piece, term, out):
        k = z // 2
        out[...] = side(term(0), 0, yr, k, slice(None)) + side(term(1), 0, yr, k, slice(None)) + piece(0)[k].astype(F32)

    u4, d4, last_own, t4 = call("last_opposite", [("even", 0, 0, zr, yr)], [gy1, c_last], [tt],
                            [(yhs, last_half(left)), (yhs, last_half(right)), (ys, last_own_body)])
    gu4, gd4 = up(u4), down(d4)
    u5, d5, t5 = call("near_sides", [("sides", 0, 0, 0, zr)], [c_up, c_down, gu2, gd2], [t4, gu3, gd3],
                      sides(0, lambda term, f, k, cols: term(0 if f == 1 else 1)[:, cols], 2))
    gu5, gd5 = up(u5), down(d5)

    def cross_body(z, piece, term, out):
        out[...] = term(0)[...] + piece(0)[...].astype(F32) + (term(1)[...] + term(2)[...])

    y3, tx = call("far_cross", [(0, 1, 0, 0, zr)], [c_far, gu3, gd3], [t5], [(zs, cross_body)])
    gy3 = swap(y3, y=2)

    def last_sides(f, h_add, i_add):
        def run(z, piece, term, out):
            k = hi(z, f)
            for h, cols in enumerate((left, right)):
                value = side(term(0), 0, yr, k, cols) + side(term(1), 0, yr, k, cols) + piece(0)[k, :, cols].astype(F32)
                out[:, cols] = value + term(i_add)[...] if h == h_add else value
        return run

    def half_body(z, piece, term, out):
        out[:quarter, :] = term(4)[...]
        out[quarter:, :] = term(0)[far_rows:, :]

    last_quarter = (gy1, (quarter, COLS), lambda x, ref: ref.at[pl.ds(far_rows, quarter), :])
    u6, d6, far_half, t6 = call("last_sides", [("sides", 0, 0, zr, yr)], [gy2, c_sides, gu4, gd4, last_quarter], [tx],
                            [(ys, last_sides(1, 0, 2)), (ys, last_sides(3, 1, 3)), ((2 * quarter, COLS), half_body)])
    gu6, gd6 = up(u6), down(d6)

    def momentum_rows(top, n):
        return (momentum, (n, COLS), lambda x, ref: ref.at[pl.ds(top, n), :])

    def near_mom(z, piece, term, out):
        mine = term(0)[...] + piece(0)[...].astype(F32)
        grad = mine + (term(1)[...] + term(2)[...]) + term(3)[...]
        out[...] = beta * term(4)[...] + grad * (1.0 / 16.0)
        near_mom.value = out

    def near_shared(z, piece, term, out):
        for b, value in enumerate(encode(near_mom.value[...], term(5)[...], term(6)[...])):
            out[b] = value

    nz, ny = zr // GROUP, yr // GROUP
    mom_top, shared_top, t7 = call(
        "near_momentum", [(0, 0, 0, 0, zr)], [c_near, gu5, gd5, gy3, momentum_rows(0, zr), vert, horiz], [t6],
        [(zs, near_mom), ((NB, nz, BAND), near_shared)], cost=9 * 10**6,
    )

    def last_mom(z, piece, term, out):
        grad = term(0)[...] + (term(1)[...] + term(2)[...])
        out[...] = beta * term(3)[...] + grad * (1.0 / 16.0)
        last_mom.value = out

    def last_shared(z, piece, term, out):
        for b, value in enumerate(encode(last_mom.value[...], term(4)[...], term(5)[...])):
            out[b, :nz, :] = term(6)[b]
            out[b, nz:, :] = value

    mom_low, shared, t8 = call(
        "last_momentum", [], [last_own, gu6, gd6, momentum_rows(zr, yr), vert, horiz, shared_top], [t7],
        [(ys, last_mom), ((NB, nz + ny, BAND), last_shared)],
    )

    def pack(z, piece, term, out):
        out[:OWN, :] = term(0)[...]
        out[OWN:, :] = term(1)[...]

    packed, _ = call("params_pack", [], [params, far_half], [t6], [((OWN + 2 * quarter, COLS), pack)])

    def residual(z, piece, term, out):
        high, low = split(term(4)[...])
        w_both = jnp.concatenate([high, low], axis=1)
        vert_now = term(3)[...][None]
        for pair in range(NB // 2):
            sides = []
            for b in (2 * pair, 2 * pair + 1):
                wide = (term(2)[b][:, None, :] * vert_now).reshape(OWN, BAND)
                wide_high, wide_low = split(wide)
                both = dot(wide_high, w_both)
                sides.append(both[:, :GROUP] + both[:, GROUP:] + dot(wide_low, w_both[:, :GROUP]))
            cols = slice(pair * 2 * GROUP, (pair + 1) * 2 * GROUP)
            value = jnp.concatenate(sides, axis=1)
            out[:zr, cols] = term(0)[:, cols] - value[:zr]
            out[zr:, cols] = term(1)[:, cols] - value[zr:]

    new_momentum, t9 = call("momentum_residual", [], [mom_top, mom_low, shared, vert, horiz_t], [t8],
                            [((OWN, COLS), residual)], cost=9 * 10**6)

    def sum_four(z, piece, term, out):
        out[...] = (term(0)[...] + term(1)[...]) + (term(2)[...] + term(3)[...])

    def sum_pairs(z, piece, term, out):
        out[0] = term(0)[...] + term(1)[...]
        out[1] = term(2)[...] + term(3)[...]

    total, t10 = call("sum_x", [], [shared] + [swap(shared, x=k) for k in (1, 2, 3)], [t9], [(shared.shape, sum_four)])
    pair, _ = call("sum_y", [], [total] + [swap(total, y=k) for k in (1, 2, 3)], [], [((2,) + shared.shape, sum_pairs)])
    far_other = swap(far_half, x=1)
    new_params = update_call(params, swap(packed, core=1), far_half, far_other, swap(far_other, core=1),
                             pair, swap(pair, core=1), table_high, table_low)
    return new_momentum, new_params


def band_table():
    held = {}

    def high(z, piece, term, out):
        lane = lax.broadcasted_iota(jnp.int32, (BAND, 2 * GROUP), 1)
        horiz = jnp.concatenate([term(1)[...]] * 2, axis=1)
        vert = term(0)[...]
        held["low"] = []
        for m in range(0, GROUP, 2):
            product = jnp.where(lane < GROUP, vert[:, m:m + 1], vert[:, m + 1:m + 2]) * horiz
            top, rest = split(product)
            out[:, m * GROUP:(m + 2) * GROUP] = top
            held["low"].append(rest)

    def low(z, piece, term, out):
        for i, rest in enumerate(held["low"]):
            out[:, 2 * i * GROUP:2 * (i + 1) * GROUP] = rest

    return [((BAND, GROUP * GROUP), high, BF16), ((BAND, GROUP * GROUP), low, BF16)]


def update_kernel(params_ref, packed_ref, far_ref, other_ref, far_core_ref, pair_ref, pair_core_ref, high_ref, low_ref,
                  out_ref, field, coeff, high, low, sems, out_sem):
    dp = lax.axis_index("dp")
    odd = (lax.axis_index("outer") // 2) % 2
    half = OWN // 2

    def rows(k, h, n):
        return pl.ds(((dp ^ k) * 2 + h) * (half // GROUP), n // GROUP)

    moves = [
        (pair_ref.at[0], coeff.at[:, dp]),
        (pair_ref.at[1], coeff.at[:, dp ^ 2]),
        (pair_core_ref.at[0], coeff.at[:, dp ^ 1]),
        (pair_core_ref.at[1], coeff.at[:, dp ^ 3]),
        (high_ref, high),
        (low_ref, low),
    ]
    for ref, top, n, to in (
        (params_ref, 0, OWN, rows(0, 0, OWN)),
        (packed_ref, 0, OWN, rows(1, 0, OWN)),
        (far_ref, 0, half, rows(2, odd, half)),
        (other_ref, 0, half, rows(2, 1 - odd, half)),
        (packed_ref, OWN, half, rows(3, odd, half)),
        (far_core_ref, 0, half, rows(3, 1 - odd, half)),
    ):
        for i in range(LANES):
            part = ref.at[pl.ds(top // GROUP, n // GROUP), :, pl.ds(i * 128, 128)]
            moves.append((part, field.at[i, to]))
    copies = [pltpu.make_async_copy(src, dst, sems.at[i]) for i, (src, dst) in enumerate(moves)]
    for copy in copies:
        copy.start()
    for copy in copies:
        copy.wait()
    c_high, c_low = split(coeff[...].reshape(NB * 32, BAND) * (1.0 / 8.0))
    both = jnp.concatenate([c_high, c_low], axis=0)
    lane = lax.broadcasted_iota(jnp.int32, (32, 2 * GROUP), 1)
    first = lane < GROUP
    step = 8

    def body(c, carry):
        cols = pl.ds(pl.multiple_of(c * step * GROUP, step * GROUP), step * GROUP)
        t_high = high[:, cols]
        wide = dot(both, t_high)
        value = wide[:NB * 32] + wide[NB * 32:] + dot(c_high, low[:, cols])
        for b in range(0, NB, 2):
            x0, x1 = [value[i * 32:(i + 1) * 32] for i in (b, b + 1)]
            rows_m = []
            for lt in range(step // 2):
                lanes = slice(lt * 2 * GROUP, (lt + 1) * 2 * GROUP)
                y0, y1 = x0[:, lanes], x1[:, lanes]
                rows_m.append(jnp.where(first, y0, pltpu.roll(y1, GROUP, 1)))
                rows_m.append(jnp.where(first, pltpu.roll(y0, GROUP, 1), y1))
            turned = jnp.swapaxes(jnp.stack(rows_m), 0, 1)
            at = pl.ds(pl.multiple_of(c * step, step), step)
            field[b // 2, :, at, :] = field[b // 2, :, at, :] - turned
        return carry

    lax.fori_loop(0, GROUP // step, body, 0)
    stores = [pltpu.make_async_copy(field.at[i], out_ref.at[:, :, pl.ds(i * 128, 128)], out_sem.at[i]) for i in range(LANES)]
    for store in stores:
        store.start()
    for store in stores:
        store.wait()


def update_call(*arrays):
    arrays = [a.reshape(-1, GROUP, COLS) if a.ndim == 2 and a.dtype == F32 else a for a in arrays]
    anywhere = pl.BlockSpec(memory_space=pl.ANY)
    return pl.pallas_call(
        update_kernel,
        in_specs=[anywhere] * len(arrays),
        out_specs=anywhere,
        out_shape=jax.ShapeDtypeStruct((4 * OWN // GROUP, GROUP, COLS), F32),
        scratch_shapes=[
            pltpu.VMEM((LANES, 4 * OWN // GROUP, GROUP, 128), F32),
            pltpu.VMEM((NB, 4, OWN // GROUP, BAND), F32),
            pltpu.VMEM((BAND, GROUP * GROUP), BF16),
            pltpu.VMEM((BAND, GROUP * GROUP), BF16),
            pltpu.SemaphoreType.DMA((6 + 6 * LANES,)),
            pltpu.SemaphoreType.DMA((LANES,)),
        ],
        compiler_params=pltpu.CompilerParams(vmem_limit_bytes=40 * 2**20),
        name="parameter_update",
    )(*arrays).reshape(4 * OWN, COLS)


def local(grad_parts, momentum, params, band):
    band = band.astype(jnp.int32)
    vert = cosine_columns(band // GROUP)
    horiz = cosine_columns(band % GROUP)
    new_momentum, new_params = step_rows(grad_parts, momentum[0], params, vert, horiz)
    return (new_momentum[None], new_params)


def solution(mesh):
    return jax.shard_map(
        local,
        mesh=mesh,
        in_specs=(
            P("outer", "fsdp", "dp", None, None),
            P("outer", ("fsdp", "dp"), None),
            P(("fsdp", "dp"), None),
            P(),
        ),
        out_specs=(P("outer", ("fsdp", "dp"), None), P("fsdp", None)),
        check_vma=False,
    )
```

time: 417 us -> 143 us (0.34)
  waiting for transfers between devices: 242 us -> 47.7 us
  local copies, waits for them, and re-layouts: 115 us -> 0.01 us
  starting transfers between devices: 0.26 us -> 49.8 us
  Pallas kernels: 0 us -> 42.3 us
  matrix products: 24.8 us -> 0 us
  other arithmetic: 19.4 us -> 1.48 us
  between operations: 13.8 us -> 1.06 us
    reduce_scatter x1 -> x0, waiting for transfers between devices: 149 us -> none  [local(): lax.psum_scatter(partial_value, ('fsdp', 'dp'), scatter_dimension=0, tile...]
    psum x1 -> x0, waiting for transfers between devices: 74.5 us -> none  [local(): total = lax.psum(shared, 'outer')]
    ppermute x0 -> x34, starting transfers between devices: none -> 49.8 us  [swap(): return lax.ppermute(value, AXES, pairs)]
    scatter x2 -> x0, local copies, waits for them, and re-layouts: 47.8 us -> none  [decode(): jnp.zeros((nrow, ncol, GROUP * GROUP), jnp.float32).at[:, :, band]]
    ppermute x0 -> x34, waiting for transfers between devices: none -> 47.7 us  [swap(): return lax.ppermute(value, AXES, pairs)]
    pallas_call x0 -> x19, Pallas kernels: none -> 42.3 us  [the longest x18 34.5 us: piece_call(): pl.pallas_call(kernel, in_specs=[pl.BlockSpec(memory_space=pltpu.HBM)] +...]
    reshape x6 -> x0, local copies, waits for them, and re-layouts: 41.2 us -> none  [the longest x2 24.3 us: decode(): placed = placed.reshape(nrow, ncol, GROUP, GROUP)]
    dot_general x6 -> x0, matrix products: 24.8 us -> none  [the longest x2 12.4 us: decode(): jnp.einsum('km,abkl->ambl', table, placed, precision=lax.Precision.HIGHEST)]
  transfers between devices with their start and end apart: 3 -> 34, of which waited for: 3 -> 14; matrix products, arithmetic and copies ran while one was open for 6% -> 1% of each run, Pallas kernels for 0% -> 23%
where the time goes in v2:
time: 143 us; the launch traced here: 142 us
  starting transfers between devices  49.8 us (35%)
  waiting for transfers between devices  47.7 us (33%)
  Pallas kernels  42.3 us (30%)
  other arithmetic  1.48 us (1%)
    ppermute x34, starting transfers between devices, swap(): return lax.ppermute(value, AXES, pairs)  49.8 us
    ppermute x34, waiting for transfers between devices, swap(): return lax.ppermute(value, AXES, pairs)  47.7 us
    pallas_call x18, Pallas kernels, piece_call(): pl.pallas_call(kernel, in_specs=[pl.BlockSpec(memory_space=pltpu.HBM)] +...  34.5 us
    pallas_call x1, Pallas kernels, update_call(): pl.pallas_call(update_kernel, in_specs=[anywhere] * len(arrays), out_spec...  7.79 us
  transfers between devices with their start and end apart: 34, of which 14 were waited for; matrix products, arithmetic and copies ran while one was open for 1% of the time, Pallas kernels for 23%

profile of v2, /device:TPU:1, one launch (start us, length us, event | category | flops | bytes accessed | tf_op | source)
XLA Modules:
  0.0 142.3 jit_solution(8985100631596324089)
XLA Ops:
  11.5 2.9 %collective-permute-start.10 = (f32[512,512]{1,0:T(8,128)S(1)}, f32[512,512]{1,0:T(8,128)S(1)}, u32[]{:S(2)}, u32[]{:S(2)}) collective-permute-start(f32[512,512]{1,0:T(8,128)S(1)} %get-tuple-element.69), channel_id=1, source_target_pairs={{0,16},{8,24},{32,48},{40,56},{64,80},{72,88},{96,112},{104,120},{... | collective-permute-start | bytes 3145736 | tf_op jit(solution)/shard_map/ppermute | solution.py:33
  14.4 2.1 %collective-permute-start.3 = (f32[320,256]{1,0:T(8,128)S(1)}, f32[320,256]{1,0:T(8,128)S(1)}, u32[]{:S(2)}, u32[]{:S(2)}) collective-permute-start(f32[320,256]{1,0:T(8,128)S(1)} %get-tuple-element.58), channel_id=1, source_target_pairs={{0,96},{8,104},{32,0},{40,8},{64,32},{72,40},{96,64},{104,72},{1,9... | collective-permute-start | bytes 983048 | tf_op jit(solution)/shard_map/ppermute | solution.py:33
  17.9 3.6 %collective-permute-done.2.refs_1_ = f32[320,256]{1,0:T(8,128)S(1)} collective-permute-done((f32[320,256]{1,0:T(8,128)S(1)}, f32[320,256]{1,0:T(8,128)S(1)}, u32[]{:S(2)}, u32[]{:S(2)}) %collective-permute-start.2) | collective-permute-done | bytes 327712 | tf_op jit(solution)/shard_map/ppermute | solution.py:33
  23.3 2.0 %far_sides.1 = (f32[320,512]{1,0:T(8,128)S(1)}, f32[320,512]{1,0:T(8,128)S(1)}, f32[512,512]{1,0:T(8,128)S(1)}, f32[8,128]{1,0:T(8,128)S(1)}) custom-call(bf16[2,2,2,2,512,512]{5,4,3,2,1,0:T(8,128)(2,1)} %bitcast.21, f32[960,512]{1,0:T(8,128)S(1)} %collective-permute-done.refs_0_, f32[320,256]{1,0:T(8,128)S(1)} %collective-permute-done.2.refs_1_, ...), custom_call_target="tpu_custom_call" | custom-call | flops 1 | bytes 1 | tf_op jit(solution)/shard_map/far_sides/pallas_call | solution.py:112
  26.7 2.1 %collective-permute-start.13 = (f32[320,512]{1,0:T(8,128)S(1)}, f32[320,512]{1,0:T(8,128)S(1)}, u32[]{:S(2)}, u32[]{:S(2)}) collective-permute-start(f32[320,512]{1,0:T(8,128)S(1)} %get-tuple-element.75), channel_id=1, source_target_pairs={{0,96},{8,104},{32,0},{40,8},{64,32},{72,40},{96,64},{104,72},{1,9... | collective-permute-start | bytes 1966088 | tf_op jit(solution)/shard_map/ppermute | solution.py:33
  30.1 18.4 %collective-permute-done.6.refs_2_.refs_3_ = f32[320,256]{1,0:T(8,128)S(1)} collective-permute-done((f32[320,256]{1,0:T(8,128)S(1)}, f32[320,256]{1,0:T(8,128)S(1)}, u32[]{:S(2)}, u32[]{:S(2)}) %collective-permute-start.6) | collective-permute-done | bytes 327712 | tf_op jit(solution)/shard_map/ppermute | solution.py:33
  48.5 2.6 %collective-permute-start.18 = (f32[512,512]{1,0:T(8,128)S(1)}, f32[512,512]{1,0:T(8,128)S(1)}, u32[]{:S(2)}, u32[]{:S(2)}) collective-permute-start(f32[512,512]{1,0:T(8,128)S(1)} %get-tuple-element.81), channel_id=1, source_target_pairs={{0,16},{8,24},{32,48},{40,56},{64,80},{72,88},{96,112},{104,120},{... | collective-permute-start | bytes 3145736 | tf_op jit(solution)/shard_map/ppermute | solution.py:33
  51.1 2.3 %widen_d.1 = (f32[320,512]{1,0:T(8,128)S(1)}, f32[320,512]{1,0:T(8,128)S(1)}, f32[320,512]{1,0:T(8,128)S(1)}, f32[320,512]{1,0:T(8,128)S(1)}, f32[384,512]{1,0:T(8,128)S(1)}, /*index=5*/f32[8,128]{1,0:T(8,128)S(1)}) custom-call(bf16[2,2,2,2,512,512]{5,4,3,2,1,0:T(8,128)(2,1)} %bitcast.22, f32[8,128]{1,0:T(8,128)S(1)} %get-tuple-element.63.refs_0_, ...), custom_call_target="tpu_custom_call" | custom-call | flops 1 | bytes 1 | tf_op jit(solution)/shard_map/widen_d/pallas_call | solution.py:112
  56.5 3.6 %band_table.1 = (bf16[256,4096]{1,0:T(8,128)(2,1)S(1)}, bf16[256,4096]{1,0:T(8,128)(2,1)S(1)}, f32[8,128]{1,0:T(8,128)S(1)}) custom-call(bf16[2,2,2,2,512,512]{5,4,3,2,1,0:T(8,128)(2,1)} %bitcast.23, f32[256,64]{1,0:T(8,128)S(1)} %get-tuple-element.113.refs_0_, f32[256,64]{1,0:T(8,128)S(1)} %get-tuple-element.112.refs_1_.refs_4_, ...), custom_call_target="tpu_custom_call" | custom-call | flops 1 | bytes 1 | tf_op jit(solution)/shard_map/band_table/pallas_call | solution.py:112
  62.9 2.9 %collective-permute-start.21 = (f32[192,256]{1,0:T(8,128)S(1)}, f32[192,256]{1,0:T(8,128)S(1)}, u32[]{:S(2)}, u32[]{:S(2)}) collective-permute-start(f32[192,256]{1,0:T(8,128)S(1)} %get-tuple-element.84), channel_id=1, source_target_pairs={{0,96},{8,104},{32,0},{40,8},{64,32},{72,40},{96,64},{104,72},{1,9... | collective-permute-start | bytes 589832 | tf_op jit(solution)/shard_map/ppermute | solution.py:33
  75.1 3.3 %collective-permute-start.24 = (f32[768,512]{1,0:T(8,128)S(1)}, f32[768,512]{1,0:T(8,128)S(1)}, u32[]{:S(2)}, u32[]{:S(2)}) collective-permute-start(f32[768,512]{1,0:T(8,128)S(1)} %get-tuple-element.98), channel_id=1, source_target_pairs={{0,8},{8,0},{32,40},{40,32},{64,72},{72,64},{96,104},{104,96},{1,9... | collective-permute-start | bytes 4718600 | tf_op jit(solution)/shard_map/ppermute | solution.py:33
  78.3 2.6 %collective-permute-start.17 = (f32[320,512]{1,0:T(8,128)S(1)}, f32[320,512]{1,0:T(8,128)S(1)}, u32[]{:S(2)}, u32[]{:S(2)}) collective-permute-start(f32[320,512]{1,0:T(8,128)S(1)} %get-tuple-element.80), channel_id=1, source_target_pairs={{0,16},{8,24},{32,48},{40,56},{64,80},{72,88},{96,112},{104,120},{... | collective-permute-start | bytes 1966088 | tf_op jit(solution)/shard_map/ppermute | solution.py:33
  82.2 3.4 %collective-permute-start.15 = (f32[320,512]{1,0:T(8,128)S(1)}, f32[320,512]{1,0:T(8,128)S(1)}, u32[]{:S(2)}, u32[]{:S(2)}) collective-permute-start(f32[320,512]{1,0:T(8,128)S(1)} %get-tuple-element.77), channel_id=1, source_target_pairs={{0,96},{8,104},{32,0},{40,8},{64,32},{72,40},{96,64},{104,72},{1,9... | collective-permute-start | bytes 1966088 | tf_op jit(solution)/shard_map/ppermute | solution.py:33
  85.6 10.6 %collective-permute-done.17.refs_3_ = f32[320,512]{1,0:T(8,128)S(1)} collective-permute-done((f32[320,512]{1,0:T(8,128)S(1)}, f32[320,512]{1,0:T(8,128)S(1)}, u32[]{:S(2)}, u32[]{:S(2)}) %collective-permute-start.17) | collective-permute-done | bytes 655392 | tf_op jit(solution)/shard_map/ppermute | solution.py:33
  97.1 2.1 %collective-permute-done.14.refs_1_ = f32[320,512]{1,0:T(8,128)S(1)} collective-permute-done((f32[320,512]{1,0:T(8,128)S(1)}, f32[320,512]{1,0:T(8,128)S(1)}, u32[]{:S(2)}, u32[]{:S(2)}) %collective-permute-start.14) | collective-permute-done | bytes 655392 | tf_op jit(solution)/shard_map/ppermute | solution.py:33
  102.3 3.3 %near_momentum.1 = (f32[320,512]{1,0:T(8,128)S(1)}, f32[8,5,256]{2,1,0:T(8,128)S(1)}, f32[8,128]{1,0:T(8,128)S(1)}) custom-call(bf16[2,2,2,2,512,512]{5,4,3,2,1,0:T(8,128)(2,1)} %bitcast.29, f32[320,512]{1,0:T(8,128)S(1)} %collective-permute-done.7.refs_0_, f32[320,512]{1,0:T(8,128)S(1)} %collective-permute-done.14.refs_1_, ...), custom_call_target="tpu_custom_call" | custom-call | flops 1 | bytes 9000000 | tf_op jit(solution)/shard_map/near_momentum/pallas_call | solution.py:112
  105.6 2.5 %collective-permute-done.22.refs_1_ = f32[192,512]{1,0:T(8,128)S(1)} collective-permute-done((f32[192,512]{1,0:T(8,128)S(1)}, f32[192,512]{1,0:T(8,128)S(1)}, u32[]{:S(2)}, u32[]{:S(2)}) %collective-permute-start.22) | collective-permute-done | bytes 393248 | tf_op jit(solution)/shard_map/ppermute | solution.py:33
  108.9 2.4 %last_momentum.1 = (f32[192,512]{1,0:T(8,128)S(1)}, f32[8,8,256]{2,1,0:T(8,128)S(1)}, f32[8,128]{1,0:T(8,128)S(1)}) custom-call(bf16[2,2,2,2,512,512]{5,4,3,2,1,0:T(8,128)(2,1)} %bitcast.30, f32[192,512]{1,0:T(8,128)S(1)} %get-tuple-element.88.refs_0_, f32[192,512]{1,0:T(8,128)S(1)} %collective-permute-done.22.refs_1_, ...), custom_call_target="tpu_custom_call" | custom-call | flops 1 | bytes 1 | tf_op jit(solution)/shard_map/last_momentum/pallas_call | solution.py:112
  112.6 2.5 %collective-permute-start.28 = (f32[8,8,256]{2,1,0:T(8,128)S(1)}, f32[8,8,256]{2,1,0:T(8,128)S(1)}, u32[]{:S(2)}, u32[]{:S(2)}) collective-permute-start(f32[8,8,256]{2,1,0:T(8,128)S(1)} %get-tuple-element.94.refs_2_.refs_0_), channel_id=1, source_target_pairs={{0,4},{8,12},{32,36},{40,44},{64,68},{72,76},{96,100},{104,108},{1... | collective-permute-start | bytes 196616 | tf_op jit(solution)/shard_map/ppermute | solution.py:33
  115.3 3.6 %momentum_residual.1 = (f32[512,512]{1,0:T(8,128)}, f32[8,128]{1,0:T(8,128)S(1)}) custom-call(bf16[2,2,2,2,512,512]{5,4,3,2,1,0:T(8,128)(2,1)} %bitcast.31, f32[320,512]{1,0:T(8,128)S(1)} %get-tuple-element.87.refs_0_, f32[192,512]{1,0:T(8,128)S(1)} %get-tuple-element.93.refs_1_, f32[8,8,256]{2,1,0:T(8,128)S(1)} %get-tuple-element.94.refs_2_.refs_0_, ...), custom_call_target="tpu_custom_call" | custom-call | flops 1 | bytes 9000000 | tf_op jit(solution)/shard_map/momentum_residual/pallas_call | solution.py:112
  121.2 2.4 %collective-permute-start.31 = (f32[8,8,256]{2,1,0:T(8,128)S(1)}, f32[8,8,256]{2,1,0:T(8,128)S(1)}, u32[]{:S(2)}, u32[]{:S(2)}) collective-permute-start(f32[8,8,256]{2,1,0:T(8,128)S(1)} %get-tuple-element.100.refs_0_), channel_id=1, source_target_pairs={{0,16},{8,24},{32,48},{40,56},{64,80},{72,88},{96,112},{104,120},{... | collective-permute-start | bytes 196616 | tf_op jit(solution)/shard_map/ppermute | solution.py:33
  126.0 2.0 %collective-permute-done.32.refs_3_ = f32[8,8,256]{2,1,0:T(8,128)S(1)} collective-permute-done((f32[8,8,256]{2,1,0:T(8,128)S(1)}, f32[8,8,256]{2,1,0:T(8,128)S(1)}, u32[]{:S(2)}, u32[]{:S(2)}) %collective-permute-start.32) | collective-permute-done | bytes 65568 | tf_op jit(solution)/shard_map/ppermute | solution.py:33
  129.1 4.2 %collective-permute-start.33 = (f32[2,8,8,256]{3,2,1,0:T(8,128)S(1)}, f32[2,8,8,256]{3,2,1,0:T(8,128)S(1)}, u32[]{:S(2)}, u32[]{:S(2)}) collective-permute-start(f32[2,8,8,256]{3,2,1,0:T(8,128)S(1)} %get-tuple-element.101.pair_ref), channel_id=1, source_target_pairs={{0,8},{8,0},{32,40},{40,32},{64,72},{72,64},{96,104},{104,96},{1,9... | collective-permute-start | bytes 393224 | tf_op jit(solution)/shard_map/ppermute | solution.py:33
  134.3 7.8 %parameter_update.1 = f32[32,64,512]{2,1,0:T(8,128)} custom-call(f32[8,64,512]{2,1,0:T(8,128)S(1)} %bitcast.9, f32[12,64,512]{2,1,0:T(8,128)S(1)} %bitcast.13, f32[4,64,512]{2,1,0:T(8,128)S(1)} %bitcast.12, f32[4,64,512]{2,1,0:T(8,128)S(1)} %bitcast.14, f32[4,64,512]{2,1,0:T(8,128)S(1)} %bitcast.15, f32[2,8,8,256]{3,2,1,0:T(8,128)S(1)} %get-tuple-element.101.pair_ref, ...), custom_call_target="tpu_custom_call" | custom-call | tf_op jit(solution)/shard_map/parameter_update/pallas_call | solution.py:429
  (73 shorter events, 46.1 us)
Async XLA Ops:
  5.3 11.2 %collective-permute-start = (f32[960,512]{1,0:T(8,128)S(1)}, f32[960,512]{1,0:T(8,128)S(1)}, u32[]{:S(2)}, u32[]{:S(2)}) collective-permute-start(f32[960,512]{1,0:T(8,128)S(1)} %get-tuple-element.54), channel_id=1, source_target_pairs={{0,8},{8,0},{32,40},{40,32},{64,72},{72,64},{96,104},{104,96},{1,9... | collective-permute-start | bytes 5898248 | tf_op jit(solution)/shard_map/ppermute | solution.py:33
  9.3 14.0 %collective-permute-start.4 = (f32[384,512]{1,0:T(8,128)S(1)}, f32[384,512]{1,0:T(8,128)S(1)}, u32[]{:S(2)}, u32[]{:S(2)}) collective-permute-start(f32[384,512]{1,0:T(8,128)S(1)} %get-tuple-element.60), channel_id=1, source_target_pairs={{0,8},{8,0},{32,40},{40,32},{64,72},{72,64},{96,104},{104,96},{1,9... | collective-permute-start | bytes 2359304 | tf_op jit(solution)/shard_map/ppermute | solution.py:33
  9.8 11.8 %collective-permute-start.2 = (f32[320,256]{1,0:T(8,128)S(1)}, f32[320,256]{1,0:T(8,128)S(1)}, u32[]{:S(2)}, u32[]{:S(2)}) collective-permute-start(f32[320,256]{1,0:T(8,128)S(1)} %get-tuple-element.57), channel_id=1, source_target_pairs={{0,32},{8,40},{32,64},{40,72},{64,96},{72,104},{96,0},{104,8},{1,3... | collective-permute-start | bytes 983048 | tf_op jit(solution)/shard_map/ppermute | solution.py:33
  11.5 43.4 %collective-permute-start.10 = (f32[512,512]{1,0:T(8,128)S(1)}, f32[512,512]{1,0:T(8,128)S(1)}, u32[]{:S(2)}, u32[]{:S(2)}) collective-permute-start(f32[512,512]{1,0:T(8,128)S(1)} %get-tuple-element.69), channel_id=1, source_target_pairs={{0,16},{8,24},{32,48},{40,56},{64,80},{72,88},{96,112},{104,120},{... | collective-permute-start | bytes 3145736 | tf_op jit(solution)/shard_map/ppermute | solution.py:33
  14.4 8.9 %collective-permute-start.3 = (f32[320,256]{1,0:T(8,128)S(1)}, f32[320,256]{1,0:T(8,128)S(1)}, u32[]{:S(2)}, u32[]{:S(2)}) collective-permute-start(f32[320,256]{1,0:T(8,128)S(1)} %get-tuple-element.58), channel_id=1, source_target_pairs={{0,96},{8,104},{32,0},{40,8},{64,32},{72,40},{96,64},{104,72},{1,9... | collective-permute-start | bytes 983048 | tf_op jit(solution)/shard_map/ppermute | solution.py:33
  17.8 10.9 %collective-permute-start.5 = (f32[320,256]{1,0:T(8,128)S(1)}, f32[320,256]{1,0:T(8,128)S(1)}, u32[]{:S(2)}, u32[]{:S(2)}) collective-permute-start(f32[320,256]{1,0:T(8,128)S(1)} %get-tuple-element.64), channel_id=1, source_target_pairs={{0,32},{8,40},{32,64},{40,72},{64,96},{72,104},{96,0},{104,8},{1,3... | collective-permute-start | bytes 983048 | tf_op jit(solution)/shard_map/ppermute | solution.py:33
  21.6 31.8 %collective-permute-start.11 = (f32[384,512]{1,0:T(8,128)S(1)}, f32[384,512]{1,0:T(8,128)S(1)}, u32[]{:S(2)}, u32[]{:S(2)}) collective-permute-start(f32[384,512]{1,0:T(8,128)S(1)} %get-tuple-element.70), channel_id=1, source_target_pairs={{0,8},{8,0},{32,40},{40,32},{64,72},{72,64},{96,104},{104,96},{1,9... | collective-permute-start | bytes 2359304 | tf_op jit(solution)/shard_map/ppermute | solution.py:33
  25.3 29.7 %collective-permute-start.12 = (f32[320,512]{1,0:T(8,128)S(1)}, f32[320,512]{1,0:T(8,128)S(1)}, u32[]{:S(2)}, u32[]{:S(2)}) collective-permute-start(f32[320,512]{1,0:T(8,128)S(1)} %get-tuple-element.74), channel_id=1, source_target_pairs={{0,32},{8,40},{32,64},{40,72},{64,96},{72,104},{96,0},{104,8},{1,3... | collective-permute-start | bytes 1966088 | tf_op jit(solution)/shard_map/ppermute | solution.py:33
  26.7 28.8 %collective-permute-start.13 = (f32[320,512]{1,0:T(8,128)S(1)}, f32[320,512]{1,0:T(8,128)S(1)}, u32[]{:S(2)}, u32[]{:S(2)}) collective-permute-start(f32[320,512]{1,0:T(8,128)S(1)} %get-tuple-element.75), channel_id=1, source_target_pairs={{0,96},{8,104},{32,0},{40,8},{64,32},{72,40},{96,64},{104,72},{1,9... | collective-permute-start | bytes 1966088 | tf_op jit(solution)/shard_map/ppermute | solution.py:33
  28.7 19.8 %collective-permute-start.6 = (f32[320,256]{1,0:T(8,128)S(1)}, f32[320,256]{1,0:T(8,128)S(1)}, u32[]{:S(2)}, u32[]{:S(2)}) collective-permute-start(f32[320,256]{1,0:T(8,128)S(1)} %get-tuple-element.65), channel_id=1, source_target_pairs={{0,96},{8,104},{32,0},{40,8},{64,32},{72,40},{96,64},{104,72},{1,9... | collective-permute-start | bytes 983048 | tf_op jit(solution)/shard_map/ppermute | solution.py:33
  48.5 23.9 %collective-permute-start.18 = (f32[512,512]{1,0:T(8,128)S(1)}, f32[512,512]{1,0:T(8,128)S(1)}, u32[]{:S(2)}, u32[]{:S(2)}) collective-permute-start(f32[512,512]{1,0:T(8,128)S(1)} %get-tuple-element.81), channel_id=1, source_target_pairs={{0,16},{8,24},{32,48},{40,56},{64,80},{72,88},{96,112},{104,120},{... | collective-permute-start | bytes 3145736 | tf_op jit(solution)/shard_map/ppermute | solution.py:33
  53.4 8.7 %collective-permute-start.8 = (f32[320,512]{1,0:T(8,128)S(1)}, f32[320,512]{1,0:T(8,128)S(1)}, u32[]{:S(2)}, u32[]{:S(2)}) collective-permute-start(f32[320,512]{1,0:T(8,128)S(1)} %get-tuple-element.67), channel_id=1, source_target_pairs={{0,8},{8,0},{32,40},{40,32},{64,72},{72,64},{96,104},{104,96},{1,9... | collective-permute-start | bytes 1966088 | tf_op jit(solution)/shard_map/ppermute | solution.py:33
  55.0 15.5 %collective-permute-start.19 = (f32[384,512]{1,0:T(8,128)S(1)}, f32[384,512]{1,0:T(8,128)S(1)}, u32[]{:S(2)}, u32[]{:S(2)}) collective-permute-start(f32[384,512]{1,0:T(8,128)S(1)} %get-tuple-element.82), channel_id=1, source_target_pairs={{0,8},{8,0},{32,40},{40,32},{64,72},{72,64},{96,104},{104,96},{1,9... | collective-permute-start | bytes 2359304 | tf_op jit(solution)/shard_map/ppermute | solution.py:33
  55.4 10.4 %collective-permute-start.16 = (f32[320,512]{1,0:T(8,128)S(1)}, f32[320,512]{1,0:T(8,128)S(1)}, u32[]{:S(2)}, u32[]{:S(2)}) collective-permute-start(f32[320,512]{1,0:T(8,128)S(1)} %get-tuple-element.78), channel_id=1, source_target_pairs={{0,8},{8,0},{32,40},{40,32},{64,72},{72,64},{96,104},{104,96},{1,9... | collective-permute-start | bytes 1966088 | tf_op jit(solution)/shard_map/ppermute | solution.py:33
  62.1 8.4 %collective-permute-start.20 = (f32[192,256]{1,0:T(8,128)S(1)}, f32[192,256]{1,0:T(8,128)S(1)}, u32[]{:S(2)}, u32[]{:S(2)}) collective-permute-start(f32[192,256]{1,0:T(8,128)S(1)} %get-tuple-element.83), channel_id=1, source_target_pairs={{0,32},{8,40},{32,64},{40,72},{64,96},{72,104},{96,0},{104,8},{1,3... | collective-permute-start | bytes 589832 | tf_op jit(solution)/shard_map/ppermute | solution.py:33
  65.8 16.3 %collective-permute-start.7 = (f32[320,512]{1,0:T(8,128)S(1)}, f32[320,512]{1,0:T(8,128)S(1)}, u32[]{:S(2)}, u32[]{:S(2)}) collective-permute-start(f32[320,512]{1,0:T(8,128)S(1)} %get-tuple-element.66), channel_id=1, source_target_pairs={{0,8},{8,0},{32,40},{40,32},{64,72},{72,64},{96,104},{104,96},{1,9... | collective-permute-start | bytes 1966088 | tf_op jit(solution)/shard_map/ppermute | solution.py:33
  75.1 59.2 %collective-permute-start.24 = (f32[768,512]{1,0:T(8,128)S(1)}, f32[768,512]{1,0:T(8,128)S(1)}, u32[]{:S(2)}, u32[]{:S(2)}) collective-permute-start(f32[768,512]{1,0:T(8,128)S(1)} %get-tuple-element.98), channel_id=1, source_target_pairs={{0,8},{8,0},{32,40},{40,32},{64,72},{72,64},{96,104},{104,96},{1,9... | collective-permute-start | bytes 4718600 | tf_op jit(solution)/shard_map/ppermute | solution.py:33
  78.3 17.8 %collective-permute-start.17 = (f32[320,512]{1,0:T(8,128)S(1)}, f32[320,512]{1,0:T(8,128)S(1)}, u32[]{:S(2)}, u32[]{:S(2)}) collective-permute-start(f32[320,512]{1,0:T(8,128)S(1)} %get-tuple-element.80), channel_id=1, source_target_pairs={{0,16},{8,24},{32,48},{40,56},{64,80},{72,88},{96,112},{104,120},{... | collective-permute-start | bytes 1966088 | tf_op jit(solution)/shard_map/ppermute | solution.py:33
  81.0 18.2 %collective-permute-start.14 = (f32[320,512]{1,0:T(8,128)S(1)}, f32[320,512]{1,0:T(8,128)S(1)}, u32[]{:S(2)}, u32[]{:S(2)}) collective-permute-start(f32[320,512]{1,0:T(8,128)S(1)} %get-tuple-element.76), channel_id=1, source_target_pairs={{0,32},{8,40},{32,64},{40,72},{64,96},{72,104},{96,0},{104,8},{1,3... | collective-permute-start | bytes 1966088 | tf_op jit(solution)/shard_map/ppermute | solution.py:33
  81.0 19.4 %collective-permute-start.25 = (f32[256,512]{1,0:T(8,128)S(1)}, f32[256,512]{1,0:T(8,128)S(1)}, u32[]{:S(2)}, u32[]{:S(2)}) collective-permute-start(f32[256,512]{1,0:T(8,128)S(1)} %get-tuple-element.97.refs_1_), channel_id=1, source_target_pairs={{0,2},{8,10},{32,34},{40,42},{64,66},{72,74},{96,98},{104,106},{1,... | collective-permute-start | bytes 1572872 | tf_op jit(solution)/shard_map/ppermute | solution.py:33
  82.2 20.1 %collective-permute-start.15 = (f32[320,512]{1,0:T(8,128)S(1)}, f32[320,512]{1,0:T(8,128)S(1)}, u32[]{:S(2)}, u32[]{:S(2)}) collective-permute-start(f32[320,512]{1,0:T(8,128)S(1)} %get-tuple-element.77), channel_id=1, source_target_pairs={{0,96},{8,104},{32,0},{40,8},{64,32},{72,40},{96,64},{104,72},{1,9... | collective-permute-start | bytes 1966088 | tf_op jit(solution)/shard_map/ppermute | solution.py:33
  96.1 12.0 %collective-permute-start.22 = (f32[192,512]{1,0:T(8,128)S(1)}, f32[192,512]{1,0:T(8,128)S(1)}, u32[]{:S(2)}, u32[]{:S(2)}) collective-permute-start(f32[192,512]{1,0:T(8,128)S(1)} %get-tuple-element.89), channel_id=1, source_target_pairs={{0,32},{8,40},{32,64},{40,72},{64,96},{72,104},{96,0},{104,8},{1,3... | collective-permute-start | bytes 1179656 | tf_op jit(solution)/shard_map/ppermute | solution.py:33
  99.2 9.8 %collective-permute-start.23 = (f32[192,512]{1,0:T(8,128)S(1)}, f32[192,512]{1,0:T(8,128)S(1)}, u32[]{:S(2)}, u32[]{:S(2)}) collective-permute-start(f32[192,512]{1,0:T(8,128)S(1)} %get-tuple-element.90), channel_id=1, source_target_pairs={{0,96},{8,104},{32,0},{40,8},{64,32},{72,40},{96,64},{104,72},{1,9... | collective-permute-start | bytes 1179656 | tf_op jit(solution)/shard_map/ppermute | solution.py:33
  100.3 34.0 %collective-permute-start.26 = (f32[256,512]{1,0:T(8,128)S(1)}, f32[256,512]{1,0:T(8,128)S(1)}, u32[]{:S(2)}, u32[]{:S(2)}) collective-permute-start(f32[256,512]{1,0:T(8,128)S(1)} %collective-permute-done.25), channel_id=1, source_target_pairs={{0,8},{8,0},{32,40},{40,32},{64,72},{72,64},{96,104},{104,96},{1,9... | collective-permute-start | bytes 1572872 | tf_op jit(solution)/shard_map/ppermute | solution.py:33
  (13 other events, 92.5 us)

commit v3 on v2

v3 whole, which is shorter than its diff:
```python
import jax
import jax.numpy as jnp
from jax import lax
from jax.experimental import pallas as pl
from jax.experimental.pallas import tpu as pltpu
from jax.sharding import PartitionSpec as P

GROUP = 64
BAND = 256
COLS = 512
NB = COLS // GROUP
OWN = 512
ZROWS = 320
FIRST = 64
LANES = COLS // 128
AXES = ("fsdp", "dp", "outer")
beta = 0.9

F32 = jnp.float32
BF16 = jnp.bfloat16


def place(x, y, z, core):
    return z * 32 + ((y // 2) * 2 + core) * 8 + x * 2 + y % 2


def swap(value, x=0, y=0, z=0, core=0):
    pairs = []
    for px in range(4):
        for py in range(4):
            for pz in range(4):
                for pc in range(2):
                    pairs.append((place(px, py, pz, pc), place(px ^ x, py ^ y, (pz + z) % 4, pc ^ core)))
    return lax.ppermute(value, AXES, pairs)


def cosine_columns(freq):
    freq = freq.astype(F32)[None, :]
    pos = jnp.arange(GROUP, dtype=F32)[:, None]
    scale = jnp.where(freq == 0, jnp.sqrt(1.0 / GROUP), jnp.sqrt(2.0 / GROUP)).astype(F32)
    return scale * jnp.cos(jnp.pi * (2.0 * pos + 1.0) * freq / (2.0 * GROUP))


def split(value):
    high = value.astype(BF16)
    return high, (value - high.astype(F32)).astype(BF16)


def dot(a, b):
    return jnp.dot(a, b, preferred_element_type=F32)


def piece_source(step, z, yh, core, parts_ref):
    f, r, c, top, rows = step
    return parts_ref.at[(z + f) % 4, (yh + r) % 2, (core + c) % 2, pl.ds(top, rows), :]


def mark(z, piece, term, out):
    out[...] = jnp.zeros((8, 128), F32)


def piece_call(name, parts, steps, terms, after, outs, cost=1):
    outs = outs + [((8, 128), mark)]
    outs = [out if len(out) == 3 else out + (F32,) for out in outs]
    n_terms, n_after, n_outs, n_steps = len(terms), len(after), len(outs), len(steps)
    picked = [i for i, t in enumerate(terms) if isinstance(t, tuple)]

    def kernel(parts_ref, *refs):
        refs = list(refs)
        take = lambda n: [refs.pop(0) for _ in range(n)]
        term_refs, _, out_refs = take(n_terms), take(n_after), take(n_outs)
        bufs, held, sems = take(n_steps), take(len(picked)), take(n_steps + len(picked))
        z, dp, x = lax.axis_index("fsdp"), lax.axis_index("dp"), lax.axis_index("outer") // 2
        sources = [piece_source(s, z, dp // 2, dp % 2, parts_ref) for s in steps]
        sources += [terms[i][2](x, term_refs[i]) for i in picked]
        loads = []
        for src, buf, sem in zip(sources, bufs + held, sems):
            copy = pltpu.make_async_copy(src, buf, sem)
            copy.start()
            loads.append(copy)
        waiting = set(range(len(loads)))

        def loaded(i):
            if i in waiting:
                waiting.remove(i)
                loads[i].wait()
            return (bufs + held)[i]

        def term(i):
            return loaded(n_steps + picked.index(i)) if i in picked else term_refs[i]

        for (_, body, _), ref in zip(outs, out_refs):
            body(z, loaded, term, ref)
        for i in sorted(waiting):
            loads[i].wait()

    here, anywhere = pl.BlockSpec(memory_space=pltpu.VMEM), pl.BlockSpec(memory_space=pl.ANY)
    hold = lambda v: pltpu.with_memory_space_constraint(v, pltpu.VMEM)
    return pl.pallas_call(
        kernel,
        in_specs=[pl.BlockSpec(memory_space=pltpu.HBM)] + [anywhere if i in picked else here for i in range(n_terms)]
        + [anywhere] * n_after,
        out_specs=[here] * n_outs,
        out_shape=[pltpu.VMEM(s, t) for s, _, t in outs],
        scratch_shapes=[pltpu.VMEM((s[4], COLS), BF16) for s in steps]
        + [pltpu.VMEM(terms[i][1], F32) for i in picked]
        + [pltpu.SemaphoreType.DMA] * (n_steps + len(picked)),
        compiler_params=pltpu.CompilerParams(vmem_limit_bytes=24 * 2**20),
        cost_estimate=pl.CostEstimate(flops=1, bytes_accessed=cost, transcendentals=0),
        name=name,
    )(parts, *[t[0] if i in picked else hold(t) for i, t in enumerate(terms)], *after)


def encode(mom, vert, horiz):
    rows = mom.shape[0]
    w_high, w_low = split(horiz)
    x_high, x_low = split(mom)
    out = []
    for b in range(NB):
        cut = slice(b * GROUP, (b + 1) * GROUP)
        half = dot(x_high[:, cut], w_high) + dot(x_low[:, cut], w_high) + dot(x_high[:, cut], w_low)
        out.append(jnp.sum(half.reshape(rows // GROUP, GROUP, BAND) * vert[None], axis=1))
    return out


def step_rows(grad_parts, momentum, params, vert, horiz):
    parts = pltpu.with_memory_space_constraint(grad_parts.reshape(4, 2, 2, OWN, COLS), pltpu.HBM)
    vert_t, horiz_t = vert.T, horiz.T
    zr, yr, half = ZROWS, OWN - ZROWS, COLS // 2
    left, right = slice(0, half), slice(half, COLS)
    call = lambda name, *rest, **options: piece_call(name, parts, *rest, **options)
    up, down = (lambda v: swap(v, z=1)), (lambda v: swap(v, z=3))
    OPP, UP, DOWN, MINE = 2, 1, 3, 0

    def z_rows(f, r, c):
        return (f, r, c, 0, zr)

    def y_rows(f, r, c):
        return (f, r, c, zr, yr)

    def widen(name, groups, after):
        outs, first = [], 0
        for group in groups:
            def body(z, piece, term, out, group=group, first=first):
                top = 0
                for i, step in enumerate(group):
                    out[top:top + step[4], :] = piece(first + i)[...].astype(F32)
                    top += step[4]

            outs.append(((sum(s[4] for s in group), COLS), body))
            first += len(group)
        return call(name, [s for group in groups for s in group], [], after, outs)

    def add(i_pieces, i_term, first, cols=slice(None), half_terms=(), full_terms=()):
        def run(z, piece, term, out):
            top = 0
            for i in i_pieces:
                n = piece(i).shape[0]
                cut = slice(top, top + n)
                value = term(i_term)[first + top:first + top + n, cols] + piece(i)[:, cols].astype(F32)
                for k in full_terms:
                    value = value + term(k)[cut, cols]
                for k in half_terms:
                    value = value + term(k)[cut]
                out[cut, :] = value
                top += n
        return run

    def side(i_pieces, i_term, first, h_add, i_add):
        def run(z, piece, term, out):
            for h, cols in enumerate((left, right)):
                body = add(i_pieces, i_term, first, cols, (i_add,) if h == h_add else ())
                body(z, piece, term, out.at[:, cols])
        return run

    def pack(z, piece, term, out):
        odd = (lax.axis_index("outer") // 2) % 2
        n = OWN // 2
        out[:OWN, :] = term(0)[...]
        out[pl.ds(pl.multiple_of(OWN + odd * n, n), n), :] = term(1)[...]
        out[pl.ds(pl.multiple_of(OWN + (1 - odd) * n, n), n), :] = term(2)[...]

    w_first, ta = widen("widen_a", [[z_rows(OPP, 0, 1), z_rows(OPP, 1, 1), y_rows(OPP, 1, 1)]], [])
    c_first = swap(w_first, core=1)
    *w_b, tb = widen("widen_b", [
        [z_rows(UP, 0, 1), z_rows(UP, 1, 1)], [z_rows(DOWN, 0, 1), z_rows(DOWN, 1, 1)],
        [y_rows(UP, 1, 1), y_rows(DOWN, 1, 1), y_rows(MINE, 1, 1), y_rows(OPP, 0, 1)],
        [z_rows(MINE, 0, 1), z_rows(MINE, 1, 1)],
        [y_rows(UP, 0, 1), y_rows(DOWN, 0, 1), y_rows(MINE, 0, 1)]], [ta])
    c_up, c_down, c_cross, c_own, c_rest = [swap(w, core=1) for w in w_b]
    def params_part(top, n):
        def pick(x, ref):
            return ref.at[pl.ds(pl.multiple_of((x % 2) * (OWN // 2) + top, 64), n), :]
        return (params, (n, COLS), pick)

    def with_params(body, i_params):
        def run(z, piece, term, out):
            n = out.shape[0] - term(i_params).shape[0]
            body(z, piece, term, out.at[:n])
            out[n:, :] = term(i_params)[...]
        return run

    u1, d1, y1, t1 = call(
        "opposite", [z_rows(OPP, 0, 0), z_rows(OPP, 1, 0), y_rows(OPP, 1, 0)], [c_first, params_part(0, FIRST)], [tb],
        [((2 * zr, half), add((0, 1), 0, 0, left)), ((2 * zr, half), add((0, 1), 0, 0, right)),
         ((yr + FIRST, COLS), with_params(add((2,), 0, 2 * zr), 1))])
    gu1, gd1, gy1 = up(u1), down(d1), swap(y1, y=2)

    table_high, table_low, tt = call("band_table", [], [vert_t, horiz_t], [t1], band_table())
    fold = yr // 2

    def onward(i, first, h_add, i_add, cols):
        def run(z, piece, term, out):
            side((2 * i, 2 * i + 1), i, 0, h_add, i_add)(z, piece, term, out.at[:2 * zr])
            value = term(4)[3 * yr:, cols] + term(5)[:yr, cols] + piece(7)[:, cols].astype(F32)
            out[2 * zr:, left] = value[:fold]
            out[2 * zr:, right] = value[fold:]
        return run

    u2, d2, y2, t2 = call(
        "sides", [z_rows(UP, 0, 0), z_rows(UP, 1, 0), z_rows(DOWN, 0, 0), z_rows(DOWN, 1, 0),
                  y_rows(UP, 1, 0), y_rows(DOWN, 1, 0), y_rows(MINE, 1, 0), y_rows(OPP, 0, 0)],
        [c_up, c_down, gu1, gd1, c_cross, gy1, params_part(FIRST, OWN // 2 - FIRST)], [tt],
        [((2 * zr + fold, COLS), onward(0, 0, 0, 2, left)), ((2 * zr + fold, COLS), onward(1, 0, 1, 3, right)),
         ((3 * yr + OWN // 2 - FIRST, COLS), with_params(add((4, 5, 6), 4, 0), 6))])
    gu2, gd2, gy2 = up(u2), down(d2), swap(y2, y=2)

    def own_body(r):
        def run(z, piece, term, out):
            cut = slice(r * zr, (r + 1) * zr)
            out[...] = term(0)[cut] + piece(r)[...].astype(F32) + (term(1)[cut] + term(2)[cut])
        return run

    def last_side(i, h_add, i_add):
        def run(z, piece, term, out):
            cut = slice(i * yr, (i + 1) * yr)
            for h, cols in enumerate((left, right)):
                value = term(3)[cut, cols] + term(4)[cut, cols] + piece(2 + i)[:, cols].astype(F32)
                if h == h_add:
                    out[:fold, cols] = value[:fold] + term(i_add)[2 * zr:, left]
                    out[fold:, cols] = value[fold:] + term(i_add)[2 * zr:, right]
                else:
                    out[:, cols] = value
        return run

    def last_own_body(z, piece, term, out):
        out[...] = term(3)[2 * yr:3 * yr] + term(4)[2 * yr:] + piece(4)[...].astype(F32)

    def far_body(z, piece, term, out):
        out[:FIRST, :] = term(5)[yr:, :]
        out[FIRST:, :] = term(3)[3 * yr:, :]

    y3, u4, d4, near, last_own, far_half, t6 = call(
        "own", [z_rows(MINE, 0, 0), z_rows(MINE, 1, 0), y_rows(UP, 0, 0), y_rows(DOWN, 0, 0), y_rows(MINE, 0, 0)],
        [c_own, gu2, gd2, gy2, c_rest, gy1], [t2],
        [((zr, COLS), own_body(1)), ((yr, COLS), last_side(0, 0, 1)), ((yr, COLS), last_side(1, 1, 2)),
         ((zr, COLS), own_body(0)), ((yr, COLS), last_own_body),
         ((OWN // 2, COLS), far_body)])
    far_other = swap(far_half, x=1)
    gy3, gu4, gd4 = swap(y3, y=2), up(u4), down(d4)
    def momentum_rows(top, n):
        return (momentum, (n, COLS), lambda x, ref: ref.at[pl.ds(top, n), :])

    def near_mom(z, piece, term, out):
        out[...] = beta * term(2)[...] + (term(0)[...] + term(1)[...]) * (1.0 / 16.0)
        near_mom.value = out

    def near_shared(z, piece, term, out):
        for b, value in enumerate(encode(near_mom.value[...], term(3)[...], term(4)[...])):
            out[b] = value

    nz, ny = zr // GROUP, yr // GROUP
    mom_top, shared_top, t7 = call(
        "near_momentum", [], [near, gy3, momentum_rows(0, zr), vert, horiz], [t6],
        [((zr, COLS), near_mom), ((NB, nz, BAND), near_shared)], cost=9 * 10**6,
    )

    def last_mom(z, piece, term, out):
        grad = term(0)[...] + (term(1)[...] + term(2)[...])
        out[...] = beta * term(3)[...] + grad * (1.0 / 16.0)
        last_mom.value = out

    def last_shared(z, piece, term, out):
        for b, value in enumerate(encode(last_mom.value[...], term(4)[...], term(5)[...])):
            out[b, :nz, :] = term(6)[b]
            out[b, nz:, :] = value

    mom_low, shared, t8 = call(
        "last_momentum", [], [last_own, gu4, gd4, momentum_rows(zr, yr), vert, horiz, shared_top], [t7],
        [((yr, COLS), last_mom), ((NB, nz + ny, BAND), last_shared)],
    )

    packed, _ = call("params_pack", [], [params, far_half, far_other], [t8], [((2 * OWN, COLS), pack)])
    packed_core = swap(packed, core=1)

    def residual(z, piece, term, out):
        high, low = split(term(4)[...])
        w_both = jnp.concatenate([high, low], axis=1)
        vert_now = term(3)[...][None]
        for pair in range(NB // 2):
            sides = []
            for b in (2 * pair, 2 * pair + 1):
                wide = (term(2)[b][:, None, :] * vert_now).reshape(OWN, BAND)
                wide_high, wide_low = split(wide)
                both = dot(wide_high, w_both)
                sides.append(both[:, :GROUP] + both[:, GROUP:] + dot(wide_low, w_both[:, :GROUP]))
            cols = slice(pair * 2 * GROUP, (pair + 1) * 2 * GROUP)
            value = jnp.concatenate(sides, axis=1)
            out[:zr, cols] = term(0)[:, cols] - value[:zr]
            out[zr:, cols] = term(1)[:, cols] - value[zr:]

    new_momentum, t9 = call("momentum_residual", [], [mom_top, mom_low, shared, vert, horiz_t], [t8],
                            [((OWN, COLS), residual)], cost=9 * 10**6)

    def sum_four(z, piece, term, out):
        out[...] = (term(0)[...] + term(1)[...]) + (term(2)[...] + term(3)[...])

    def sum_pairs(z, piece, term, out):
        out[0] = term(0)[...] + term(1)[...]
        out[1] = term(2)[...] + term(3)[...]

    total, t10 = call("sum_x", [], [shared] + [swap(shared, x=k) for k in (1, 2, 3)], [t9], [(shared.shape, sum_four)])
    pair, _ = call("sum_y", [], [total] + [swap(total, y=k) for k in (1, 2, 3)], [], [((2,) + shared.shape, sum_pairs)])
    new_params = update_call(packed, packed_core, pair, swap(pair, core=1), table_high, table_low)
    return new_momentum, new_params


def band_table():
    held = {}

    def high(z, piece, term, out):
        lane = lax.broadcasted_iota(jnp.int32, (BAND, 2 * GROUP), 1)
        horiz = jnp.concatenate([term(1)[...]] * 2, axis=1)
        vert = term(0)[...]
        held["low"] = []
        for m in range(0, GROUP, 2):
            product = jnp.where(lane < GROUP, vert[:, m:m + 1], vert[:, m + 1:m + 2]) * horiz
            top, rest = split(product)
            out[:, m * GROUP:(m + 2) * GROUP] = top
            held["low"].append(rest)

    def low(z, piece, term, out):
        for i, rest in enumerate(held["low"]):
            out[:, 2 * i * GROUP:2 * (i + 1) * GROUP] = rest

    return [((BAND, GROUP * GROUP), high, BF16), ((BAND, GROUP * GROUP), low, BF16)]


def update_kernel(rows_ref, rows_core_ref, pair_ref, pair_core_ref, high_ref, low_ref, out_ref, coeff, field, sems):
    dp = lax.axis_index("dp")
    nblock = OWN // GROUP
    for k in range(4):
        coeff[:, k] = (pair_ref, pair_core_ref)[k % 2][k // 2]
    c_high, c_low = split(coeff[...].reshape(NB * 4 * nblock, BAND) * (1.0 / 8.0))
    both = jnp.concatenate([c_high, c_low], axis=0)
    lane = lax.broadcasted_iota(jnp.int32, (4 * nblock, 2 * GROUP), 1)
    first = lane < GROUP
    step = 8
    stores = []
    for c in range(GROUP // step):
        cols = slice(c * step * GROUP, (c + 1) * step * GROUP)
        wide = dot(both, high_ref[:, cols])
        value = wide[:NB * 4 * nblock] + wide[NB * 4 * nblock:] + dot(c_high, low_ref[:, cols])
        at = slice(c * step, (c + 1) * step)
        for b in range(0, NB, 2):
            x0, x1 = [value[i * 4 * nblock:(i + 1) * 4 * nblock] for i in (b, b + 1)]
            rows_m = []
            for lt in range(step // 2):
                lanes = slice(lt * 2 * GROUP, (lt + 1) * 2 * GROUP)
                y0, y1 = x0[:, lanes], x1[:, lanes]
                rows_m.append(jnp.where(first, y0, pltpu.roll(y1, GROUP, 1)))
                rows_m.append(jnp.where(first, pltpu.roll(y0, GROUP, 1), y1))
            turned = jnp.swapaxes(jnp.stack(rows_m), 0, 1)
            out_cols = slice(b * GROUP, (b + 2) * GROUP)
            for k in range(4):
                held = (rows_ref, rows_core_ref)[k % 2][k // 2, :, at, out_cols]
                field[k, :, at, out_cols] = held - turned[k * nblock:(k + 1) * nblock]
        for k in range(4):
            store = pltpu.make_async_copy(field.at[k, :, pl.ds(c * step, step), :],
                                          out_ref.at[dp ^ k, :, pl.ds(c * step, step), :], sems.at[c * 4 + k])
            store.start()
            stores.append(store)
    for store in stores:
        store.wait()


def update_call(rows, rows_core, *arrays):
    shape = (2, OWN // GROUP, GROUP, COLS)
    arrays = (rows.reshape(shape), rows_core.reshape(shape)) + arrays
    return pl.pallas_call(
        update_kernel,
        in_specs=[pl.BlockSpec(memory_space=pltpu.VMEM)] * len(arrays),
        out_specs=pl.BlockSpec(memory_space=pl.ANY),
        out_shape=jax.ShapeDtypeStruct((4, OWN // GROUP, GROUP, COLS), F32),
        scratch_shapes=[
            pltpu.VMEM((NB, 4, OWN // GROUP, BAND), F32),
            pltpu.VMEM((4, OWN // GROUP, GROUP, COLS), F32),
            pltpu.SemaphoreType.DMA((4 * GROUP // 8,)),
        ],
        compiler_params=pltpu.CompilerParams(vmem_limit_bytes=24 * 2**20),
        name="parameter_update",
    )(*[pltpu.with_memory_space_constraint(a, pltpu.VMEM) for a in arrays]).reshape(4 * OWN, COLS)


def local(grad_parts, momentum, params, band):
    band = band.astype(jnp.int32)
    vert = cosine_columns(band // GROUP)
    horiz = cosine_columns(band % GROUP)
    new_momentum, new_params = step_rows(grad_parts, momentum[0], params, vert, horiz)
    return (new_momentum[None], new_params)


def solution(mesh):
    return jax.shard_map(
        local,
        mesh=mesh,
        in_specs=(
            P("outer", "fsdp", "dp", None, None),
            P("outer", ("fsdp", "dp"), None),
            P(("fsdp", "dp"), None),
            P(),
        ),
        out_specs=(P("outer", ("fsdp", "dp"), None), P("fsdp", None)),
        check_vma=False,
    )
```

time: 143 us -> 115 us (0.80)
  Pallas kernels: 42.3 us -> 20.3 us
  starting transfers between devices: 49.8 us -> 36.2 us
  waiting for transfers between devices: 47.7 us -> 54.4 us
    pallas_call x18 -> x12, Pallas kernels: 34.5 us -> 16.8 us  [piece_call(): pl.pallas_call(kernel, in_specs=[pl.BlockSpec(memory_space=pltpu.HBM)] +...]
    ppermute x34 -> x24, starting transfers between devices: 49.8 us -> 36.2 us  [swap(): return lax.ppermute(value, AXES, pairs)]
    ppermute x34 -> x24, waiting for transfers between devices: 47.7 us -> 54.4 us  [swap(): return lax.ppermute(value, AXES, pairs)]
    pallas_call x1, Pallas kernels: 7.79 us -> 3.46 us  [update_call(): pl.pallas_call(update_kernel, in_specs=[pl.BlockSpec(memory_space=pltpu.V...]
  transfers between devices with their start and end apart: 34 -> 24, of which waited for: 14 -> 10; matrix products, arithmetic and copies ran while one was open for 1% -> 2% of each run, Pallas kernels for 23% -> 10%
where the time goes in v3:
time: 115 us; the launch traced here: 114 us
  waiting for transfers between devices  54.4 us (47%)
  starting transfers between devices  36.2 us (31%)
  Pallas kernels  20.3 us (18%)
  other arithmetic  1.48 us (1%)
    ppermute x24, waiting for transfers between devices, swap(): return lax.ppermute(value, AXES, pairs)  54.4 us
    ppermute x24, starting transfers between devices, swap(): return lax.ppermute(value, AXES, pairs)  36.2 us
    pallas_call x12, Pallas kernels, piece_call(): pl.pallas_call(kernel, in_specs=[pl.BlockSpec(memory_space=pltpu.HBM)] +...  16.8 us
    pallas_call x1, Pallas kernels, update_call(): pl.pallas_call(update_kernel, in_specs=[pl.BlockSpec(memory_space=pltpu.V...  3.46 us
  transfers between devices with their start and end apart: 24, of which 10 were waited for; matrix products, arithmetic and copies ran while one was open for 2% of the time, Pallas kernels for 10%

profile of v3, /device:TPU:1, one launch (start us, length us, event | category | flops | bytes accessed | tf_op | source)
XLA Modules:
  0.0 114.3 jit_solution(17819205950590088523)
XLA Ops:
  3.3 2.1 %widen_b.1 = (f32[640,512]{1,0:T(8,128)S(1)}, f32[640,512]{1,0:T(8,128)S(1)}, f32[768,512]{1,0:T(8,128)S(1)}, f32[640,512]{1,0:T(8,128)S(1)}, f32[576,512]{1,0:T(8,128)S(1)}, /*index=5*/f32[8,128]{1,0:T(8,128)S(1)}) custom-call(bf16[4,2,2,512,512]{4,3,2,1,0:T(8,128)(2,1)} %bitcast.12, f32[8,128]{1,0:T(8,128)S(1)} %get-tuple-element.39.refs_0_), custom_call_target="tpu_custom_call" | custom-call | flops 1 | bytes 1 | tf_op jit(solution)/shard_map/widen_b/pallas_call | solution.py:99
  7.9 1.8 %collective-permute-start.4 = (f32[640,256]{1,0:T(8,128)S(1)}, f32[640,256]{1,0:T(8,128)S(1)}, u32[]{:S(2)}, u32[]{:S(2)}) collective-permute-start(f32[640,256]{1,0:T(8,128)S(1)} %get-tuple-element.45), channel_id=1, source_target_pairs={{0,32},{8,40},{32,64},{40,72},{64,96},{72,104},{96,0},{104,8},{1,3... | collective-permute-start | bytes 1966088 | tf_op jit(solution)/shard_map/ppermute | solution.py:34
  9.6 2.2 %collective-permute-start.5 = (f32[640,256]{1,0:T(8,128)S(1)}, f32[640,256]{1,0:T(8,128)S(1)}, u32[]{:S(2)}, u32[]{:S(2)}) collective-permute-start(f32[640,256]{1,0:T(8,128)S(1)} %get-tuple-element.46), channel_id=1, source_target_pairs={{0,96},{8,104},{32,0},{40,8},{64,32},{72,40},{96,64},{104,72},{1,9... | collective-permute-start | bytes 1966088 | tf_op jit(solution)/shard_map/ppermute | solution.py:34
  11.9 2.9 %collective-permute-start.7 = (f32[256,512]{1,0:T(8,128)S(1)}, f32[256,512]{1,0:T(8,128)S(1)}, u32[]{:S(2)}, u32[]{:S(2)}) collective-permute-start(f32[256,512]{1,0:T(8,128)S(1)} %get-tuple-element.48), channel_id=1, source_target_pairs={{0,16},{8,24},{32,48},{40,56},{64,80},{72,88},{96,112},{104,120},{... | collective-permute-start | bytes 1572872 | tf_op jit(solution)/shard_map/ppermute | solution.py:34
  15.8 2.4 %band_table.1 = (bf16[256,4096]{1,0:T(8,128)(2,1)S(1)}, bf16[256,4096]{1,0:T(8,128)(2,1)S(1)}, f32[8,128]{1,0:T(8,128)S(1)}) custom-call(bf16[4,2,2,512,512]{4,3,2,1,0:T(8,128)(2,1)} %bitcast.14, f32[256,64]{1,0:T(8,128)S(1)} %get-tuple-element.85.refs_0_, f32[256,64]{1,0:T(8,128)S(1)} %get-tuple-element.84.refs_1_.refs_4_, ...), custom_call_target="tpu_custom_call" | custom-call | flops 1 | bytes 1 | tf_op jit(solution)/shard_map/band_table/pallas_call | solution.py:99
  18.2 8.0 %collective-permute-done.7.refs_5_ = f32[256,512]{1,0:T(8,128)S(1)} collective-permute-done((f32[256,512]{1,0:T(8,128)S(1)}, f32[256,512]{1,0:T(8,128)S(1)}, u32[]{:S(2)}, u32[]{:S(2)}) %collective-permute-start.7) | collective-permute-done | bytes 524320 | tf_op jit(solution)/shard_map/ppermute | solution.py:34
  26.6 2.0 %sides.1 = (f32[736,512]{1,0:T(8,128)S(1)}, f32[736,512]{1,0:T(8,128)S(1)}, f32[768,512]{1,0:T(8,128)S(1)}, f32[8,128]{1,0:T(8,128)S(1)}) custom-call(bf16[4,2,2,512,512]{4,3,2,1,0:T(8,128)(2,1)} %bitcast.15, f32[640,512]{1,0:T(8,128)S(1)} %collective-permute-done.1.refs_0_, f32[640,512]{1,0:T(8,128)S(1)} %collective-permute-done.2.refs_1_, ...), custom_call_target="tpu_custom_call" | custom-call | flops 1 | bytes 1 | tf_op jit(solution)/shard_map/sides/pallas_call | solution.py:99
  28.6 3.0 %collective-permute-start.10 = (f32[768,512]{1,0:T(8,128)S(1)}, f32[768,512]{1,0:T(8,128)S(1)}, u32[]{:S(2)}, u32[]{:S(2)}) collective-permute-start(f32[768,512]{1,0:T(8,128)S(1)} %get-tuple-element.53), channel_id=1, source_target_pairs={{0,16},{8,24},{32,48},{40,56},{64,80},{72,88},{96,112},{104,120},{... | collective-permute-start | bytes 4718600 | tf_op jit(solution)/shard_map/ppermute | solution.py:34
  31.9 2.3 %collective-permute-start.9 = (f32[736,512]{1,0:T(8,128)S(1)}, f32[736,512]{1,0:T(8,128)S(1)}, u32[]{:S(2)}, u32[]{:S(2)}) collective-permute-start(f32[736,512]{1,0:T(8,128)S(1)} %get-tuple-element.52), channel_id=1, source_target_pairs={{0,96},{8,104},{32,0},{40,8},{64,32},{72,40},{96,64},{104,72},{1,9... | collective-permute-start | bytes 4521992 | tf_op jit(solution)/shard_map/ppermute | solution.py:34
  34.2 2.0 %collective-permute-start = (f32[640,512]{1,0:T(8,128)S(1)}, f32[640,512]{1,0:T(8,128)S(1)}, u32[]{:S(2)}, u32[]{:S(2)}) collective-permute-start(f32[640,512]{1,0:T(8,128)S(1)} %get-tuple-element.40), channel_id=1, source_target_pairs={{0,8},{8,0},{32,40},{40,32},{64,72},{72,64},{96,104},{104,96},{1,9... | collective-permute-start | bytes 3932168 | tf_op jit(solution)/shard_map/ppermute | solution.py:34
  36.2 4.3 %collective-permute-done.11.refs_4_ = f32[576,512]{1,0:T(8,128)S(1)} collective-permute-done((f32[576,512]{1,0:T(8,128)S(1)}, f32[576,512]{1,0:T(8,128)S(1)}, u32[]{:S(2)}, u32[]{:S(2)}) %collective-permute-start.11) | collective-permute-done | bytes 1179680 | tf_op jit(solution)/shard_map/ppermute | solution.py:34
  40.6 25.3 %collective-permute-done.8.refs_1_ = f32[736,512]{1,0:T(8,128)S(1)} collective-permute-done((f32[736,512]{1,0:T(8,128)S(1)}, f32[736,512]{1,0:T(8,128)S(1)}, u32[]{:S(2)}, u32[]{:S(2)}) %collective-permute-start.8) | collective-permute-done | bytes 1507360 | tf_op jit(solution)/shard_map/ppermute | solution.py:34
  65.9 1.9 %own.1 = (f32[320,512]{1,0:T(8,128)S(1)}, f32[192,512]{1,0:T(8,128)S(1)}, f32[192,512]{1,0:T(8,128)S(1)}, f32[320,512]{1,0:T(8,128)S(1)}, f32[192,512]{1,0:T(8,1...) custom-call(bf16[4,2,2,512,512]{4,3,2,1,0:T(8,128)(2,1)} %bitcast.16, ...), custom_call_target="tpu_custom_call" | custom-call | flops 1 | bytes 1 | tf_op jit(solution)/shard_map/own/pallas_call | solution.py:99
  67.7 2.0 %collective-permute-start.12 = (f32[320,512]{1,0:T(8,128)S(1)}, f32[320,512]{1,0:T(8,128)S(1)}, u32[]{:S(2)}, u32[]{:S(2)}) collective-permute-start(f32[320,512]{1,0:T(8,128)S(1)} %get-tuple-element.57), channel_id=1, source_target_pairs={{0,16},{8,24},{32,48},{40,56},{64,80},{72,88},{96,112},{104,120},{... | collective-permute-start | bytes 1966088 | tf_op jit(solution)/shard_map/ppermute | solution.py:34
  71.0 2.7 %collective-permute-start.14 = (f32[192,512]{1,0:T(8,128)S(1)}, f32[192,512]{1,0:T(8,128)S(1)}, u32[]{:S(2)}, u32[]{:S(2)}) collective-permute-start(f32[192,512]{1,0:T(8,128)S(1)} %get-tuple-element.62), channel_id=1, source_target_pairs={{0,96},{8,104},{32,0},{40,8},{64,32},{72,40},{96,64},{104,72},{1,9... | collective-permute-start | bytes 1179656 | tf_op jit(solution)/shard_map/ppermute | solution.py:34
  74.2 9.0 %collective-permute-done.12.refs_1_ = f32[320,512]{1,0:T(8,128)S(1)} collective-permute-done((f32[320,512]{1,0:T(8,128)S(1)}, f32[320,512]{1,0:T(8,128)S(1)}, u32[]{:S(2)}, u32[]{:S(2)}) %collective-permute-start.12) | collective-permute-done | bytes 655392 | tf_op jit(solution)/shard_map/ppermute | solution.py:34
  86.5 3.3 %collective-permute-start.16 = (f32[1024,512]{1,0:T(8,128)S(1)}, f32[1024,512]{1,0:T(8,128)S(1)}, u32[]{:S(2)}, u32[]{:S(2)}) collective-permute-start(f32[1024,512]{1,0:T(8,128)S(1)} %get-tuple-element.70), channel_id=1, source_target_pairs={{0,8},{8,0},{32,40},{40,32},{64,72},{72,64},{96,104},{104,96},{1,9... | collective-permute-start | bytes 6291464 | tf_op jit(solution)/shard_map/ppermute | solution.py:34
  91.0 2.4 %collective-permute-start.18 = (f32[8,8,256]{2,1,0:T(8,128)S(1)}, f32[8,8,256]{2,1,0:T(8,128)S(1)}, u32[]{:S(2)}, u32[]{:S(2)}) collective-permute-start(f32[8,8,256]{2,1,0:T(8,128)S(1)} %get-tuple-element.66.refs_2_.refs_0_), channel_id=1, source_target_pairs={{0,4},{8,12},{32,36},{40,44},{64,68},{72,76},{96,100},{104,108},{1... | collective-permute-start | bytes 196616 | tf_op jit(solution)/shard_map/ppermute | solution.py:34
  93.6 1.5 %momentum_residual.1 = (f32[512,512]{1,0:T(8,128)S(1)}, f32[8,128]{1,0:T(8,128)S(1)}) custom-call(bf16[4,2,2,512,512]{4,3,2,1,0:T(8,128)(2,1)} %bitcast.20, f32[320,512]{1,0:T(8,128)S(1)} %get-tuple-element.59.refs_0_, f32[192,512]{1,0:T(8,128)S(1)} %get-tuple-element.65.refs_1_, f32[8,8,256]{2,1,0:T(8,128)S(1)} %get-tuple-element.66.refs_2_.refs_0_, ...), custom_call_target="tpu_custom_call" | custom-call | flops 1 | bytes 9000000 | tf_op jit(solution)/shard_map/momentum_residual/pallas_call | solution.py:99
  95.2 1.9 %collective-permute-done.18.refs_2_ = f32[8,8,256]{2,1,0:T(8,128)S(1)} collective-permute-done((f32[8,8,256]{2,1,0:T(8,128)S(1)}, f32[8,8,256]{2,1,0:T(8,128)S(1)}, u32[]{:S(2)}, u32[]{:S(2)}) %collective-permute-start.18) | collective-permute-done | bytes 65568 | tf_op jit(solution)/shard_map/ppermute | solution.py:34
  98.9 2.6 %collective-permute-start.21 = (f32[8,8,256]{2,1,0:T(8,128)S(1)}, f32[8,8,256]{2,1,0:T(8,128)S(1)}, u32[]{:S(2)}, u32[]{:S(2)}) collective-permute-start(f32[8,8,256]{2,1,0:T(8,128)S(1)} %get-tuple-element.72.refs_0_), channel_id=1, source_target_pairs={{0,16},{8,24},{32,48},{40,56},{64,80},{72,88},{96,112},{104,120},{... | collective-permute-start | bytes 196616 | tf_op jit(solution)/shard_map/ppermute | solution.py:34
  103.8 2.7 %collective-permute-done.22.refs_3_ = f32[8,8,256]{2,1,0:T(8,128)S(1)} collective-permute-done((f32[8,8,256]{2,1,0:T(8,128)S(1)}, f32[8,8,256]{2,1,0:T(8,128)S(1)}, u32[]{:S(2)}, u32[]{:S(2)}) %collective-permute-start.22) | collective-permute-done | bytes 65568 | tf_op jit(solution)/shard_map/ppermute | solution.py:34
  107.1 2.6 %collective-permute-start.23 = (f32[2,8,8,256]{3,2,1,0:T(8,128)S(1)}, f32[2,8,8,256]{3,2,1,0:T(8,128)S(1)}, u32[]{:S(2)}, u32[]{:S(2)}) collective-permute-start(f32[2,8,8,256]{3,2,1,0:T(8,128)S(1)} %get-tuple-element.73.pair_ref), channel_id=1, source_target_pairs={{0,8},{8,0},{32,40},{40,32},{64,72},{72,64},{96,104},{104,96},{1,9... | collective-permute-start | bytes 393224 | tf_op jit(solution)/shard_map/ppermute | solution.py:34
  110.7 3.5 %parameter_update.1 = f32[4,8,64,512]{3,2,1,0:T(8,128)} custom-call(f32[2,8,64,512]{3,2,1,0:T(8,128)S(1)} %bitcast.9, f32[2,8,64,512]{3,2,1,0:T(8,128)S(1)} %bitcast.10, f32[2,8,8,256]{3,2,1,0:T(8,128)S(1)} %get-tuple-element.73.pair_ref, f32[2,8,8,256]{3,2,1,0:T(8,128)S(1)} %collective-permute-done.23.pair_core_ref, ...), custom_call_target="tpu_custom_call" | custom-call | tf_op jit(solution)/shard_map/parameter_update/pallas_call | solution.py:390
  (48 shorter events, 19.0 us)
Async XLA Ops:
  1.8 4.7 %collective-permute-start.3 = (f32[832,512]{1,0:T(8,128)S(1)}, f32[832,512]{1,0:T(8,128)S(1)}, u32[]{:S(2)}, u32[]{:S(2)}) collective-permute-start(f32[832,512]{1,0:T(8,128)S(1)} %get-tuple-element.43), channel_id=1, source_target_pairs={{0,8},{8,0},{32,40},{40,32},{64,72},{72,64},{96,104},{104,96},{1,9... | collective-permute-start | bytes 5111816 | tf_op jit(solution)/shard_map/ppermute | solution.py:34
  5.5 6.4 %collective-permute-start.1 = (f32[640,512]{1,0:T(8,128)S(1)}, f32[640,512]{1,0:T(8,128)S(1)}, u32[]{:S(2)}, u32[]{:S(2)}) collective-permute-start(f32[640,512]{1,0:T(8,128)S(1)} %get-tuple-element.41), channel_id=1, source_target_pairs={{0,8},{8,0},{32,40},{40,32},{64,72},{72,64},{96,104},{104,96},{1,9... | collective-permute-start | bytes 3932168 | tf_op jit(solution)/shard_map/ppermute | solution.py:34
  5.6 12.6 %collective-permute-start.6 = (f32[768,512]{1,0:T(8,128)S(1)}, f32[768,512]{1,0:T(8,128)S(1)}, u32[]{:S(2)}, u32[]{:S(2)}) collective-permute-start(f32[768,512]{1,0:T(8,128)S(1)} %get-tuple-element.47), channel_id=1, source_target_pairs={{0,8},{8,0},{32,40},{40,32},{64,72},{72,64},{96,104},{104,96},{1,9... | collective-permute-start | bytes 4718600 | tf_op jit(solution)/shard_map/ppermute | solution.py:34
  6.0 12.1 %collective-permute-start.2 = (f32[640,512]{1,0:T(8,128)S(1)}, f32[640,512]{1,0:T(8,128)S(1)}, u32[]{:S(2)}, u32[]{:S(2)}) collective-permute-start(f32[640,512]{1,0:T(8,128)S(1)} %get-tuple-element.42), channel_id=1, source_target_pairs={{0,8},{8,0},{32,40},{40,32},{64,72},{72,64},{96,104},{104,96},{1,9... | collective-permute-start | bytes 3932168 | tf_op jit(solution)/shard_map/ppermute | solution.py:34
  7.9 18.7 %collective-permute-start.4 = (f32[640,256]{1,0:T(8,128)S(1)}, f32[640,256]{1,0:T(8,128)S(1)}, u32[]{:S(2)}, u32[]{:S(2)}) collective-permute-start(f32[640,256]{1,0:T(8,128)S(1)} %get-tuple-element.45), channel_id=1, source_target_pairs={{0,32},{8,40},{32,64},{40,72},{64,96},{72,104},{96,0},{104,8},{1,3... | collective-permute-start | bytes 1966088 | tf_op jit(solution)/shard_map/ppermute | solution.py:34
  9.6 16.9 %collective-permute-start.5 = (f32[640,256]{1,0:T(8,128)S(1)}, f32[640,256]{1,0:T(8,128)S(1)}, u32[]{:S(2)}, u32[]{:S(2)}) collective-permute-start(f32[640,256]{1,0:T(8,128)S(1)} %get-tuple-element.46), channel_id=1, source_target_pairs={{0,96},{8,104},{32,0},{40,8},{64,32},{72,40},{96,64},{104,72},{1,9... | collective-permute-start | bytes 1966088 | tf_op jit(solution)/shard_map/ppermute | solution.py:34
  11.9 14.3 %collective-permute-start.7 = (f32[256,512]{1,0:T(8,128)S(1)}, f32[256,512]{1,0:T(8,128)S(1)}, u32[]{:S(2)}, u32[]{:S(2)}) collective-permute-start(f32[256,512]{1,0:T(8,128)S(1)} %get-tuple-element.48), channel_id=1, source_target_pairs={{0,16},{8,24},{32,48},{40,56},{64,80},{72,88},{96,112},{104,120},{... | collective-permute-start | bytes 1572872 | tf_op jit(solution)/shard_map/ppermute | solution.py:34
  28.6 37.3 %collective-permute-start.10 = (f32[768,512]{1,0:T(8,128)S(1)}, f32[768,512]{1,0:T(8,128)S(1)}, u32[]{:S(2)}, u32[]{:S(2)}) collective-permute-start(f32[768,512]{1,0:T(8,128)S(1)} %get-tuple-element.53), channel_id=1, source_target_pairs={{0,16},{8,24},{32,48},{40,56},{64,80},{72,88},{96,112},{104,120},{... | collective-permute-start | bytes 4718600 | tf_op jit(solution)/shard_map/ppermute | solution.py:34
  31.6 34.3 %collective-permute-start.8 = (f32[736,512]{1,0:T(8,128)S(1)}, f32[736,512]{1,0:T(8,128)S(1)}, u32[]{:S(2)}, u32[]{:S(2)}) collective-permute-start(f32[736,512]{1,0:T(8,128)S(1)} %get-tuple-element.51), channel_id=1, source_target_pairs={{0,32},{8,40},{32,64},{40,72},{64,96},{72,104},{96,0},{104,8},{1,3... | collective-permute-start | bytes 4521992 | tf_op jit(solution)/shard_map/ppermute | solution.py:34
  31.9 34.0 %collective-permute-start.9 = (f32[736,512]{1,0:T(8,128)S(1)}, f32[736,512]{1,0:T(8,128)S(1)}, u32[]{:S(2)}, u32[]{:S(2)}) collective-permute-start(f32[736,512]{1,0:T(8,128)S(1)} %get-tuple-element.52), channel_id=1, source_target_pairs={{0,96},{8,104},{32,0},{40,8},{64,32},{72,40},{96,64},{104,72},{1,9... | collective-permute-start | bytes 4521992 | tf_op jit(solution)/shard_map/ppermute | solution.py:34
  34.2 6.3 %collective-permute-start = (f32[640,512]{1,0:T(8,128)S(1)}, f32[640,512]{1,0:T(8,128)S(1)}, u32[]{:S(2)}, u32[]{:S(2)}) collective-permute-start(f32[640,512]{1,0:T(8,128)S(1)} %get-tuple-element.40), channel_id=1, source_target_pairs={{0,8},{8,0},{32,40},{40,32},{64,72},{72,64},{96,104},{104,96},{1,9... | collective-permute-start | bytes 3932168 | tf_op jit(solution)/shard_map/ppermute | solution.py:34
  36.2 4.3 %collective-permute-start.11 = (f32[576,512]{1,0:T(8,128)S(1)}, f32[576,512]{1,0:T(8,128)S(1)}, u32[]{:S(2)}, u32[]{:S(2)}) collective-permute-start(f32[576,512]{1,0:T(8,128)S(1)} %get-tuple-element.54), channel_id=1, source_target_pairs={{0,8},{8,0},{32,40},{40,32},{64,72},{72,64},{96,104},{104,96},{1,9... | collective-permute-start | bytes 3538952 | tf_op jit(solution)/shard_map/ppermute | solution.py:34
  67.7 15.5 %collective-permute-start.12 = (f32[320,512]{1,0:T(8,128)S(1)}, f32[320,512]{1,0:T(8,128)S(1)}, u32[]{:S(2)}, u32[]{:S(2)}) collective-permute-start(f32[320,512]{1,0:T(8,128)S(1)} %get-tuple-element.57), channel_id=1, source_target_pairs={{0,16},{8,24},{32,48},{40,56},{64,80},{72,88},{96,112},{104,120},{... | collective-permute-start | bytes 1966088 | tf_op jit(solution)/shard_map/ppermute | solution.py:34
  69.8 16.0 %collective-permute-start.15 = (f32[256,512]{1,0:T(8,128)S(1)}, f32[256,512]{1,0:T(8,128)S(1)}, u32[]{:S(2)}, u32[]{:S(2)}) collective-permute-start(f32[256,512]{1,0:T(8,128)S(1)} %get-tuple-element.69.refs_1_), channel_id=1, source_target_pairs={{0,2},{8,10},{32,34},{40,42},{64,66},{72,74},{96,98},{104,106},{1,... | collective-permute-start | bytes 1572872 | tf_op jit(solution)/shard_map/ppermute | solution.py:34
  71.0 13.7 %collective-permute-start.13 = (f32[192,512]{1,0:T(8,128)S(1)}, f32[192,512]{1,0:T(8,128)S(1)}, u32[]{:S(2)}, u32[]{:S(2)}) collective-permute-start(f32[192,512]{1,0:T(8,128)S(1)} %get-tuple-element.61), channel_id=1, source_target_pairs={{0,32},{8,40},{32,64},{40,72},{64,96},{72,104},{96,0},{104,8},{1,3... | collective-permute-start | bytes 1179656 | tf_op jit(solution)/shard_map/ppermute | solution.py:34
  71.0 13.7 %collective-permute-start.14 = (f32[192,512]{1,0:T(8,128)S(1)}, f32[192,512]{1,0:T(8,128)S(1)}, u32[]{:S(2)}, u32[]{:S(2)}) collective-permute-start(f32[192,512]{1,0:T(8,128)S(1)} %get-tuple-element.62), channel_id=1, source_target_pairs={{0,96},{8,104},{32,0},{40,8},{64,32},{72,40},{96,64},{104,72},{1,9... | collective-permute-start | bytes 1179656 | tf_op jit(solution)/shard_map/ppermute | solution.py:34
  86.5 24.2 %collective-permute-start.16 = (f32[1024,512]{1,0:T(8,128)S(1)}, f32[1024,512]{1,0:T(8,128)S(1)}, u32[]{:S(2)}, u32[]{:S(2)}) collective-permute-start(f32[1024,512]{1,0:T(8,128)S(1)} %get-tuple-element.70), channel_id=1, source_target_pairs={{0,8},{8,0},{32,40},{40,32},{64,72},{72,64},{96,104},{104,96},{1,9... | collective-permute-start | bytes 6291464 | tf_op jit(solution)/shard_map/ppermute | solution.py:34
  89.8 5.4 %collective-permute-start.17 = (f32[8,8,256]{2,1,0:T(8,128)S(1)}, f32[8,8,256]{2,1,0:T(8,128)S(1)}, u32[]{:S(2)}, u32[]{:S(2)}) collective-permute-start(f32[8,8,256]{2,1,0:T(8,128)S(1)} %get-tuple-element.66.refs_2_.refs_0_), channel_id=1, source_target_pairs={{0,2},{8,10},{32,34},{40,42},{64,66},{72,74},{96,98},{104,106},{1,... | collective-permute-start | bytes 196616 | tf_op jit(solution)/shard_map/ppermute | solution.py:34
  91.0 6.1 %collective-permute-start.18 = (f32[8,8,256]{2,1,0:T(8,128)S(1)}, f32[8,8,256]{2,1,0:T(8,128)S(1)}, u32[]{:S(2)}, u32[]{:S(2)}) collective-permute-start(f32[8,8,256]{2,1,0:T(8,128)S(1)} %get-tuple-element.66.refs_2_.refs_0_), channel_id=1, source_target_pairs={{0,4},{8,12},{32,36},{40,44},{64,68},{72,76},{96,100},{104,108},{1... | collective-permute-start | bytes 196616 | tf_op jit(solution)/shard_map/ppermute | solution.py:34
  93.4 4.5 %collective-permute-start.19 = (f32[8,8,256]{2,1,0:T(8,128)S(1)}, f32[8,8,256]{2,1,0:T(8,128)S(1)}, u32[]{:S(2)}, u32[]{:S(2)}) collective-permute-start(f32[8,8,256]{2,1,0:T(8,128)S(1)} %get-tuple-element.66.refs_2_.refs_0_), channel_id=1, source_target_pairs={{0,6},{8,14},{32,38},{40,46},{64,70},{72,78},{96,102},{104,110},{1... | collective-permute-start | bytes 196616 | tf_op jit(solution)/shard_map/ppermute | solution.py:34
  98.5 3.9 %collective-permute-start.20 = (f32[8,8,256]{2,1,0:T(8,128)S(1)}, f32[8,8,256]{2,1,0:T(8,128)S(1)}, u32[]{:S(2)}, u32[]{:S(2)}) collective-permute-start(f32[8,8,256]{2,1,0:T(8,128)S(1)} %get-tuple-element.72.refs_0_), channel_id=1, source_target_pairs={{0,1},{8,9},{32,33},{40,41},{64,65},{72,73},{96,97},{104,105},{1,0... | collective-permute-start | bytes 196616 | tf_op jit(solution)/shard_map/ppermute | solution.py:34
  98.9 4.9 %collective-permute-start.21 = (f32[8,8,256]{2,1,0:T(8,128)S(1)}, f32[8,8,256]{2,1,0:T(8,128)S(1)}, u32[]{:S(2)}, u32[]{:S(2)}) collective-permute-start(f32[8,8,256]{2,1,0:T(8,128)S(1)} %get-tuple-element.72.refs_0_), channel_id=1, source_target_pairs={{0,16},{8,24},{32,48},{40,56},{64,80},{72,88},{96,112},{104,120},{... | collective-permute-start | bytes 196616 | tf_op jit(solution)/shard_map/ppermute | solution.py:34
  101.5 5.0 %collective-permute-start.22 = (f32[8,8,256]{2,1,0:T(8,128)S(1)}, f32[8,8,256]{2,1,0:T(8,128)S(1)}, u32[]{:S(2)}, u32[]{:S(2)}) collective-permute-start(f32[8,8,256]{2,1,0:T(8,128)S(1)} %get-tuple-element.72.refs_0_), channel_id=1, source_target_pairs={{0,17},{8,25},{32,49},{40,57},{64,81},{72,89},{96,113},{104,121},{... | collective-permute-start | bytes 196616 | tf_op jit(solution)/shard_map/ppermute | solution.py:34
  107.1 3.6 %collective-permute-start.23 = (f32[2,8,8,256]{3,2,1,0:T(8,128)S(1)}, f32[2,8,8,256]{3,2,1,0:T(8,128)S(1)}, u32[]{:S(2)}, u32[]{:S(2)}) collective-permute-start(f32[2,8,8,256]{3,2,1,0:T(8,128)S(1)} %get-tuple-element.73.pair_ref), channel_id=1, source_target_pairs={{0,8},{8,0},{32,40},{40,32},{64,72},{72,64},{96,104},{104,96},{1,9... | collective-permute-start | bytes 393224 | tf_op jit(solution)/shard_map/ppermute | solution.py:34
  (3 other events, 28.8 us)

commit v4 on v3

--- a/solution.py
+++ b/solution.py
@@ -11,7 +11,7 @@
 NB = COLS // GROUP
 OWN = 512
 ZROWS = 320
-FIRST = 64
+FIRST = 32
 LANES = COLS // 128
 AXES = ("fsdp", "dp", "outer")
 beta = 0.9
@@ -59,7 +59,7 @@
     out[...] = jnp.zeros((8, 128), F32)
 
 
-def piece_call(name, parts, steps, terms, after, outs, cost=1):
+def piece_call(name, parts, steps, terms, after, outs, cost=1, result=False):
     outs = outs + [((8, 128), mark)]
     outs = [out if len(out) == 3 else out + (F32,) for out in outs]
     n_terms, n_after, n_outs, n_steps = len(terms), len(after), len(outs), len(steps)
@@ -101,12 +101,12 @@
         in_specs=[pl.BlockSpec(memory_space=pltpu.HBM)] + [anywhere if i in picked else here for i in range(n_terms)]
         + [anywhere] * n_after,
         out_specs=[here] * n_outs,
-        out_shape=[pltpu.VMEM(s, t) for s, _, t in outs],
+        out_shape=[(jax.ShapeDtypeStruct if result and i == 0 else pltpu.VMEM)(s, t) for i, (s, _, t) in enumerate(outs)],
         scratch_shapes=[pltpu.VMEM((s[4], COLS), BF16) for s in steps]
         + [pltpu.VMEM(terms[i][1], F32) for i in picked]
         + [pltpu.SemaphoreType.DMA] * (n_steps + len(picked)),
         compiler_params=pltpu.CompilerParams(vmem_limit_bytes=24 * 2**20),
-        cost_estimate=pl.CostEstimate(flops=1, bytes_accessed=cost, transcendentals=0),
+        cost_estimate=pl.CostEstimate(flops=cost*100, bytes_accessed=cost, transcendentals=0),
         name=name,
     )(parts, *[t[0] if i in picked else hold(t) for i, t in enumerate(terms)], *after)
 
@@ -138,18 +138,23 @@
     def y_rows(f, r, c):
         return (f, r, c, zr, yr)
 
-    def widen(name, groups, after):
+    def widen(name, groups, after, more=None):
+        extra = 0 if more is None else more.shape[0]
         outs, first = [], 0
         for group in groups:
-            def body(z, piece, term, out, group=group, first=first):
+            tail = extra if group is groups[-1] else 0
+
+            def body(z, piece, term, out, group=group, first=first, tail=tail):
                 top = 0
                 for i, step in enumerate(group):
                     out[top:top + step[4], :] = piece(first + i)[...].astype(F32)
                     top += step[4]
-
-            outs.append(((sum(s[4] for s in group), COLS), body))
+                if tail:
+                    out[top:, :] = term(0)[...]
+
+            outs.append(((sum(s[4] for s in group) + tail, COLS), body))
             first += len(group)
-        return call(name, [s for group in groups for s in group], [], after, outs)
+        return call(name, [s for group in groups for s in group], [] if more is None else [more], after, outs)
 
     def add(i_pieces, i_term, first, cols=slice(None), half_terms=(), full_terms=()):
         def run(z, piece, term, out):
@@ -173,24 +178,17 @@
                 body(z, piece, term, out.at[:, cols])
         return run
 
-    def pack(z, piece, term, out):
-        odd = (lax.axis_index("outer") // 2) % 2
-        n = OWN // 2
-        out[:OWN, :] = term(0)[...]
-        out[pl.ds(pl.multiple_of(OWN + odd * n, n), n), :] = term(1)[...]
-        out[pl.ds(pl.multiple_of(OWN + (1 - odd) * n, n), n), :] = term(2)[...]
-
     w_first, ta = widen("widen_a", [[z_rows(OPP, 0, 1), z_rows(OPP, 1, 1), y_rows(OPP, 1, 1)]], [])
     c_first = swap(w_first, core=1)
     *w_b, tb = widen("widen_b", [
         [z_rows(UP, 0, 1), z_rows(UP, 1, 1)], [z_rows(DOWN, 0, 1), z_rows(DOWN, 1, 1)],
         [y_rows(UP, 1, 1), y_rows(DOWN, 1, 1), y_rows(MINE, 1, 1), y_rows(OPP, 0, 1)],
         [z_rows(MINE, 0, 1), z_rows(MINE, 1, 1)],
-        [y_rows(UP, 0, 1), y_rows(DOWN, 0, 1), y_rows(MINE, 0, 1)]], [ta])
+        [y_rows(UP, 0, 1), y_rows(DOWN, 0, 1), y_rows(MINE, 0, 1)]], [ta], params)
     c_up, c_down, c_cross, c_own, c_rest = [swap(w, core=1) for w in w_b]
     def params_part(top, n):
         def pick(x, ref):
-            return ref.at[pl.ds(pl.multiple_of((x % 2) * (OWN // 2) + top, 64), n), :]
+            return ref.at[pl.ds(pl.multiple_of((x % 2) * (OWN // 2) + top, FIRST), n), :]
         return (params, (n, COLS), pick)
 
     def with_params(body, i_params):
@@ -244,54 +242,78 @@
         return run
 
     def last_own_body(z, piece, term, out):
-        out[...] = term(3)[2 * yr:3 * yr] + term(4)[2 * yr:] + piece(4)[...].astype(F32)
+        out[...] = term(3)[2 * yr:3 * yr] + term(4)[2 * yr:3 * yr] + piece(4)[...].astype(F32)
 
     def far_body(z, piece, term, out):
         out[:FIRST, :] = term(5)[yr:, :]
         out[FIRST:, :] = term(3)[3 * yr:, :]
 
-    y3, u4, d4, near, last_own, far_half, t6 = call(
+    far_rows, u4, d4, near, last_own, far_half, t6 = call(
         "own", [z_rows(MINE, 0, 0), z_rows(MINE, 1, 0), y_rows(UP, 0, 0), y_rows(DOWN, 0, 0), y_rows(MINE, 0, 0)],
         [c_own, gu2, gd2, gy2, c_rest, gy1], [t2],
         [((zr, COLS), own_body(1)), ((yr, COLS), last_side(0, 0, 1)), ((yr, COLS), last_side(1, 1, 2)),
          ((zr, COLS), own_body(0)), ((yr, COLS), last_own_body),
          ((OWN // 2, COLS), far_body)])
     far_other = swap(far_half, x=1)
-    gy3, gu4, gd4 = swap(y3, y=2), up(u4), down(d4)
+    from_core = [swap(far_half, core=1)]
+    gu4, gd4 = up(u4), down(d4)
     def momentum_rows(top, n):
         return (momentum, (n, COLS), lambda x, ref: ref.at[pl.ds(top, n), :])
 
-    def near_mom(z, piece, term, out):
-        out[...] = beta * term(2)[...] + (term(0)[...] + term(1)[...]) * (1.0 / 16.0)
-        near_mom.value = out
-
-    def near_shared(z, piece, term, out):
-        for b, value in enumerate(encode(near_mom.value[...], term(3)[...], term(4)[...])):
-            out[b] = value
-
     nz, ny = zr // GROUP, yr // GROUP
-    mom_top, shared_top, t7 = call(
-        "near_momentum", [], [near, gy3, momentum_rows(0, zr), vert, horiz], [t6],
-        [((zr, COLS), near_mom), ((NB, nz, BAND), near_shared)], cost=9 * 10**6,
-    )
+
+    def near_partial(z, piece, term, out):
+        value = beta * term(2)[...] + term(0)[...] * (1.0 / 16.0)
+        for b, (mine, theirs) in enumerate(zip(encode(value, term(3)[...], term(4)[...]),
+                                               encode(term(1)[...] * (1.0 / 16.0), term(3)[...], term(4)[...]))):
+            out[b, :nz, :] = mine
+            out[b, nz:, :] = theirs
+
+    def hand_on(z, piece, term, out):
+        out[...] = term(1)[...]
+
+    partial, y3, _ = call("partial_encode", [], [near, far_rows, momentum_rows(0, zr), vert, horiz], [t6],
+                        [((NB, 2 * nz, BAND), near_partial), ((zr, COLS), hand_on)])
+    gy3 = swap(y3, y=2)
 
     def last_mom(z, piece, term, out):
         grad = term(0)[...] + (term(1)[...] + term(2)[...])
         out[...] = beta * term(3)[...] + grad * (1.0 / 16.0)
         last_mom.value = out
 
-    def last_shared(z, piece, term, out):
+    def last_coeffs(z, piece, term, out):
         for b, value in enumerate(encode(last_mom.value[...], term(4)[...], term(5)[...])):
-            out[b, :nz, :] = term(6)[b]
-            out[b, nz:, :] = value
-
-    mom_low, shared, t8 = call(
-        "last_momentum", [], [last_own, gu4, gd4, momentum_rows(zr, yr), vert, horiz, shared_top], [t7],
-        [((yr, COLS), last_mom), ((NB, nz + ny, BAND), last_shared)],
+            out[b, :nz, :] = term(6)[b, :nz]
+            out[b, nz:nz + ny, :] = value
+            out[b, nz + ny:, :] = term(6)[b, nz:]
+
+    mom_low, coeffs, t7 = call(
+        "last_momentum", [], [last_own, gu4, gd4, momentum_rows(zr, yr), vert, horiz, partial], [t6, far_other, from_core[0]],
+        [((yr, COLS), last_mom), ((NB, 2 * nz + ny, BAND), last_coeffs)], cost=4 * 10**6,
     )
 
-    packed, _ = call("params_pack", [], [params, far_half, far_other], [t8], [((2 * OWN, COLS), pack)])
-    packed_core = swap(packed, core=1)
+    def sum_four(z, piece, term, out):
+        out[...] = (term(0)[...] + term(2)[...]) + (term(1)[...] + term(3)[...])
+
+    total, tx = call("sum_x", [], [coeffs] + [swap(coeffs, x=k) for k in (2, 1, 3)], [], [(coeffs.shape, sum_four)],
+                    cost=20000000)
+    def near_mom(z, piece, term, out):
+        out[...] = beta * term(2)[...] + (term(0)[...] + term(1)[...]) * (1.0 / 16.0)
+        near_mom.value = out
+
+    def near_shared(z, piece, term, out):
+        for b, value in enumerate(encode(near_mom.value[...], term(3)[...], term(4)[...])):
+            out[b, :nz, :] = value
+            out[b, nz:, :] = term(5)[b, nz:nz + ny]
+
+    def far_copy(z, piece, term, out):
+        out[...] = term(6)[...]
+
+    mom_top, shared, far_late, t8 = call(
+        "near_momentum", [], [near, gy3, momentum_rows(0, zr), vert, horiz, coeffs, far_other], [tx],
+        [((zr, COLS), near_mom), ((NB, nz + ny, BAND), near_shared), ((OWN // 2, COLS), far_copy)], cost=5 * 10**6,
+    )
+    from_core.append(swap(far_late, core=1))
 
     def residual(z, piece, term, out):
         high, low = split(term(4)[...])
@@ -310,18 +332,18 @@
             out[zr:, cols] = term(1)[:, cols] - value[zr:]
 
     new_momentum, t9 = call("momentum_residual", [], [mom_top, mom_low, shared, vert, horiz_t], [t8],
-                            [((OWN, COLS), residual)], cost=9 * 10**6)
-
-    def sum_four(z, piece, term, out):
-        out[...] = (term(0)[...] + term(1)[...]) + (term(2)[...] + term(3)[...])
+                            [((OWN, COLS), residual)], cost=9 * 10**6, result=True)
 
     def sum_pairs(z, piece, term, out):
-        out[0] = term(0)[...] + term(1)[...]
-        out[1] = term(2)[...] + term(3)[...]
-
-    total, t10 = call("sum_x", [], [shared] + [swap(shared, x=k) for k in (1, 2, 3)], [t9], [(shared.shape, sum_four)])
-    pair, _ = call("sum_y", [], [total] + [swap(total, y=k) for k in (1, 2, 3)], [], [((2,) + shared.shape, sum_pairs)])
-    new_params = update_call(packed, packed_core, pair, swap(pair, core=1), table_high, table_low)
+        top, low, far = slice(0, nz), slice(nz, nz + ny), slice(nz + ny, None)
+        for k, (a, b, c, d) in enumerate(((0, 2, 1, 3), (1, 3, 0, 2))):
+            own = [term(a)[:, cut] + term(b)[:, cut] for cut in (top, low)]
+            out[k, :, :nz, :] = own[0] + (term(c)[:, far] + term(d)[:, far])
+            out[k, :, nz:, :] = own[1]
+
+    pair, _ = call("sum_y", [], [total] + [swap(total, y=k) for k in (2, 1, 3)], [t9], [((2,) + shared.shape, sum_pairs)],
+                   cost=7 * 10**7)
+    new_params = update_call([params, far_half, far_other, c_rest] + from_core, pair, swap(pair, core=1), table_high, table_low)
     return new_momentum, new_params
 
 
@@ -346,11 +368,20 @@
     return [((BAND, GROUP * GROUP), high, BF16), ((BAND, GROUP * GROUP), low, BF16)]
 
 
-def update_kernel(rows_ref, rows_core_ref, pair_ref, pair_core_ref, high_ref, low_ref, out_ref, coeff, field, sems):
+def update_kernel(own_ref, far_ref, other_ref, core_own_ref, core_far_ref, core_other_ref,
+                  pair_ref, pair_core_ref, high_ref, low_ref, out_ref, coeff, field, sems):
     dp = lax.axis_index("dp")
+    odd = (lax.axis_index("outer") // 2) % 2
     nblock = OWN // GROUP
+    part = nblock // 2
+    core_own = core_own_ref.at[core_own_ref.shape[0] - nblock:]
+    rows = ((own_ref,), (core_own,), (far_ref, other_ref), (core_far_ref, core_other_ref))
     for k in range(4):
-        coeff[:, k] = (pair_ref, pair_core_ref)[k % 2][k // 2]
+        value = (pair_ref, pair_core_ref)[k % 2][k // 2]
+        if k >= 2:
+            turned = jnp.concatenate([value[:, part:], value[:, :part]], axis=1)
+            value = jnp.where(odd == 1, turned, value)
+        coeff[:, k] = value
     c_high, c_low = split(coeff[...].reshape(NB * 4 * nblock, BAND) * (1.0 / 8.0))
     both = jnp.concatenate([c_high, c_low], axis=0)
     lane = lax.broadcasted_iota(jnp.int32, (4 * nblock, 2 * GROUP), 1)
@@ -373,20 +404,24 @@
             turned = jnp.swapaxes(jnp.stack(rows_m), 0, 1)
             out_cols = slice(b * GROUP, (b + 2) * GROUP)
             for k in range(4):
-                held = (rows_ref, rows_core_ref)[k % 2][k // 2, :, at, out_cols]
-                field[k, :, at, out_cols] = held - turned[k * nblock:(k + 1) * nblock]
+                n = nblock // len(rows[k])
+                for i, ref in enumerate(rows[k]):
+                    cut = slice(i * n, (i + 1) * n)
+                    field[k, cut, at, out_cols] = ref[:, at, out_cols] - turned[k * nblock + i * n:k * nblock + (i + 1) * n]
         for k in range(4):
-            store = pltpu.make_async_copy(field.at[k, :, pl.ds(c * step, step), :],
-                                          out_ref.at[dp ^ k, :, pl.ds(c * step, step), :], sems.at[c * 4 + k])
-            store.start()
-            stores.append(store)
+            for i in range(2):
+                to = (part * i if k < 2 else part * ((odd + i) % 2))
+                store = pltpu.make_async_copy(field.at[k, pl.ds(i * part, part), pl.ds(c * step, step), :],
+                                              out_ref.at[dp ^ k, pl.ds(to, part), pl.ds(c * step, step), :],
+                                              sems.at[(c * 4 + k) * 2 + i])
+                store.start()
+                stores.append(store)
     for store in stores:
         store.wait()
 
 
-def update_call(rows, rows_core, *arrays):
-    shape = (2, OWN // GROUP, GROUP, COLS)
-    arrays = (rows.reshape(shape), rows_core.reshape(shape)) + arrays
+def update_call(rows, *arrays):
+    arrays = [r.reshape(-1, GROUP, COLS) for r in rows] + list(arrays)
     return pl.pallas_call(
         update_kernel,
         in_specs=[pl.BlockSpec(memory_space=pltpu.VMEM)] * len(arrays),
@@ -395,7 +430,7 @@
         scratch_shapes=[
             pltpu.VMEM((NB, 4, OWN // GROUP, BAND), F32),
             pltpu.VMEM((4, OWN // GROUP, GROUP, COLS), F32),
-            pltpu.SemaphoreType.DMA((4 * GROUP // 8,)),
+            pltpu.SemaphoreType.DMA((8 * GROUP // 8,)),
         ],
         compiler_params=pltpu.CompilerParams(vmem_limit_bytes=24 * 2**20),
         name="parameter_update",

time: 115 us -> 112 us (0.974)
  waiting for transfers between devices: 54.4 us -> 48.5 us
  Pallas kernels: 20.3 us -> 24 us
    ppermute x24 -> x25, waiting for transfers between devices: 54.4 us -> 48.5 us  [swap(): return lax.ppermute(value, AXES, pairs)]
    pallas_call x12, Pallas kernels: 16.8 us -> 20.2 us  [piece_call(): pl.pallas_call(kernel, in_specs=[pl.BlockSpec(memory_space=pltpu.HBM)] +...]
    ppermute x24 -> x25, starting transfers between devices: 36.2 us -> 37 us  [swap(): return lax.ppermute(value, AXES, pairs)]
  transfers between devices with their start and end apart: 24 -> 25, of which waited for: 10 -> 11; matrix products, arithmetic and copies ran while one was open for 2% -> 1% of each run, Pallas kernels for 10% -> 15%
where the time goes in v4:
time: 112 us
  waiting for transfers between devices  48.5 us (43%)
  starting transfers between devices  37 us (33%)
  Pallas kernels  24 us (21%)
  other arithmetic  1.48 us (1%)
    ppermute x25, waiting for transfers between devices, swap(): return lax.ppermute(value, AXES, pairs)  48.5 us
    ppermute x25, starting transfers between devices, swap(): return lax.ppermute(value, AXES, pairs)  37 us
    pallas_call x12, Pallas kernels, piece_call(): pl.pallas_call(kernel, in_specs=[pl.BlockSpec(memory_space=pltpu.HBM)] +...  20.2 us
    pallas_call x1, Pallas kernels, update_call(): pl.pallas_call(update_kernel, in_specs=[pl.BlockSpec(memory_space=pltpu.V...  3.8 us
  transfers between devices with their start and end apart: 25, of which 11 were waited for; matrix products, arithmetic and copies ran while one was open for 1% of the time, Pallas kernels for 15%

profile of v4, /device:TPU:1, one launch (start us, length us, event | category | flops | bytes accessed | tf_op | source)
XLA Modules:
  0.0 111.9 jit_solution(10048146034741569809)
XLA Ops:
  3.4 2.1 %widen_b.1 = (f32[640,512]{1,0:T(8,128)S(1)}, f32[640,512]{1,0:T(8,128)S(1)}, f32[768,512]{1,0:T(8,128)S(1)}, f32[640,512]{1,0:T(8,128)S(1)}, f32[1088,512]{1,0:T(8,128)S(1)}, /*index=5*/f32[8,128]{1,0:T(8,128)S(1)}) custom-call(bf16[4,2,2,512,512]{4,3,2,1,0:T(8,128)(2,1)} %bitcast.20, f32[512,512]{1,0:T(8,128)S(1)} %copy-done, ...), custom_call_target="tpu_custom_call" | custom-call | flops 100 | bytes 1 | tf_op jit(solution)/shard_map/widen_b/pallas_call | solution.py:99
  7.9 1.8 %collective-permute-start.4 = (f32[640,256]{1,0:T(8,128)S(1)}, f32[640,256]{1,0:T(8,128)S(1)}, u32[]{:S(2)}, u32[]{:S(2)}) collective-permute-start(f32[640,256]{1,0:T(8,128)S(1)} %get-tuple-element.47), channel_id=1, source_target_pairs={{0,32},{8,40},{32,64},{40,72},{64,96},{72,104},{96,0},{104,8},{1,3... | collective-permute-start | bytes 1966088 | tf_op jit(solution)/shard_map/ppermute | solution.py:34
  9.7 2.2 %collective-permute-start.5 = (f32[640,256]{1,0:T(8,128)S(1)}, f32[640,256]{1,0:T(8,128)S(1)}, u32[]{:S(2)}, u32[]{:S(2)}) collective-permute-start(f32[640,256]{1,0:T(8,128)S(1)} %get-tuple-element.48), channel_id=1, source_target_pairs={{0,96},{8,104},{32,0},{40,8},{64,32},{72,40},{96,64},{104,72},{1,9... | collective-permute-start | bytes 1966088 | tf_op jit(solution)/shard_map/ppermute | solution.py:34
  12.6 2.9 %collective-permute-start.7 = (f32[224,512]{1,0:T(8,128)S(1)}, f32[224,512]{1,0:T(8,128)S(1)}, u32[]{:S(2)}, u32[]{:S(2)}) collective-permute-start(f32[224,512]{1,0:T(8,128)S(1)} %get-tuple-element.50), channel_id=1, source_target_pairs={{0,16},{8,24},{32,48},{40,56},{64,80},{72,88},{96,112},{104,120},{... | collective-permute-start | bytes 1376264 | tf_op jit(solution)/shard_map/ppermute | solution.py:34
  16.5 2.4 %band_table.1 = (bf16[256,4096]{1,0:T(8,128)(2,1)S(1)}, bf16[256,4096]{1,0:T(8,128)(2,1)S(1)}, f32[8,128]{1,0:T(8,128)S(1)}) custom-call(bf16[4,2,2,512,512]{4,3,2,1,0:T(8,128)(2,1)} %bitcast.22, f32[256,64]{1,0:T(8,128)S(1)} %get-tuple-element.89.refs_0_, f32[256,64]{1,0:T(8,128)S(1)} %get-tuple-element.88.refs_1_.refs_4_, ...), custom_call_target="tpu_custom_call" | custom-call | flops 100 | bytes 1 | tf_op jit(solution)/shard_map/band_table/pallas_call | solution.py:99
  19.0 7.2 %collective-permute-done.7.refs_5_ = f32[224,512]{1,0:T(8,128)S(1)} collective-permute-done((f32[224,512]{1,0:T(8,128)S(1)}, f32[224,512]{1,0:T(8,128)S(1)}, u32[]{:S(2)}, u32[]{:S(2)}) %collective-permute-start.7) | collective-permute-done | bytes 458784 | tf_op jit(solution)/shard_map/ppermute | solution.py:34
  26.7 2.0 %sides.1 = (f32[736,512]{1,0:T(8,128)S(1)}, f32[736,512]{1,0:T(8,128)S(1)}, f32[800,512]{1,0:T(8,128)S(1)}, f32[8,128]{1,0:T(8,128)S(1)}) custom-call(bf16[4,2,2,512,512]{4,3,2,1,0:T(8,128)(2,1)} %bitcast.23, f32[640,512]{1,0:T(8,128)S(1)} %collective-permute-done.1.refs_0_, f32[640,512]{1,0:T(8,128)S(1)} %collective-permute-done.2.refs_1_, ...), custom_call_target="tpu_custom_call" | custom-call | flops 100 | bytes 1 | tf_op jit(solution)/shard_map/sides/pallas_call | solution.py:99
  28.7 3.0 %collective-permute-start.10 = (f32[800,512]{1,0:T(8,128)S(1)}, f32[800,512]{1,0:T(8,128)S(1)}, u32[]{:S(2)}, u32[]{:S(2)}) collective-permute-start(f32[800,512]{1,0:T(8,128)S(1)} %get-tuple-element.55), channel_id=1, source_target_pairs={{0,16},{8,24},{32,48},{40,56},{64,80},{72,88},{96,112},{104,120},{... | collective-permute-start | bytes 4915208 | tf_op jit(solution)/shard_map/ppermute | solution.py:34
  32.0 2.3 %collective-permute-start.9 = (f32[736,512]{1,0:T(8,128)S(1)}, f32[736,512]{1,0:T(8,128)S(1)}, u32[]{:S(2)}, u32[]{:S(2)}) collective-permute-start(f32[736,512]{1,0:T(8,128)S(1)} %get-tuple-element.54), channel_id=1, source_target_pairs={{0,96},{8,104},{32,0},{40,8},{64,32},{72,40},{96,64},{104,72},{1,9... | collective-permute-start | bytes 4521992 | tf_op jit(solution)/shard_map/ppermute | solution.py:34
  36.1 2.7 %collective-permute-done.refs_0_ = f32[640,512]{1,0:T(8,128)S(1)} collective-permute-done((f32[640,512]{1,0:T(8,128)S(1)}, f32[640,512]{1,0:T(8,128)S(1)}, u32[]{:S(2)}, u32[]{:S(2)}) %collective-permute-start) | collective-permute-done | bytes 1310752 | tf_op jit(solution)/shard_map/ppermute | solution.py:34
  38.7 27.5 %collective-permute-done.8.refs_1_ = f32[736,512]{1,0:T(8,128)S(1)} collective-permute-done((f32[736,512]{1,0:T(8,128)S(1)}, f32[736,512]{1,0:T(8,128)S(1)}, u32[]{:S(2)}, u32[]{:S(2)}) %collective-permute-start.8) | collective-permute-done | bytes 1507360 | tf_op jit(solution)/shard_map/ppermute | solution.py:34
  66.7 1.8 %own.1 = (f32[320,512]{1,0:T(8,128)S(1)}, f32[192,512]{1,0:T(8,128)S(1)}, f32[192,512]{1,0:T(8,128)S(1)}, f32[320,512]{1,0:T(8,128)S(1)}, f32[192,512]{1,0:T(8,1...) custom-call(bf16[4,2,2,512,512]{4,3,2,1,0:T(8,128)(2,1)} %bitcast.24, ...), custom_call_target="tpu_custom_call" | custom-call | flops 100 | bytes 1 | tf_op jit(solution)/shard_map/own/pallas_call | solution.py:99
  69.8 2.1 %collective-permute-start.16 = (f32[256,512]{1,0:T(8,128)S(1)}, f32[256,512]{1,0:T(8,128)S(1)}, u32[]{:S(2)}, u32[]{:S(2)}) collective-permute-start(f32[256,512]{1,0:T(8,128)S(1)} %get-tuple-element.66), channel_id=1, source_target_pairs={{0,8},{8,0},{32,40},{40,32},{64,72},{72,64},{96,104},{104,96},{1,9... | collective-permute-start | bytes 1572872 | tf_op jit(solution)/shard_map/ppermute | solution.py:34
  72.3 2.2 %collective-permute-start.14 = (f32[192,512]{1,0:T(8,128)S(1)}, f32[192,512]{1,0:T(8,128)S(1)}, u32[]{:S(2)}, u32[]{:S(2)}) collective-permute-start(f32[192,512]{1,0:T(8,128)S(1)} %get-tuple-element.64), channel_id=1, source_target_pairs={{0,96},{8,104},{32,0},{40,8},{64,32},{72,40},{96,64},{104,72},{1,9... | collective-permute-start | bytes 1179656 | tf_op jit(solution)/shard_map/ppermute | solution.py:34
  75.1 3.0 %partial_encode.1 = (f32[8,10,256]{2,1,0:T(8,128)S(1)}, f32[320,512]{1,0:T(8,128)S(1)}, f32[8,128]{1,0:T(8,128)}) custom-call(bf16[4,2,2,512,512]{4,3,2,1,0:T(8,128)(2,1)} %bitcast.25, f32[320,512]{1,0:T(8,128)S(1)} %get-tuple-element.58.refs_0_, f32[320,512]{1,0:T(8,128)S(1)} %get-tuple-element.59.refs_1_, f32[512,512]{1,0:T(8,128)S(1)} %bitcast.11, ...), custom_call_target="tpu_custom_call" | custom-call | flops 100 | bytes 1 | tf_op jit(solution)/shard_map/partial_encode/pallas_call | solution.py:99
  78.1 3.0 %collective-permute-start.12 = (f32[320,512]{1,0:T(8,128)S(1)}, f32[320,512]{1,0:T(8,128)S(1)}, u32[]{:S(2)}, u32[]{:S(2)}) collective-permute-start(f32[320,512]{1,0:T(8,128)S(1)} %get-tuple-element.61), channel_id=1, source_target_pairs={{0,16},{8,24},{32,48},{40,56},{64,80},{72,88},{96,112},{104,120},{... | collective-permute-start | bytes 1966088 | tf_op jit(solution)/shard_map/ppermute | solution.py:34
  81.1 2.7 %collective-permute-done.13.refs_1_ = f32[192,512]{1,0:T(8,128)S(1)} collective-permute-done((f32[192,512]{1,0:T(8,128)S(1)}, f32[192,512]{1,0:T(8,128)S(1)}, u32[]{:S(2)}, u32[]{:S(2)}) %collective-permute-start.13) | collective-permute-done | bytes 393248 | tf_op jit(solution)/shard_map/ppermute | solution.py:34
  85.5 2.5 %collective-permute-start.17 = (f32[8,13,256]{2,1,0:T(8,128)S(1)}, f32[8,13,256]{2,1,0:T(8,128)S(1)}, u32[]{:S(2)}, u32[]{:S(2)}) collective-permute-start(f32[8,13,256]{2,1,0:T(8,128)S(1)} %get-tuple-element.67.refs_0_.refs_5_), channel_id=1, source_target_pairs={{0,4},{8,12},{32,36},{40,44},{64,68},{72,76},{96,100},{104,108},{1... | collective-permute-start | bytes 319496 | tf_op jit(solution)/shard_map/ppermute | solution.py:34
  88.8 2.5 %collective-permute-done.17.refs_1_ = f32[8,13,256]{2,1,0:T(8,128)S(1)} collective-permute-done((f32[8,13,256]{2,1,0:T(8,128)S(1)}, f32[8,13,256]{2,1,0:T(8,128)S(1)}, u32[]{:S(2)}, u32[]{:S(2)}) %collective-permute-start.17) | collective-permute-done | bytes 106528 | tf_op jit(solution)/shard_map/ppermute | solution.py:34
  91.3 2.2 %collective-permute-done.18.refs_2_ = f32[8,13,256]{2,1,0:T(8,128)S(1)} collective-permute-done((f32[8,13,256]{2,1,0:T(8,128)S(1)}, f32[8,13,256]{2,1,0:T(8,128)S(1)}, u32[]{:S(2)}, u32[]{:S(2)}) %collective-permute-start.18) | collective-permute-done | bytes 106528 | tf_op jit(solution)/shard_map/ppermute | solution.py:34
  94.8 3.0 %collective-permute-start.21 = (f32[8,13,256]{2,1,0:T(8,128)S(1)}, f32[8,13,256]{2,1,0:T(8,128)S(1)}, u32[]{:S(2)}, u32[]{:S(2)}) collective-permute-start(f32[8,13,256]{2,1,0:T(8,128)S(1)} %get-tuple-element.75.refs_0_), channel_id=1, source_target_pairs={{0,16},{8,24},{32,48},{40,56},{64,80},{72,88},{96,112},{104,120},{... | collective-permute-start | bytes 319496 | tf_op jit(solution)/shard_map/ppermute | solution.py:34
  100.1 2.0 %collective-permute-start.20 = (f32[256,512]{1,0:T(8,128)S(1)}, f32[256,512]{1,0:T(8,128)S(1)}, u32[]{:S(2)}, u32[]{:S(2)}) collective-permute-start(f32[256,512]{1,0:T(8,128)S(1)} %get-tuple-element.74), channel_id=1, source_target_pairs={{0,8},{8,0},{32,40},{40,32},{64,72},{72,64},{96,104},{104,96},{1,9... | collective-permute-start | bytes 1572872 | tf_op jit(solution)/shard_map/ppermute | solution.py:34
  102.0 2.5 %momentum_residual.1 = (f32[512,512]{1,0:T(8,128)}, f32[8,128]{1,0:T(8,128)S(1)}) custom-call(bf16[4,2,2,512,512]{4,3,2,1,0:T(8,128)(2,1)} %bitcast.29, f32[320,512]{1,0:T(8,128)S(1)} %get-tuple-element.69.refs_0_, f32[192,512]{1,0:T(8,128)S(1)} %get-tuple-element.70.refs_1_, f32[8,8,256]{2,1,0:T(8,128)S(1)} %get-tuple-element.71.refs_2_, ...), custom_call_target="tpu_custom_call" | custom-call | flops 900000000 | bytes 9000000 | tf_op jit(solution)/shard_map/momentum_residual/pallas_call | solution.py:99
  107.9 3.8 %parameter_update.1 = f32[4,8,64,512]{3,2,1,0:T(8,128)} custom-call(f32[8,64,512]{2,1,0:T(8,128)S(1)} %bitcast.10, f32[4,64,512]{2,1,0:T(8,128)S(1)} %bitcast.17, f32[4,64,512]{2,1,0:T(8,128)S(1)} %bitcast.15, f32[17,64,512]{2,1,0:T(8,128)S(1)} %bitcast.14, f32[4,64,512]{2,1,0:T(8,128)S(1)} %bitcast.16, f32[4,64,512]{2,1,0:T(8,128)S(1)} %bitcast.18, ...), custom_call_target="tpu_custom_call" | custom-call | tf_op jit(solution)/shard_map/parameter_update/pallas_call | solution.py:425
  (49 shorter events, 21.4 us)
Async XLA Ops:
  1.9 4.7 %collective-permute-start.3 = (f32[832,512]{1,0:T(8,128)S(1)}, f32[832,512]{1,0:T(8,128)S(1)}, u32[]{:S(2)}, u32[]{:S(2)}) collective-permute-start(f32[832,512]{1,0:T(8,128)S(1)} %get-tuple-element.45), channel_id=1, source_target_pairs={{0,8},{8,0},{32,40},{40,32},{64,72},{72,64},{96,104},{104,96},{1,9... | collective-permute-start | bytes 5111816 | tf_op jit(solution)/shard_map/ppermute | solution.py:34
  5.5 6.4 %collective-permute-start.1 = (f32[640,512]{1,0:T(8,128)S(1)}, f32[640,512]{1,0:T(8,128)S(1)}, u32[]{:S(2)}, u32[]{:S(2)}) collective-permute-start(f32[640,512]{1,0:T(8,128)S(1)} %get-tuple-element.43), channel_id=1, source_target_pairs={{0,8},{8,0},{32,40},{40,32},{64,72},{72,64},{96,104},{104,96},{1,9... | collective-permute-start | bytes 3932168 | tf_op jit(solution)/shard_map/ppermute | solution.py:34
  5.7 6.9 %collective-permute-start.2 = (f32[640,512]{1,0:T(8,128)S(1)}, f32[640,512]{1,0:T(8,128)S(1)}, u32[]{:S(2)}, u32[]{:S(2)}) collective-permute-start(f32[640,512]{1,0:T(8,128)S(1)} %get-tuple-element.44), channel_id=1, source_target_pairs={{0,8},{8,0},{32,40},{40,32},{64,72},{72,64},{96,104},{104,96},{1,9... | collective-permute-start | bytes 3932168 | tf_op jit(solution)/shard_map/ppermute | solution.py:34
  6.1 12.8 %collective-permute-start.6 = (f32[768,512]{1,0:T(8,128)S(1)}, f32[768,512]{1,0:T(8,128)S(1)}, u32[]{:S(2)}, u32[]{:S(2)}) collective-permute-start(f32[768,512]{1,0:T(8,128)S(1)} %get-tuple-element.49), channel_id=1, source_target_pairs={{0,8},{8,0},{32,40},{40,32},{64,72},{72,64},{96,104},{104,96},{1,9... | collective-permute-start | bytes 4718600 | tf_op jit(solution)/shard_map/ppermute | solution.py:34
  7.9 18.7 %collective-permute-start.4 = (f32[640,256]{1,0:T(8,128)S(1)}, f32[640,256]{1,0:T(8,128)S(1)}, u32[]{:S(2)}, u32[]{:S(2)}) collective-permute-start(f32[640,256]{1,0:T(8,128)S(1)} %get-tuple-element.47), channel_id=1, source_target_pairs={{0,32},{8,40},{32,64},{40,72},{64,96},{72,104},{96,0},{104,8},{1,3... | collective-permute-start | bytes 1966088 | tf_op jit(solution)/shard_map/ppermute | solution.py:34
  9.7 16.9 %collective-permute-start.5 = (f32[640,256]{1,0:T(8,128)S(1)}, f32[640,256]{1,0:T(8,128)S(1)}, u32[]{:S(2)}, u32[]{:S(2)}) collective-permute-start(f32[640,256]{1,0:T(8,128)S(1)} %get-tuple-element.48), channel_id=1, source_target_pairs={{0,96},{8,104},{32,0},{40,8},{64,32},{72,40},{96,64},{104,72},{1,9... | collective-permute-start | bytes 1966088 | tf_op jit(solution)/shard_map/ppermute | solution.py:34
  11.9 26.8 %collective-permute-start.11 = (f32[1088,512]{1,0:T(8,128)S(1)}, f32[1088,512]{1,0:T(8,128)S(1)}, u32[]{:S(2)}, u32[]{:S(2)}) collective-permute-start(f32[1088,512]{1,0:T(8,128)S(1)} %get-tuple-element.56), channel_id=1, source_target_pairs={{0,8},{8,0},{32,40},{40,32},{64,72},{72,64},{96,104},{104,96},{1,9... | collective-permute-start | bytes 6684680 | tf_op jit(solution)/shard_map/ppermute | solution.py:34
  12.6 13.6 %collective-permute-start.7 = (f32[224,512]{1,0:T(8,128)S(1)}, f32[224,512]{1,0:T(8,128)S(1)}, u32[]{:S(2)}, u32[]{:S(2)}) collective-permute-start(f32[224,512]{1,0:T(8,128)S(1)} %get-tuple-element.50), channel_id=1, source_target_pairs={{0,16},{8,24},{32,48},{40,56},{64,80},{72,88},{96,112},{104,120},{... | collective-permute-start | bytes 1376264 | tf_op jit(solution)/shard_map/ppermute | solution.py:34
  28.7 38.0 %collective-permute-start.10 = (f32[800,512]{1,0:T(8,128)S(1)}, f32[800,512]{1,0:T(8,128)S(1)}, u32[]{:S(2)}, u32[]{:S(2)}) collective-permute-start(f32[800,512]{1,0:T(8,128)S(1)} %get-tuple-element.55), channel_id=1, source_target_pairs={{0,16},{8,24},{32,48},{40,56},{64,80},{72,88},{96,112},{104,120},{... | collective-permute-start | bytes 4915208 | tf_op jit(solution)/shard_map/ppermute | solution.py:34
  31.7 34.5 %collective-permute-start.8 = (f32[736,512]{1,0:T(8,128)S(1)}, f32[736,512]{1,0:T(8,128)S(1)}, u32[]{:S(2)}, u32[]{:S(2)}) collective-permute-start(f32[736,512]{1,0:T(8,128)S(1)} %get-tuple-element.53), channel_id=1, source_target_pairs={{0,32},{8,40},{32,64},{40,72},{64,96},{72,104},{96,0},{104,8},{1,3... | collective-permute-start | bytes 4521992 | tf_op jit(solution)/shard_map/ppermute | solution.py:34
  32.0 34.2 %collective-permute-start.9 = (f32[736,512]{1,0:T(8,128)S(1)}, f32[736,512]{1,0:T(8,128)S(1)}, u32[]{:S(2)}, u32[]{:S(2)}) collective-permute-start(f32[736,512]{1,0:T(8,128)S(1)} %get-tuple-element.54), channel_id=1, source_target_pairs={{0,96},{8,104},{32,0},{40,8},{64,32},{72,40},{96,64},{104,72},{1,9... | collective-permute-start | bytes 4521992 | tf_op jit(solution)/shard_map/ppermute | solution.py:34
  34.3 4.4 %collective-permute-start = (f32[640,512]{1,0:T(8,128)S(1)}, f32[640,512]{1,0:T(8,128)S(1)}, u32[]{:S(2)}, u32[]{:S(2)}) collective-permute-start(f32[640,512]{1,0:T(8,128)S(1)} %get-tuple-element.42), channel_id=1, source_target_pairs={{0,8},{8,0},{32,40},{40,32},{64,72},{72,64},{96,104},{104,96},{1,9... | collective-permute-start | bytes 3932168 | tf_op jit(solution)/shard_map/ppermute | solution.py:34
  68.5 15.3 %collective-permute-start.15 = (f32[256,512]{1,0:T(8,128)S(1)}, f32[256,512]{1,0:T(8,128)S(1)}, u32[]{:S(2)}, u32[]{:S(2)}) collective-permute-start(f32[256,512]{1,0:T(8,128)S(1)} %get-tuple-element.66), channel_id=1, source_target_pairs={{0,2},{8,10},{32,34},{40,42},{64,66},{72,74},{96,98},{104,106},{1,... | collective-permute-start | bytes 1572872 | tf_op jit(solution)/shard_map/ppermute | solution.py:34
  69.8 14.0 %collective-permute-start.16 = (f32[256,512]{1,0:T(8,128)S(1)}, f32[256,512]{1,0:T(8,128)S(1)}, u32[]{:S(2)}, u32[]{:S(2)}) collective-permute-start(f32[256,512]{1,0:T(8,128)S(1)} %get-tuple-element.66), channel_id=1, source_target_pairs={{0,8},{8,0},{32,40},{40,32},{64,72},{72,64},{96,104},{104,96},{1,9... | collective-permute-start | bytes 1572872 | tf_op jit(solution)/shard_map/ppermute | solution.py:34
  71.9 12.0 %collective-permute-start.13 = (f32[192,512]{1,0:T(8,128)S(1)}, f32[192,512]{1,0:T(8,128)S(1)}, u32[]{:S(2)}, u32[]{:S(2)}) collective-permute-start(f32[192,512]{1,0:T(8,128)S(1)} %get-tuple-element.63), channel_id=1, source_target_pairs={{0,32},{8,40},{32,64},{40,72},{64,96},{72,104},{96,0},{104,8},{1,3... | collective-permute-start | bytes 1179656 | tf_op jit(solution)/shard_map/ppermute | solution.py:34
  72.3 11.5 %collective-permute-start.14 = (f32[192,512]{1,0:T(8,128)S(1)}, f32[192,512]{1,0:T(8,128)S(1)}, u32[]{:S(2)}, u32[]{:S(2)}) collective-permute-start(f32[192,512]{1,0:T(8,128)S(1)} %get-tuple-element.64), channel_id=1, source_target_pairs={{0,96},{8,104},{32,0},{40,8},{64,32},{72,40},{96,64},{104,72},{1,9... | collective-permute-start | bytes 1179656 | tf_op jit(solution)/shard_map/ppermute | solution.py:34
  78.1 20.5 %collective-permute-start.12 = (f32[320,512]{1,0:T(8,128)S(1)}, f32[320,512]{1,0:T(8,128)S(1)}, u32[]{:S(2)}, u32[]{:S(2)}) collective-permute-start(f32[320,512]{1,0:T(8,128)S(1)} %get-tuple-element.61), channel_id=1, source_target_pairs={{0,16},{8,24},{32,48},{40,56},{64,80},{72,88},{96,112},{104,120},{... | collective-permute-start | bytes 1966088 | tf_op jit(solution)/shard_map/ppermute | solution.py:34
  85.5 5.8 %collective-permute-start.17 = (f32[8,13,256]{2,1,0:T(8,128)S(1)}, f32[8,13,256]{2,1,0:T(8,128)S(1)}, u32[]{:S(2)}, u32[]{:S(2)}) collective-permute-start(f32[8,13,256]{2,1,0:T(8,128)S(1)} %get-tuple-element.67.refs_0_.refs_5_), channel_id=1, source_target_pairs={{0,4},{8,12},{32,36},{40,44},{64,68},{72,76},{96,100},{104,108},{1... | collective-permute-start | bytes 319496 | tf_op jit(solution)/shard_map/ppermute | solution.py:34
  88.0 5.5 %collective-permute-start.18 = (f32[8,13,256]{2,1,0:T(8,128)S(1)}, f32[8,13,256]{2,1,0:T(8,128)S(1)}, u32[]{:S(2)}, u32[]{:S(2)}) collective-permute-start(f32[8,13,256]{2,1,0:T(8,128)S(1)} %get-tuple-element.67.refs_0_.refs_5_), channel_id=1, source_target_pairs={{0,2},{8,10},{32,34},{40,42},{64,66},{72,74},{96,98},{104,106},{1,... | collective-permute-start | bytes 319496 | tf_op jit(solution)/shard_map/ppermute | solution.py:34
  88.0 6.8 %collective-permute-start.19 = (f32[8,13,256]{2,1,0:T(8,128)S(1)}, f32[8,13,256]{2,1,0:T(8,128)S(1)}, u32[]{:S(2)}, u32[]{:S(2)}) collective-permute-start(f32[8,13,256]{2,1,0:T(8,128)S(1)} %get-tuple-element.67.refs_0_.refs_5_), channel_id=1, source_target_pairs={{0,6},{8,14},{32,38},{40,46},{64,70},{72,78},{96,102},{104,110},{1... | collective-permute-start | bytes 319496 | tf_op jit(solution)/shard_map/ppermute | solution.py:34
  94.8 9.7 %collective-permute-start.21 = (f32[8,13,256]{2,1,0:T(8,128)S(1)}, f32[8,13,256]{2,1,0:T(8,128)S(1)}, u32[]{:S(2)}, u32[]{:S(2)}) collective-permute-start(f32[8,13,256]{2,1,0:T(8,128)S(1)} %get-tuple-element.75.refs_0_), channel_id=1, source_target_pairs={{0,16},{8,24},{32,48},{40,56},{64,80},{72,88},{96,112},{104,120},{... | collective-permute-start | bytes 319496 | tf_op jit(solution)/shard_map/ppermute | solution.py:34
  97.8 6.7 %collective-permute-start.22 = (f32[8,13,256]{2,1,0:T(8,128)S(1)}, f32[8,13,256]{2,1,0:T(8,128)S(1)}, u32[]{:S(2)}, u32[]{:S(2)}) collective-permute-start(f32[8,13,256]{2,1,0:T(8,128)S(1)} %get-tuple-element.75.refs_0_), channel_id=1, source_target_pairs={{0,1},{8,9},{32,33},{40,41},{64,65},{72,73},{96,97},{104,105},{1,0... | collective-permute-start | bytes 319496 | tf_op jit(solution)/shard_map/ppermute | solution.py:34
  98.2 6.3 %collective-permute-start.23 = (f32[8,13,256]{2,1,0:T(8,128)S(1)}, f32[8,13,256]{2,1,0:T(8,128)S(1)}, u32[]{:S(2)}, u32[]{:S(2)}) collective-permute-start(f32[8,13,256]{2,1,0:T(8,128)S(1)} %get-tuple-element.75.refs_0_), channel_id=1, source_target_pairs={{0,17},{8,25},{32,49},{40,57},{64,81},{72,89},{96,113},{104,121},{... | collective-permute-start | bytes 319496 | tf_op jit(solution)/shard_map/ppermute | solution.py:34
  100.1 7.8 %collective-permute-start.20 = (f32[256,512]{1,0:T(8,128)S(1)}, f32[256,512]{1,0:T(8,128)S(1)}, u32[]{:S(2)}, u32[]{:S(2)}) collective-permute-start(f32[256,512]{1,0:T(8,128)S(1)} %get-tuple-element.74), channel_id=1, source_target_pairs={{0,8},{8,0},{32,40},{40,32},{64,72},{72,64},{96,104},{104,96},{1,9... | collective-permute-start | bytes 1572872 | tf_op jit(solution)/shard_map/ppermute | solution.py:34
  (4 other events, 22.8 us)

commit v5 on v4

--- a/solution.py
+++ b/solution.py
@@ -210,17 +210,19 @@
     def onward(i, first, h_add, i_add, cols):
         def run(z, piece, term, out):
             side((2 * i, 2 * i + 1), i, 0, h_add, i_add)(z, piece, term, out.at[:2 * zr])
-            value = term(4)[3 * yr:, cols] + term(5)[:yr, cols] + piece(7)[:, cols].astype(F32)
+            value = term(4)[3 * yr:, cols] + term(5)[:yr, cols] + piece(4)[:, cols].astype(F32)
             out[2 * zr:, left] = value[:fold]
             out[2 * zr:, right] = value[fold:]
         return run
 
-    u2, d2, y2, t2 = call(
-        "sides", [z_rows(UP, 0, 0), z_rows(UP, 1, 0), z_rows(DOWN, 0, 0), z_rows(DOWN, 1, 0),
-                  y_rows(UP, 1, 0), y_rows(DOWN, 1, 0), y_rows(MINE, 1, 0), y_rows(OPP, 0, 0)],
-        [c_up, c_down, gu1, gd1, c_cross, gy1, params_part(FIRST, OWN // 2 - FIRST)], [tt],
-        [((2 * zr + fold, COLS), onward(0, 0, 0, 2, left)), ((2 * zr + fold, COLS), onward(1, 0, 1, 3, right)),
-         ((3 * yr + OWN // 2 - FIRST, COLS), with_params(add((4, 5, 6), 4, 0), 6))])
+    y2, _ = call(
+        "crossing", [y_rows(UP, 1, 0), y_rows(DOWN, 1, 0), y_rows(MINE, 1, 0)],
+        [c_cross, params_part(FIRST, OWN // 2 - FIRST)], [t1],
+        [((3 * yr + OWN // 2 - FIRST, COLS), with_params(add((0, 1, 2), 0, 0), 1))])
+    u2, d2, t2 = call(
+        "sides", [z_rows(UP, 0, 0), z_rows(UP, 1, 0), z_rows(DOWN, 0, 0), z_rows(DOWN, 1, 0), y_rows(OPP, 0, 0)],
+        [c_up, c_down, gu1, gd1, c_cross, gy1], [tt],
+        [((2 * zr + fold, COLS), onward(0, 0, 0, 2, left)), ((2 * zr + fold, COLS), onward(1, 0, 1, 3, right))], cost=100000000)
     gu2, gd2, gy2 = up(u2), down(d2), swap(y2, y=2)
 
     def own_body(r):

time: 112 us -> 109 us (0.973)
  starting transfers between devices: 37 us -> 34.2 us
  waiting for transfers between devices: 48.5 us -> 46.4 us
  Pallas kernels: 24 us -> 25.3 us
    ppermute x25, starting transfers between devices: 37 us -> 34.2 us  [swap(): return lax.ppermute(value, AXES, pairs)]
    ppermute x25, waiting for transfers between devices: 48.5 us -> 46.4 us  [swap(): return lax.ppermute(value, AXES, pairs)]
    pallas_call x12 -> x13, Pallas kernels: 20.2 us -> 21.5 us  [piece_call(): pl.pallas_call(kernel, in_specs=[pl.BlockSpec(memory_space=pltpu.HBM)] +...]
  transfers between devices with their start and end apart: 25 -> 25, of which waited for: 11 -> 11; matrix products, arithmetic and copies ran while one was open for 1% -> 1% of each run, Pallas kernels for 15% -> 17%
where the time goes in v5:
time: 109 us; the launch traced here: 108 us
  waiting for transfers between devices  46.4 us (43%)
  starting transfers between devices  34.2 us (31%)
  Pallas kernels  25.3 us (23%)
  other arithmetic  1.48 us (1%)
    ppermute x25, waiting for transfers between devices, swap(): return lax.ppermute(value, AXES, pairs)  46.4 us
    ppermute x25, starting transfers between devices, swap(): return lax.ppermute(value, AXES, pairs)  34.2 us
    pallas_call x13, Pallas kernels, piece_call(): pl.pallas_call(kernel, in_specs=[pl.BlockSpec(memory_space=pltpu.HBM)] +...  21.5 us
    pallas_call x1, Pallas kernels, update_call(): pl.pallas_call(update_kernel, in_specs=[pl.BlockSpec(memory_space=pltpu.V...  3.79 us
  transfers between devices with their start and end apart: 25, of which 11 were waited for; matrix products, arithmetic and copies ran while one was open for 1% of the time, Pallas kernels for 17%

profile of v5, /device:TPU:1, one launch (start us, length us, event | category | flops | bytes accessed | tf_op | source)
XLA Modules:
  0.0 108.3 jit_solution(147776981302725574)
XLA Ops:
  3.4 2.1 %widen_b.1 = (f32[640,512]{1,0:T(8,128)S(1)}, f32[640,512]{1,0:T(8,128)S(1)}, f32[768,512]{1,0:T(8,128)S(1)}, f32[640,512]{1,0:T(8,128)S(1)}, f32[1088,512]{1,0:T(8,128)S(1)}, /*index=5*/f32[8,128]{1,0:T(8,128)S(1)}) custom-call(bf16[4,2,2,512,512]{4,3,2,1,0:T(8,128)(2,1)} %bitcast.20, f32[512,512]{1,0:T(8,128)S(1)} %copy-done, ...), custom_call_target="tpu_custom_call" | custom-call | flops 100 | bytes 1 | tf_op jit(solution)/shard_map/widen_b/pallas_call | solution.py:99
  7.9 1.8 %collective-permute-start.4 = (f32[640,256]{1,0:T(8,128)S(1)}, f32[640,256]{1,0:T(8,128)S(1)}, u32[]{:S(2)}, u32[]{:S(2)}) collective-permute-start(f32[640,256]{1,0:T(8,128)S(1)} %get-tuple-element.47), channel_id=1, source_target_pairs={{0,32},{8,40},{32,64},{40,72},{64,96},{72,104},{96,0},{104,8},{1,3... | collective-permute-start | bytes 1966088 | tf_op jit(solution)/shard_map/ppermute | solution.py:34
  9.7 2.2 %collective-permute-start.5 = (f32[640,256]{1,0:T(8,128)S(1)}, f32[640,256]{1,0:T(8,128)S(1)}, u32[]{:S(2)}, u32[]{:S(2)}) collective-permute-start(f32[640,256]{1,0:T(8,128)S(1)} %get-tuple-element.48), channel_id=1, source_target_pairs={{0,96},{8,104},{32,0},{40,8},{64,32},{72,40},{96,64},{104,72},{1,9... | collective-permute-start | bytes 1966088 | tf_op jit(solution)/shard_map/ppermute | solution.py:34
  11.9 2.9 %collective-permute-start.7 = (f32[224,512]{1,0:T(8,128)S(1)}, f32[224,512]{1,0:T(8,128)S(1)}, u32[]{:S(2)}, u32[]{:S(2)}) collective-permute-start(f32[224,512]{1,0:T(8,128)S(1)} %get-tuple-element.50), channel_id=1, source_target_pairs={{0,16},{8,24},{32,48},{40,56},{64,80},{72,88},{96,112},{104,120},{... | collective-permute-start | bytes 1376264 | tf_op jit(solution)/shard_map/ppermute | solution.py:34
  15.8 2.4 %band_table.1 = (bf16[256,4096]{1,0:T(8,128)(2,1)S(1)}, bf16[256,4096]{1,0:T(8,128)(2,1)S(1)}, f32[8,128]{1,0:T(8,128)S(1)}) custom-call(bf16[4,2,2,512,512]{4,3,2,1,0:T(8,128)(2,1)} %bitcast.22, f32[256,64]{1,0:T(8,128)S(1)} %get-tuple-element.89.refs_0_, f32[256,64]{1,0:T(8,128)S(1)} %get-tuple-element.88.refs_1_.refs_4_, ...), custom_call_target="tpu_custom_call" | custom-call | flops 100 | bytes 1 | tf_op jit(solution)/shard_map/band_table/pallas_call | solution.py:99
  21.1 3.7 %collective-permute-done.7.refs_5_ = f32[224,512]{1,0:T(8,128)S(1)} collective-permute-done((f32[224,512]{1,0:T(8,128)S(1)}, f32[224,512]{1,0:T(8,128)S(1)}, u32[]{:S(2)}, u32[]{:S(2)}) %collective-permute-start.7) | collective-permute-done | bytes 458784 | tf_op jit(solution)/shard_map/ppermute | solution.py:34
  24.9 1.8 %collective-permute-done.4.refs_2_ = f32[640,256]{1,0:T(8,128)S(1)} collective-permute-done((f32[640,256]{1,0:T(8,128)S(1)}, f32[640,256]{1,0:T(8,128)S(1)}, u32[]{:S(2)}, u32[]{:S(2)}) %collective-permute-start.4) | collective-permute-done | bytes 655392 | tf_op jit(solution)/shard_map/ppermute | solution.py:34
  28.7 2.3 %collective-permute-start.9 = (f32[736,512]{1,0:T(8,128)S(1)}, f32[736,512]{1,0:T(8,128)S(1)}, u32[]{:S(2)}, u32[]{:S(2)}) collective-permute-start(f32[736,512]{1,0:T(8,128)S(1)} %get-tuple-element.54), channel_id=1, source_target_pairs={{0,96},{8,104},{32,0},{40,8},{64,32},{72,40},{96,64},{104,72},{1,9... | collective-permute-start | bytes 4521992 | tf_op jit(solution)/shard_map/ppermute | solution.py:34
  32.5 2.7 %collective-permute-done.refs_0_ = f32[640,512]{1,0:T(8,128)S(1)} collective-permute-done((f32[640,512]{1,0:T(8,128)S(1)}, f32[640,512]{1,0:T(8,128)S(1)}, u32[]{:S(2)}, u32[]{:S(2)}) %collective-permute-start) | collective-permute-done | bytes 1310752 | tf_op jit(solution)/shard_map/ppermute | solution.py:34
  35.1 25.3 %collective-permute-done.10.refs_3_ = f32[800,512]{1,0:T(8,128)S(1)} collective-permute-done((f32[800,512]{1,0:T(8,128)S(1)}, f32[800,512]{1,0:T(8,128)S(1)}, u32[]{:S(2)}, u32[]{:S(2)}) %collective-permute-start.10) | collective-permute-done | bytes 1638432 | tf_op jit(solution)/shard_map/ppermute | solution.py:34
  60.5 2.7 %collective-permute-done.8.refs_1_ = f32[736,512]{1,0:T(8,128)S(1)} collective-permute-done((f32[736,512]{1,0:T(8,128)S(1)}, f32[736,512]{1,0:T(8,128)S(1)}, u32[]{:S(2)}, u32[]{:S(2)}) %collective-permute-start.8) | collective-permute-done | bytes 1507360 | tf_op jit(solution)/shard_map/ppermute | solution.py:34
  63.2 1.8 %own.1 = (f32[320,512]{1,0:T(8,128)S(1)}, f32[192,512]{1,0:T(8,128)S(1)}, f32[192,512]{1,0:T(8,128)S(1)}, f32[320,512]{1,0:T(8,128)S(1)}, f32[192,512]{1,0:T(8,1...) custom-call(bf16[4,2,2,512,512]{4,3,2,1,0:T(8,128)(2,1)} %bitcast.25, ...), custom_call_target="tpu_custom_call" | custom-call | flops 100 | bytes 1 | tf_op jit(solution)/shard_map/own/pallas_call | solution.py:99
  66.3 2.1 %collective-permute-start.16 = (f32[256,512]{1,0:T(8,128)S(1)}, f32[256,512]{1,0:T(8,128)S(1)}, u32[]{:S(2)}, u32[]{:S(2)}) collective-permute-start(f32[256,512]{1,0:T(8,128)S(1)} %get-tuple-element.66), channel_id=1, source_target_pairs={{0,8},{8,0},{32,40},{40,32},{64,72},{72,64},{96,104},{104,96},{1,9... | collective-permute-start | bytes 1572872 | tf_op jit(solution)/shard_map/ppermute | solution.py:34
  69.0 2.1 %collective-permute-start.14 = (f32[192,512]{1,0:T(8,128)S(1)}, f32[192,512]{1,0:T(8,128)S(1)}, u32[]{:S(2)}, u32[]{:S(2)}) collective-permute-start(f32[192,512]{1,0:T(8,128)S(1)} %get-tuple-element.64), channel_id=1, source_target_pairs={{0,96},{8,104},{32,0},{40,8},{64,32},{72,40},{96,64},{104,72},{1,9... | collective-permute-start | bytes 1179656 | tf_op jit(solution)/shard_map/ppermute | solution.py:34
  71.6 3.0 %partial_encode.1 = (f32[8,10,256]{2,1,0:T(8,128)S(1)}, f32[320,512]{1,0:T(8,128)S(1)}, f32[8,128]{1,0:T(8,128)}) custom-call(bf16[4,2,2,512,512]{4,3,2,1,0:T(8,128)(2,1)} %bitcast.26, f32[320,512]{1,0:T(8,128)S(1)} %get-tuple-element.58.refs_0_, f32[320,512]{1,0:T(8,128)S(1)} %get-tuple-element.59.refs_1_, f32[512,512]{1,0:T(8,128)S(1)} %bitcast.11, ...), custom_call_target="tpu_custom_call" | custom-call | flops 100 | bytes 1 | tf_op jit(solution)/shard_map/partial_encode/pallas_call | solution.py:99
  74.6 3.0 %collective-permute-start.12 = (f32[320,512]{1,0:T(8,128)S(1)}, f32[320,512]{1,0:T(8,128)S(1)}, u32[]{:S(2)}, u32[]{:S(2)}) collective-permute-start(f32[320,512]{1,0:T(8,128)S(1)} %get-tuple-element.61), channel_id=1, source_target_pairs={{0,16},{8,24},{32,48},{40,56},{64,80},{72,88},{96,112},{104,120},{... | collective-permute-start | bytes 1966088 | tf_op jit(solution)/shard_map/ppermute | solution.py:34
  77.6 2.7 %collective-permute-done.13.refs_1_ = f32[192,512]{1,0:T(8,128)S(1)} collective-permute-done((f32[192,512]{1,0:T(8,128)S(1)}, f32[192,512]{1,0:T(8,128)S(1)}, u32[]{:S(2)}, u32[]{:S(2)}) %collective-permute-start.13) | collective-permute-done | bytes 393248 | tf_op jit(solution)/shard_map/ppermute | solution.py:34
  82.0 2.5 %collective-permute-start.17 = (f32[8,13,256]{2,1,0:T(8,128)S(1)}, f32[8,13,256]{2,1,0:T(8,128)S(1)}, u32[]{:S(2)}, u32[]{:S(2)}) collective-permute-start(f32[8,13,256]{2,1,0:T(8,128)S(1)} %get-tuple-element.67.refs_0_.refs_5_), channel_id=1, source_target_pairs={{0,4},{8,12},{32,36},{40,44},{64,68},{72,76},{96,100},{104,108},{1... | collective-permute-start | bytes 319496 | tf_op jit(solution)/shard_map/ppermute | solution.py:34
  85.3 2.5 %collective-permute-done.17.refs_1_ = f32[8,13,256]{2,1,0:T(8,128)S(1)} collective-permute-done((f32[8,13,256]{2,1,0:T(8,128)S(1)}, f32[8,13,256]{2,1,0:T(8,128)S(1)}, u32[]{:S(2)}, u32[]{:S(2)}) %collective-permute-start.17) | collective-permute-done | bytes 106528 | tf_op jit(solution)/shard_map/ppermute | solution.py:34
  87.8 2.2 %collective-permute-done.18.refs_2_ = f32[8,13,256]{2,1,0:T(8,128)S(1)} collective-permute-done((f32[8,13,256]{2,1,0:T(8,128)S(1)}, f32[8,13,256]{2,1,0:T(8,128)S(1)}, u32[]{:S(2)}, u32[]{:S(2)}) %collective-permute-start.18) | collective-permute-done | bytes 106528 | tf_op jit(solution)/shard_map/ppermute | solution.py:34
  91.3 3.0 %collective-permute-start.21 = (f32[8,13,256]{2,1,0:T(8,128)S(1)}, f32[8,13,256]{2,1,0:T(8,128)S(1)}, u32[]{:S(2)}, u32[]{:S(2)}) collective-permute-start(f32[8,13,256]{2,1,0:T(8,128)S(1)} %get-tuple-element.75.refs_0_), channel_id=1, source_target_pairs={{0,16},{8,24},{32,48},{40,56},{64,80},{72,88},{96,112},{104,120},{... | collective-permute-start | bytes 319496 | tf_op jit(solution)/shard_map/ppermute | solution.py:34
  96.6 2.0 %collective-permute-start.20 = (f32[256,512]{1,0:T(8,128)S(1)}, f32[256,512]{1,0:T(8,128)S(1)}, u32[]{:S(2)}, u32[]{:S(2)}) collective-permute-start(f32[256,512]{1,0:T(8,128)S(1)} %get-tuple-element.74), channel_id=1, source_target_pairs={{0,8},{8,0},{32,40},{40,32},{64,72},{72,64},{96,104},{104,96},{1,9... | collective-permute-start | bytes 1572872 | tf_op jit(solution)/shard_map/ppermute | solution.py:34
  98.5 2.5 %momentum_residual.1 = (f32[512,512]{1,0:T(8,128)}, f32[8,128]{1,0:T(8,128)S(1)}) custom-call(bf16[4,2,2,512,512]{4,3,2,1,0:T(8,128)(2,1)} %bitcast.30, f32[320,512]{1,0:T(8,128)S(1)} %get-tuple-element.69.refs_0_, f32[192,512]{1,0:T(8,128)S(1)} %get-tuple-element.70.refs_1_, f32[8,8,256]{2,1,0:T(8,128)S(1)} %get-tuple-element.71.refs_2_, ...), custom_call_target="tpu_custom_call" | custom-call | flops 900000000 | bytes 9000000 | tf_op jit(solution)/shard_map/momentum_residual/pallas_call | solution.py:99
  104.4 3.8 %parameter_update.1 = f32[4,8,64,512]{3,2,1,0:T(8,128)} custom-call(f32[8,64,512]{2,1,0:T(8,128)S(1)} %bitcast.10, f32[4,64,512]{2,1,0:T(8,128)S(1)} %bitcast.17, f32[4,64,512]{2,1,0:T(8,128)S(1)} %bitcast.15, f32[17,64,512]{2,1,0:T(8,128)S(1)} %bitcast.14, f32[4,64,512]{2,1,0:T(8,128)S(1)} %bitcast.16, f32[4,64,512]{2,1,0:T(8,128)S(1)} %bitcast.18, ...), custom_call_target="tpu_custom_call" | custom-call | tf_op jit(solution)/shard_map/parameter_update/pallas_call | solution.py:427
  (50 shorter events, 24.3 us)
Async XLA Ops:
  1.9 4.7 %collective-permute-start.3 = (f32[832,512]{1,0:T(8,128)S(1)}, f32[832,512]{1,0:T(8,128)S(1)}, u32[]{:S(2)}, u32[]{:S(2)}) collective-permute-start(f32[832,512]{1,0:T(8,128)S(1)} %get-tuple-element.45), channel_id=1, source_target_pairs={{0,8},{8,0},{32,40},{40,32},{64,72},{72,64},{96,104},{104,96},{1,9... | collective-permute-start | bytes 5111816 | tf_op jit(solution)/shard_map/ppermute | solution.py:34
  5.5 6.4 %collective-permute-start.6 = (f32[768,512]{1,0:T(8,128)S(1)}, f32[768,512]{1,0:T(8,128)S(1)}, u32[]{:S(2)}, u32[]{:S(2)}) collective-permute-start(f32[768,512]{1,0:T(8,128)S(1)} %get-tuple-element.49), channel_id=1, source_target_pairs={{0,8},{8,0},{32,40},{40,32},{64,72},{72,64},{96,104},{104,96},{1,9... | collective-permute-start | bytes 4718600 | tf_op jit(solution)/shard_map/ppermute | solution.py:34
  5.7 14.3 %collective-permute-start.1 = (f32[640,512]{1,0:T(8,128)S(1)}, f32[640,512]{1,0:T(8,128)S(1)}, u32[]{:S(2)}, u32[]{:S(2)}) collective-permute-start(f32[640,512]{1,0:T(8,128)S(1)} %get-tuple-element.43), channel_id=1, source_target_pairs={{0,8},{8,0},{32,40},{40,32},{64,72},{72,64},{96,104},{104,96},{1,9... | collective-permute-start | bytes 3932168 | tf_op jit(solution)/shard_map/ppermute | solution.py:34
  6.1 15.0 %collective-permute-start.2 = (f32[640,512]{1,0:T(8,128)S(1)}, f32[640,512]{1,0:T(8,128)S(1)}, u32[]{:S(2)}, u32[]{:S(2)}) collective-permute-start(f32[640,512]{1,0:T(8,128)S(1)} %get-tuple-element.44), channel_id=1, source_target_pairs={{0,8},{8,0},{32,40},{40,32},{64,72},{72,64},{96,104},{104,96},{1,9... | collective-permute-start | bytes 3932168 | tf_op jit(solution)/shard_map/ppermute | solution.py:34
  7.9 18.7 %collective-permute-start.4 = (f32[640,256]{1,0:T(8,128)S(1)}, f32[640,256]{1,0:T(8,128)S(1)}, u32[]{:S(2)}, u32[]{:S(2)}) collective-permute-start(f32[640,256]{1,0:T(8,128)S(1)} %get-tuple-element.47), channel_id=1, source_target_pairs={{0,32},{8,40},{32,64},{40,72},{64,96},{72,104},{96,0},{104,8},{1,3... | collective-permute-start | bytes 1966088 | tf_op jit(solution)/shard_map/ppermute | solution.py:34
  9.7 16.9 %collective-permute-start.5 = (f32[640,256]{1,0:T(8,128)S(1)}, f32[640,256]{1,0:T(8,128)S(1)}, u32[]{:S(2)}, u32[]{:S(2)}) collective-permute-start(f32[640,256]{1,0:T(8,128)S(1)} %get-tuple-element.48), channel_id=1, source_target_pairs={{0,96},{8,104},{32,0},{40,8},{64,32},{72,40},{96,64},{104,72},{1,9... | collective-permute-start | bytes 1966088 | tf_op jit(solution)/shard_map/ppermute | solution.py:34
  11.9 12.9 %collective-permute-start.7 = (f32[224,512]{1,0:T(8,128)S(1)}, f32[224,512]{1,0:T(8,128)S(1)}, u32[]{:S(2)}, u32[]{:S(2)}) collective-permute-start(f32[224,512]{1,0:T(8,128)S(1)} %get-tuple-element.50), channel_id=1, source_target_pairs={{0,16},{8,24},{32,48},{40,56},{64,80},{72,88},{96,112},{104,120},{... | collective-permute-start | bytes 1376264 | tf_op jit(solution)/shard_map/ppermute | solution.py:34
  20.1 15.1 %collective-permute-start.11 = (f32[1088,512]{1,0:T(8,128)S(1)}, f32[1088,512]{1,0:T(8,128)S(1)}, u32[]{:S(2)}, u32[]{:S(2)}) collective-permute-start(f32[1088,512]{1,0:T(8,128)S(1)} %get-tuple-element.56), channel_id=1, source_target_pairs={{0,8},{8,0},{32,40},{40,32},{64,72},{72,64},{96,104},{104,96},{1,9... | collective-permute-start | bytes 6684680 | tf_op jit(solution)/shard_map/ppermute | solution.py:34
  21.1 39.4 %collective-permute-start.10 = (f32[800,512]{1,0:T(8,128)S(1)}, f32[800,512]{1,0:T(8,128)S(1)}, u32[]{:S(2)}, u32[]{:S(2)}) collective-permute-start(f32[800,512]{1,0:T(8,128)S(1)} %get-tuple-element.55), channel_id=1, source_target_pairs={{0,16},{8,24},{32,48},{40,56},{64,80},{72,88},{96,112},{104,120},{... | collective-permute-start | bytes 4915208 | tf_op jit(solution)/shard_map/ppermute | solution.py:34
  28.3 34.9 %collective-permute-start.8 = (f32[736,512]{1,0:T(8,128)S(1)}, f32[736,512]{1,0:T(8,128)S(1)}, u32[]{:S(2)}, u32[]{:S(2)}) collective-permute-start(f32[736,512]{1,0:T(8,128)S(1)} %get-tuple-element.53), channel_id=1, source_target_pairs={{0,32},{8,40},{32,64},{40,72},{64,96},{72,104},{96,0},{104,8},{1,3... | collective-permute-start | bytes 4521992 | tf_op jit(solution)/shard_map/ppermute | solution.py:34
  28.7 34.5 %collective-permute-start.9 = (f32[736,512]{1,0:T(8,128)S(1)}, f32[736,512]{1,0:T(8,128)S(1)}, u32[]{:S(2)}, u32[]{:S(2)}) collective-permute-start(f32[736,512]{1,0:T(8,128)S(1)} %get-tuple-element.54), channel_id=1, source_target_pairs={{0,96},{8,104},{32,0},{40,8},{64,32},{72,40},{96,64},{104,72},{1,9... | collective-permute-start | bytes 4521992 | tf_op jit(solution)/shard_map/ppermute | solution.py:34
  31.0 4.1 %collective-permute-start = (f32[640,512]{1,0:T(8,128)S(1)}, f32[640,512]{1,0:T(8,128)S(1)}, u32[]{:S(2)}, u32[]{:S(2)}) collective-permute-start(f32[640,512]{1,0:T(8,128)S(1)} %get-tuple-element.42), channel_id=1, source_target_pairs={{0,8},{8,0},{32,40},{40,32},{64,72},{72,64},{96,104},{104,96},{1,9... | collective-permute-start | bytes 3932168 | tf_op jit(solution)/shard_map/ppermute | solution.py:34
  65.0 15.3 %collective-permute-start.15 = (f32[256,512]{1,0:T(8,128)S(1)}, f32[256,512]{1,0:T(8,128)S(1)}, u32[]{:S(2)}, u32[]{:S(2)}) collective-permute-start(f32[256,512]{1,0:T(8,128)S(1)} %get-tuple-element.66), channel_id=1, source_target_pairs={{0,2},{8,10},{32,34},{40,42},{64,66},{72,74},{96,98},{104,106},{1,... | collective-permute-start | bytes 1572872 | tf_op jit(solution)/shard_map/ppermute | solution.py:34
  66.3 14.0 %collective-permute-start.16 = (f32[256,512]{1,0:T(8,128)S(1)}, f32[256,512]{1,0:T(8,128)S(1)}, u32[]{:S(2)}, u32[]{:S(2)}) collective-permute-start(f32[256,512]{1,0:T(8,128)S(1)} %get-tuple-element.66), channel_id=1, source_target_pairs={{0,8},{8,0},{32,40},{40,32},{64,72},{72,64},{96,104},{104,96},{1,9... | collective-permute-start | bytes 1572872 | tf_op jit(solution)/shard_map/ppermute | solution.py:34
  68.4 12.0 %collective-permute-start.13 = (f32[192,512]{1,0:T(8,128)S(1)}, f32[192,512]{1,0:T(8,128)S(1)}, u32[]{:S(2)}, u32[]{:S(2)}) collective-permute-start(f32[192,512]{1,0:T(8,128)S(1)} %get-tuple-element.63), channel_id=1, source_target_pairs={{0,32},{8,40},{32,64},{40,72},{64,96},{72,104},{96,0},{104,8},{1,3... | collective-permute-start | bytes 1179656 | tf_op jit(solution)/shard_map/ppermute | solution.py:34
  69.0 11.3 %collective-permute-start.14 = (f32[192,512]{1,0:T(8,128)S(1)}, f32[192,512]{1,0:T(8,128)S(1)}, u32[]{:S(2)}, u32[]{:S(2)}) collective-permute-start(f32[192,512]{1,0:T(8,128)S(1)} %get-tuple-element.64), channel_id=1, source_target_pairs={{0,96},{8,104},{32,0},{40,8},{64,32},{72,40},{96,64},{104,72},{1,9... | collective-permute-start | bytes 1179656 | tf_op jit(solution)/shard_map/ppermute | solution.py:34
  74.6 20.5 %collective-permute-start.12 = (f32[320,512]{1,0:T(8,128)S(1)}, f32[320,512]{1,0:T(8,128)S(1)}, u32[]{:S(2)}, u32[]{:S(2)}) collective-permute-start(f32[320,512]{1,0:T(8,128)S(1)} %get-tuple-element.61), channel_id=1, source_target_pairs={{0,16},{8,24},{32,48},{40,56},{64,80},{72,88},{96,112},{104,120},{... | collective-permute-start | bytes 1966088 | tf_op jit(solution)/shard_map/ppermute | solution.py:34
  82.0 5.8 %collective-permute-start.17 = (f32[8,13,256]{2,1,0:T(8,128)S(1)}, f32[8,13,256]{2,1,0:T(8,128)S(1)}, u32[]{:S(2)}, u32[]{:S(2)}) collective-permute-start(f32[8,13,256]{2,1,0:T(8,128)S(1)} %get-tuple-element.67.refs_0_.refs_5_), channel_id=1, source_target_pairs={{0,4},{8,12},{32,36},{40,44},{64,68},{72,76},{96,100},{104,108},{1... | collective-permute-start | bytes 319496 | tf_op jit(solution)/shard_map/ppermute | solution.py:34
  84.5 5.5 %collective-permute-start.18 = (f32[8,13,256]{2,1,0:T(8,128)S(1)}, f32[8,13,256]{2,1,0:T(8,128)S(1)}, u32[]{:S(2)}, u32[]{:S(2)}) collective-permute-start(f32[8,13,256]{2,1,0:T(8,128)S(1)} %get-tuple-element.67.refs_0_.refs_5_), channel_id=1, source_target_pairs={{0,2},{8,10},{32,34},{40,42},{64,66},{72,74},{96,98},{104,106},{1,... | collective-permute-start | bytes 319496 | tf_op jit(solution)/shard_map/ppermute | solution.py:34
  84.5 6.8 %collective-permute-start.19 = (f32[8,13,256]{2,1,0:T(8,128)S(1)}, f32[8,13,256]{2,1,0:T(8,128)S(1)}, u32[]{:S(2)}, u32[]{:S(2)}) collective-permute-start(f32[8,13,256]{2,1,0:T(8,128)S(1)} %get-tuple-element.67.refs_0_.refs_5_), channel_id=1, source_target_pairs={{0,6},{8,14},{32,38},{40,46},{64,70},{72,78},{96,102},{104,110},{1... | collective-permute-start | bytes 319496 | tf_op jit(solution)/shard_map/ppermute | solution.py:34
  91.3 9.7 %collective-permute-start.21 = (f32[8,13,256]{2,1,0:T(8,128)S(1)}, f32[8,13,256]{2,1,0:T(8,128)S(1)}, u32[]{:S(2)}, u32[]{:S(2)}) collective-permute-start(f32[8,13,256]{2,1,0:T(8,128)S(1)} %get-tuple-element.75.refs_0_), channel_id=1, source_target_pairs={{0,16},{8,24},{32,48},{40,56},{64,80},{72,88},{96,112},{104,120},{... | collective-permute-start | bytes 319496 | tf_op jit(solution)/shard_map/ppermute | solution.py:34
  94.3 6.7 %collective-permute-start.22 = (f32[8,13,256]{2,1,0:T(8,128)S(1)}, f32[8,13,256]{2,1,0:T(8,128)S(1)}, u32[]{:S(2)}, u32[]{:S(2)}) collective-permute-start(f32[8,13,256]{2,1,0:T(8,128)S(1)} %get-tuple-element.75.refs_0_), channel_id=1, source_target_pairs={{0,1},{8,9},{32,33},{40,41},{64,65},{72,73},{96,97},{104,105},{1,0... | collective-permute-start | bytes 319496 | tf_op jit(solution)/shard_map/ppermute | solution.py:34
  94.7 6.3 %collective-permute-start.23 = (f32[8,13,256]{2,1,0:T(8,128)S(1)}, f32[8,13,256]{2,1,0:T(8,128)S(1)}, u32[]{:S(2)}, u32[]{:S(2)}) collective-permute-start(f32[8,13,256]{2,1,0:T(8,128)S(1)} %get-tuple-element.75.refs_0_), channel_id=1, source_target_pairs={{0,17},{8,25},{32,49},{40,57},{64,81},{72,89},{96,113},{104,121},{... | collective-permute-start | bytes 319496 | tf_op jit(solution)/shard_map/ppermute | solution.py:34
  96.6 7.8 %collective-permute-start.20 = (f32[256,512]{1,0:T(8,128)S(1)}, f32[256,512]{1,0:T(8,128)S(1)}, u32[]{:S(2)}, u32[]{:S(2)}) collective-permute-start(f32[256,512]{1,0:T(8,128)S(1)} %get-tuple-element.74), channel_id=1, source_target_pairs={{0,8},{8,0},{32,40},{40,32},{64,72},{72,64},{96,104},{104,96},{1,9... | collective-permute-start | bytes 1572872 | tf_op jit(solution)/shard_map/ppermute | solution.py:34
  (4 other events, 22.1 us)

commit v6 on v5

--- a/solution.py
+++ b/solution.py
@@ -247,15 +247,15 @@
         out[...] = term(3)[2 * yr:3 * yr] + term(4)[2 * yr:3 * yr] + piece(4)[...].astype(F32)
 
     def far_body(z, piece, term, out):
-        out[:FIRST, :] = term(5)[yr:, :]
-        out[FIRST:, :] = term(3)[3 * yr:, :]
-
-    far_rows, u4, d4, near, last_own, far_half, t6 = call(
+        out[:FIRST, :] = term(0)[yr:, :]
+        out[FIRST:, :] = term(1)[3 * yr:, :]
+
+    far_half, tf = call("far_rows", [], [gy1, gy2], [t2], [((OWN // 2, COLS), far_body)], cost=1)
+    far_rows, u4, d4, near, last_own, t6 = call(
         "own", [z_rows(MINE, 0, 0), z_rows(MINE, 1, 0), y_rows(UP, 0, 0), y_rows(DOWN, 0, 0), y_rows(MINE, 0, 0)],
-        [c_own, gu2, gd2, gy2, c_rest, gy1], [t2],
+        [c_own, gu2, gd2, gy2, c_rest], [tf],
         [((zr, COLS), own_body(1)), ((yr, COLS), last_side(0, 0, 1)), ((yr, COLS), last_side(1, 1, 2)),
-         ((zr, COLS), own_body(0)), ((yr, COLS), last_own_body),
-         ((OWN // 2, COLS), far_body)])
+         ((zr, COLS), own_body(0)), ((yr, COLS), last_own_body)])
     far_other = swap(far_half, x=1)
     from_core = [swap(far_half, core=1)]
     gu4, gd4 = up(u4), down(d4)

time: 109 us -> 105 us (0.963)
  waiting for transfers between devices: 46.4 us -> 42 us
    ppermute x25, waiting for transfers between devices: 46.4 us -> 42 us  [swap(): return lax.ppermute(value, AXES, pairs)]
    pallas_call x13 -> x14, Pallas kernels: 21.5 us -> 21.6 us  [piece_call(): pl.pallas_call(kernel, in_specs=[pl.BlockSpec(memory_space=pltpu.HBM)] +...]
  transfers between devices with their start and end apart: 25 -> 25, of which waited for: 11 -> 10; matrix products, arithmetic and copies ran while one was open for 1% -> 1% of each run, Pallas kernels for 17% -> 19%
where the time goes in v6:
time: 105 us
  waiting for transfers between devices  42 us (40%)
  starting transfers between devices  35.2 us (34%)
  Pallas kernels  25.4 us (24%)
  other arithmetic  1.48 us (1%)
    ppermute x25, waiting for transfers between devices, swap(): return lax.ppermute(value, AXES, pairs)  42 us
    ppermute x25, starting transfers between devices, swap(): return lax.ppermute(value, AXES, pairs)  35.2 us
    pallas_call x14, Pallas kernels, piece_call(): pl.pallas_call(kernel, in_specs=[pl.BlockSpec(memory_space=pltpu.HBM)] +...  21.6 us
    pallas_call x1, Pallas kernels, update_call(): pl.pallas_call(update_kernel, in_specs=[pl.BlockSpec(memory_space=pltpu.V...  3.82 us
  transfers between devices with their start and end apart: 25, of which 10 were waited for; matrix products, arithmetic and copies ran while one was open for 1% of the time, Pallas kernels for 19%

profile of v6, /device:TPU:1, one launch (start us, length us, event | category | flops | bytes accessed | tf_op | source)
XLA Modules:
  0.0 105.1 jit_solution(5304196765032382044)
XLA Ops:
  3.4 2.1 %widen_b.1 = (f32[640,512]{1,0:T(8,128)S(1)}, f32[640,512]{1,0:T(8,128)S(1)}, f32[768,512]{1,0:T(8,128)S(1)}, f32[640,512]{1,0:T(8,128)S(1)}, f32[1088,512]{1,0:T(8,128)S(1)}, /*index=5*/f32[8,128]{1,0:T(8,128)S(1)}) custom-call(bf16[4,2,2,512,512]{4,3,2,1,0:T(8,128)(2,1)} %bitcast.20, f32[512,512]{1,0:T(8,128)S(1)} %copy-done, ...), custom_call_target="tpu_custom_call" | custom-call | flops 100 | bytes 1 | tf_op jit(solution)/shard_map/widen_b/pallas_call | solution.py:99
  7.9 1.8 %collective-permute-start.4 = (f32[640,256]{1,0:T(8,128)S(1)}, f32[640,256]{1,0:T(8,128)S(1)}, u32[]{:S(2)}, u32[]{:S(2)}) collective-permute-start(f32[640,256]{1,0:T(8,128)S(1)} %get-tuple-element.48), channel_id=1, source_target_pairs={{0,32},{8,40},{32,64},{40,72},{64,96},{72,104},{96,0},{104,8},{1,3... | collective-permute-start | bytes 1966088 | tf_op jit(solution)/shard_map/ppermute | solution.py:34
  9.7 2.2 %collective-permute-start.5 = (f32[640,256]{1,0:T(8,128)S(1)}, f32[640,256]{1,0:T(8,128)S(1)}, u32[]{:S(2)}, u32[]{:S(2)}) collective-permute-start(f32[640,256]{1,0:T(8,128)S(1)} %get-tuple-element.49), channel_id=1, source_target_pairs={{0,96},{8,104},{32,0},{40,8},{64,32},{72,40},{96,64},{104,72},{1,9... | collective-permute-start | bytes 1966088 | tf_op jit(solution)/shard_map/ppermute | solution.py:34
  11.9 2.9 %collective-permute-start.7 = (f32[224,512]{1,0:T(8,128)S(1)}, f32[224,512]{1,0:T(8,128)S(1)}, u32[]{:S(2)}, u32[]{:S(2)}) collective-permute-start(f32[224,512]{1,0:T(8,128)S(1)} %get-tuple-element.51), channel_id=1, source_target_pairs={{0,16},{8,24},{32,48},{40,56},{64,80},{72,88},{96,112},{104,120},{... | collective-permute-start | bytes 1376264 | tf_op jit(solution)/shard_map/ppermute | solution.py:34
  15.8 2.4 %band_table.1 = (bf16[256,4096]{1,0:T(8,128)(2,1)S(1)}, bf16[256,4096]{1,0:T(8,128)(2,1)S(1)}, f32[8,128]{1,0:T(8,128)S(1)}) custom-call(bf16[4,2,2,512,512]{4,3,2,1,0:T(8,128)(2,1)} %bitcast.22, f32[256,64]{1,0:T(8,128)S(1)} %get-tuple-element.91.refs_0_, f32[256,64]{1,0:T(8,128)S(1)} %get-tuple-element.90.refs_1_.refs_4_, ...), custom_call_target="tpu_custom_call" | custom-call | flops 100 | bytes 1 | tf_op jit(solution)/shard_map/band_table/pallas_call | solution.py:99
  18.3 1.8 %crossing.1 = (f32[800,512]{1,0:T(8,128)S(1)}, f32[8,128]{1,0:T(8,128)}) custom-call(bf16[4,2,2,512,512]{4,3,2,1,0:T(8,128)(2,1)} %bitcast.23, f32[768,512]{1,0:T(8,128)S(1)} %collective-permute-done.6.refs_4_.refs_0_, f32[512,512]{1,0:T(8,128)S(1)} %copy-done, f32[8,128]{1,0:T(8,128)S(1)} %get-tuple-element.52.refs_2_), custom_call_target="tpu_custom_call" | custom-call | flops 100 | bytes 1 | tf_op jit(solution)/shard_map/crossing/pallas_call | solution.py:99
  21.2 3.7 %collective-permute-done.7.refs_5_.refs_0_ = f32[224,512]{1,0:T(8,128)S(1)} collective-permute-done((f32[224,512]{1,0:T(8,128)S(1)}, f32[224,512]{1,0:T(8,128)S(1)}, u32[]{:S(2)}, u32[]{:S(2)}) %collective-permute-start.7) | collective-permute-done | bytes 458784 | tf_op jit(solution)/shard_map/ppermute | solution.py:34
  24.9 1.8 %collective-permute-done.4.refs_2_ = f32[640,256]{1,0:T(8,128)S(1)} collective-permute-done((f32[640,256]{1,0:T(8,128)S(1)}, f32[640,256]{1,0:T(8,128)S(1)}, u32[]{:S(2)}, u32[]{:S(2)}) %collective-permute-start.4) | collective-permute-done | bytes 655392 | tf_op jit(solution)/shard_map/ppermute | solution.py:34
  26.7 1.6 %sides.1 = (f32[736,512]{1,0:T(8,128)S(1)}, f32[736,512]{1,0:T(8,128)S(1)}, f32[8,128]{1,0:T(8,128)S(1)}) custom-call(bf16[4,2,2,512,512]{4,3,2,1,0:T(8,128)(2,1)} %bitcast.24, f32[640,512]{1,0:T(8,128)S(1)} %collective-permute-done.1.refs_0_, f32[640,512]{1,0:T(8,128)S(1)} %collective-permute-done.2.refs_1_, f32[640,256]{1,0:T(8,128)S(1)} %collective-permute-done.4.refs_2_, ...), custom_call_target="tpu_custom_call" | custom-call | flops 10000000000 | bytes 100000000 | tf_op jit(solution)/shard_map/sides/pallas_call | solution.py:99
  28.7 2.3 %collective-permute-start.9 = (f32[736,512]{1,0:T(8,128)S(1)}, f32[736,512]{1,0:T(8,128)S(1)}, u32[]{:S(2)}, u32[]{:S(2)}) collective-permute-start(f32[736,512]{1,0:T(8,128)S(1)} %get-tuple-element.55), channel_id=1, source_target_pairs={{0,96},{8,104},{32,0},{40,8},{64,32},{72,40},{96,64},{104,72},{1,9... | collective-permute-start | bytes 4521992 | tf_op jit(solution)/shard_map/ppermute | solution.py:34
  32.5 28.0 %collective-permute-done.10.refs_1_.refs_3_ = f32[800,512]{1,0:T(8,128)S(1)} collective-permute-done((f32[800,512]{1,0:T(8,128)S(1)}, f32[800,512]{1,0:T(8,128)S(1)}, u32[]{:S(2)}, u32[]{:S(2)}) %collective-permute-start.10) | collective-permute-done | bytes 1638432 | tf_op jit(solution)/shard_map/ppermute | solution.py:34
  63.2 1.8 %own.1 = (f32[320,512]{1,0:T(8,128)S(1)}, f32[192,512]{1,0:T(8,128)S(1)}, f32[192,512]{1,0:T(8,128)S(1)}, f32[320,512]{1,0:T(8,128)S(1)}, f32[192,512]{1,0:T(8,128)S(1)}, /*index=5*/f32[8,128]{1,0:T(8,128)S(1)}) custom-call(bf16[4,2,2,512,512]{4,3,2,1,0:T(8,128)(2,1)} %bitcast.26, f32[640,512]{1,0:T(8,128)S(1)} %collective-permute-done.refs_0_, ...), custom_call_target="tpu_custom_call" | custom-call | flops 100 | bytes 1 | tf_op jit(solution)/shard_map/own/pallas_call | solution.py:99
  65.1 2.7 %collective-permute-start.14 = (f32[192,512]{1,0:T(8,128)S(1)}, f32[192,512]{1,0:T(8,128)S(1)}, u32[]{:S(2)}, u32[]{:S(2)}) collective-permute-start(f32[192,512]{1,0:T(8,128)S(1)} %get-tuple-element.66), channel_id=1, source_target_pairs={{0,96},{8,104},{32,0},{40,8},{64,32},{72,40},{96,64},{104,72},{1,9... | collective-permute-start | bytes 1179656 | tf_op jit(solution)/shard_map/ppermute | solution.py:34
  68.3 3.0 %partial_encode.1 = (f32[8,10,256]{2,1,0:T(8,128)S(1)}, f32[320,512]{1,0:T(8,128)S(1)}, f32[8,128]{1,0:T(8,128)}) custom-call(bf16[4,2,2,512,512]{4,3,2,1,0:T(8,128)(2,1)} %bitcast.27, f32[320,512]{1,0:T(8,128)S(1)} %get-tuple-element.60.refs_0_, f32[320,512]{1,0:T(8,128)S(1)} %get-tuple-element.61.refs_1_, f32[512,512]{1,0:T(8,128)S(1)} %bitcast.11, ...), custom_call_target="tpu_custom_call" | custom-call | flops 100 | bytes 1 | tf_op jit(solution)/shard_map/partial_encode/pallas_call | solution.py:99
  71.3 3.0 %collective-permute-start.12 = (f32[320,512]{1,0:T(8,128)S(1)}, f32[320,512]{1,0:T(8,128)S(1)}, u32[]{:S(2)}, u32[]{:S(2)}) collective-permute-start(f32[320,512]{1,0:T(8,128)S(1)} %get-tuple-element.63), channel_id=1, source_target_pairs={{0,16},{8,24},{32,48},{40,56},{64,80},{72,88},{96,112},{104,120},{... | collective-permute-start | bytes 1966088 | tf_op jit(solution)/shard_map/ppermute | solution.py:34
  75.1 1.6 %last_momentum.1 = (f32[192,512]{1,0:T(8,128)S(1)}, f32[8,13,256]{2,1,0:T(8,128)S(1)}, f32[8,128]{1,0:T(8,128)}) custom-call(bf16[4,2,2,512,512]{4,3,2,1,0:T(8,128)(2,1)} %bitcast.28, f32[192,512]{1,0:T(8,128)S(1)} %get-tuple-element.64.refs_0_, f32[192,512]{1,0:T(8,128)S(1)} %collective-permute-done.13.refs_1_, ...), custom_call_target="tpu_custom_call" | custom-call | flops 400000000 | bytes 4000000 | tf_op jit(solution)/shard_map/last_momentum/pallas_call | solution.py:99
  76.7 2.8 %collective-permute-start.17 = (f32[8,13,256]{2,1,0:T(8,128)S(1)}, f32[8,13,256]{2,1,0:T(8,128)S(1)}, u32[]{:S(2)}, u32[]{:S(2)}) collective-permute-start(f32[8,13,256]{2,1,0:T(8,128)S(1)} %get-tuple-element.69.refs_0_.refs_5_), channel_id=1, source_target_pairs={{0,4},{8,12},{32,36},{40,44},{64,68},{72,76},{96,100},{104,108},{1... | collective-permute-start | bytes 319496 | tf_op jit(solution)/shard_map/ppermute | solution.py:34
  80.4 2.0 %collective-permute-done.17.refs_1_ = f32[8,13,256]{2,1,0:T(8,128)S(1)} collective-permute-done((f32[8,13,256]{2,1,0:T(8,128)S(1)}, f32[8,13,256]{2,1,0:T(8,128)S(1)}, u32[]{:S(2)}, u32[]{:S(2)}) %collective-permute-start.17) | collective-permute-done | bytes 106528 | tf_op jit(solution)/shard_map/ppermute | solution.py:34
  83.9 2.7 %collective-permute-done.19.refs_3_ = f32[8,13,256]{2,1,0:T(8,128)S(1)} collective-permute-done((f32[8,13,256]{2,1,0:T(8,128)S(1)}, f32[8,13,256]{2,1,0:T(8,128)S(1)}, u32[]{:S(2)}, u32[]{:S(2)}) %collective-permute-start.19) | collective-permute-done | bytes 106528 | tf_op jit(solution)/shard_map/ppermute | solution.py:34
  86.6 2.8 %collective-permute-start.21 = (f32[8,13,256]{2,1,0:T(8,128)S(1)}, f32[8,13,256]{2,1,0:T(8,128)S(1)}, u32[]{:S(2)}, u32[]{:S(2)}) collective-permute-start(f32[8,13,256]{2,1,0:T(8,128)S(1)} %get-tuple-element.77.refs_0_), channel_id=1, source_target_pairs={{0,16},{8,24},{32,48},{40,56},{64,80},{72,88},{96,112},{104,120},{... | collective-permute-start | bytes 319496 | tf_op jit(solution)/shard_map/ppermute | solution.py:34
  91.7 3.5 %collective-permute-start.20 = (f32[256,512]{1,0:T(8,128)S(1)}, f32[256,512]{1,0:T(8,128)S(1)}, u32[]{:S(2)}, u32[]{:S(2)}) collective-permute-start(f32[256,512]{1,0:T(8,128)S(1)} %get-tuple-element.76), channel_id=1, source_target_pairs={{0,8},{8,0},{32,40},{40,32},{64,72},{72,64},{96,104},{104,96},{1,9... | collective-permute-start | bytes 1572872 | tf_op jit(solution)/shard_map/ppermute | solution.py:34
  95.3 2.5 %momentum_residual.1 = (f32[512,512]{1,0:T(8,128)}, f32[8,128]{1,0:T(8,128)S(1)}) custom-call(bf16[4,2,2,512,512]{4,3,2,1,0:T(8,128)(2,1)} %bitcast.31, f32[320,512]{1,0:T(8,128)S(1)} %get-tuple-element.71.refs_0_, f32[192,512]{1,0:T(8,128)S(1)} %get-tuple-element.72.refs_1_, f32[8,8,256]{2,1,0:T(8,128)S(1)} %get-tuple-element.73.refs_2_, ...), custom_call_target="tpu_custom_call" | custom-call | flops 900000000 | bytes 9000000 | tf_op jit(solution)/shard_map/momentum_residual/pallas_call | solution.py:99
  98.4 1.7 %collective-permute-start.24 = (f32[2,8,8,256]{3,2,1,0:T(8,128)S(1)}, f32[2,8,8,256]{3,2,1,0:T(8,128)S(1)}, u32[]{:S(2)}, u32[]{:S(2)}) collective-permute-start(f32[2,8,8,256]{3,2,1,0:T(8,128)S(1)} %get-tuple-element.79.pair_ref), channel_id=1, source_target_pairs={{0,8},{8,0},{32,40},{40,32},{64,72},{72,64},{96,104},{104,96},{1,9... | collective-permute-start | bytes 393224 | tf_op jit(solution)/shard_map/ppermute | solution.py:34
  101.1 3.8 %parameter_update.1 = f32[4,8,64,512]{3,2,1,0:T(8,128)} custom-call(f32[8,64,512]{2,1,0:T(8,128)S(1)} %bitcast.10, f32[4,64,512]{2,1,0:T(8,128)S(1)} %bitcast.17, f32[4,64,512]{2,1,0:T(8,128)S(1)} %bitcast.15, f32[17,64,512]{2,1,0:T(8,128)S(1)} %bitcast.14, f32[4,64,512]{2,1,0:T(8,128)S(1)} %bitcast.16, f32[4,64,512]{2,1,0:T(8,128)S(1)} %bitcast.18, ...), custom_call_target="tpu_custom_call" | custom-call | tf_op jit(solution)/shard_map/parameter_update/pallas_call | solution.py:427
  (51 shorter events, 19.5 us)
Async XLA Ops:
  1.9 4.7 %collective-permute-start.3 = (f32[832,512]{1,0:T(8,128)S(1)}, f32[832,512]{1,0:T(8,128)S(1)}, u32[]{:S(2)}, u32[]{:S(2)}) collective-permute-start(f32[832,512]{1,0:T(8,128)S(1)} %get-tuple-element.46), channel_id=1, source_target_pairs={{0,8},{8,0},{32,40},{40,32},{64,72},{72,64},{96,104},{104,96},{1,9... | collective-permute-start | bytes 5111816 | tf_op jit(solution)/shard_map/ppermute | solution.py:34
  5.5 6.4 %collective-permute-start.6 = (f32[768,512]{1,0:T(8,128)S(1)}, f32[768,512]{1,0:T(8,128)S(1)}, u32[]{:S(2)}, u32[]{:S(2)}) collective-permute-start(f32[768,512]{1,0:T(8,128)S(1)} %get-tuple-element.50), channel_id=1, source_target_pairs={{0,8},{8,0},{32,40},{40,32},{64,72},{72,64},{96,104},{104,96},{1,9... | collective-permute-start | bytes 4718600 | tf_op jit(solution)/shard_map/ppermute | solution.py:34
  5.7 14.4 %collective-permute-start.1 = (f32[640,512]{1,0:T(8,128)S(1)}, f32[640,512]{1,0:T(8,128)S(1)}, u32[]{:S(2)}, u32[]{:S(2)}) collective-permute-start(f32[640,512]{1,0:T(8,128)S(1)} %get-tuple-element.44), channel_id=1, source_target_pairs={{0,8},{8,0},{32,40},{40,32},{64,72},{72,64},{96,104},{104,96},{1,9... | collective-permute-start | bytes 3932168 | tf_op jit(solution)/shard_map/ppermute | solution.py:34
  6.1 15.0 %collective-permute-start.2 = (f32[640,512]{1,0:T(8,128)S(1)}, f32[640,512]{1,0:T(8,128)S(1)}, u32[]{:S(2)}, u32[]{:S(2)}) collective-permute-start(f32[640,512]{1,0:T(8,128)S(1)} %get-tuple-element.45), channel_id=1, source_target_pairs={{0,8},{8,0},{32,40},{40,32},{64,72},{72,64},{96,104},{104,96},{1,9... | collective-permute-start | bytes 3932168 | tf_op jit(solution)/shard_map/ppermute | solution.py:34
  7.9 18.7 %collective-permute-start.4 = (f32[640,256]{1,0:T(8,128)S(1)}, f32[640,256]{1,0:T(8,128)S(1)}, u32[]{:S(2)}, u32[]{:S(2)}) collective-permute-start(f32[640,256]{1,0:T(8,128)S(1)} %get-tuple-element.48), channel_id=1, source_target_pairs={{0,32},{8,40},{32,64},{40,72},{64,96},{72,104},{96,0},{104,8},{1,3... | collective-permute-start | bytes 1966088 | tf_op jit(solution)/shard_map/ppermute | solution.py:34
  9.7 16.9 %collective-permute-start.5 = (f32[640,256]{1,0:T(8,128)S(1)}, f32[640,256]{1,0:T(8,128)S(1)}, u32[]{:S(2)}, u32[]{:S(2)}) collective-permute-start(f32[640,256]{1,0:T(8,128)S(1)} %get-tuple-element.49), channel_id=1, source_target_pairs={{0,96},{8,104},{32,0},{40,8},{64,32},{72,40},{96,64},{104,72},{1,9... | collective-permute-start | bytes 1966088 | tf_op jit(solution)/shard_map/ppermute | solution.py:34
  11.9 12.9 %collective-permute-start.7 = (f32[224,512]{1,0:T(8,128)S(1)}, f32[224,512]{1,0:T(8,128)S(1)}, u32[]{:S(2)}, u32[]{:S(2)}) collective-permute-start(f32[224,512]{1,0:T(8,128)S(1)} %get-tuple-element.51), channel_id=1, source_target_pairs={{0,16},{8,24},{32,48},{40,56},{64,80},{72,88},{96,112},{104,120},{... | collective-permute-start | bytes 1376264 | tf_op jit(solution)/shard_map/ppermute | solution.py:34
  20.1 43.0 %collective-permute-start.11 = (f32[1088,512]{1,0:T(8,128)S(1)}, f32[1088,512]{1,0:T(8,128)S(1)}, u32[]{:S(2)}, u32[]{:S(2)}) collective-permute-start(f32[1088,512]{1,0:T(8,128)S(1)} %get-tuple-element.57), channel_id=1, source_target_pairs={{0,8},{8,0},{32,40},{40,32},{64,72},{72,64},{96,104},{104,96},{1,9... | collective-permute-start | bytes 6684680 | tf_op jit(solution)/shard_map/ppermute | solution.py:34
  21.1 39.4 %collective-permute-start.10 = (f32[800,512]{1,0:T(8,128)S(1)}, f32[800,512]{1,0:T(8,128)S(1)}, u32[]{:S(2)}, u32[]{:S(2)}) collective-permute-start(f32[800,512]{1,0:T(8,128)S(1)} %get-tuple-element.56), channel_id=1, source_target_pairs={{0,16},{8,24},{32,48},{40,56},{64,80},{72,88},{96,112},{104,120},{... | collective-permute-start | bytes 4915208 | tf_op jit(solution)/shard_map/ppermute | solution.py:34
  28.3 34.9 %collective-permute-start.8 = (f32[736,512]{1,0:T(8,128)S(1)}, f32[736,512]{1,0:T(8,128)S(1)}, u32[]{:S(2)}, u32[]{:S(2)}) collective-permute-start(f32[736,512]{1,0:T(8,128)S(1)} %get-tuple-element.54), channel_id=1, source_target_pairs={{0,32},{8,40},{32,64},{40,72},{64,96},{72,104},{96,0},{104,8},{1,3... | collective-permute-start | bytes 4521992 | tf_op jit(solution)/shard_map/ppermute | solution.py:34
  28.7 34.5 %collective-permute-start.9 = (f32[736,512]{1,0:T(8,128)S(1)}, f32[736,512]{1,0:T(8,128)S(1)}, u32[]{:S(2)}, u32[]{:S(2)}) collective-permute-start(f32[736,512]{1,0:T(8,128)S(1)} %get-tuple-element.55), channel_id=1, source_target_pairs={{0,96},{8,104},{32,0},{40,8},{64,32},{72,40},{96,64},{104,72},{1,9... | collective-permute-start | bytes 4521992 | tf_op jit(solution)/shard_map/ppermute | solution.py:34
  31.0 30.8 %collective-permute-start = (f32[640,512]{1,0:T(8,128)S(1)}, f32[640,512]{1,0:T(8,128)S(1)}, u32[]{:S(2)}, u32[]{:S(2)}) collective-permute-start(f32[640,512]{1,0:T(8,128)S(1)} %get-tuple-element.43), channel_id=1, source_target_pairs={{0,8},{8,0},{32,40},{40,32},{64,72},{72,64},{96,104},{104,96},{1,9... | collective-permute-start | bytes 3932168 | tf_op jit(solution)/shard_map/ppermute | solution.py:34
  60.5 13.8 %collective-permute-start.15 = (f32[256,512]{1,0:T(8,128)S(1)}, f32[256,512]{1,0:T(8,128)S(1)}, u32[]{:S(2)}, u32[]{:S(2)}) collective-permute-start(f32[256,512]{1,0:T(8,128)S(1)} %get-tuple-element.68), channel_id=1, source_target_pairs={{0,2},{8,10},{32,34},{40,42},{64,66},{72,74},{96,98},{104,106},{1,... | collective-permute-start | bytes 1572872 | tf_op jit(solution)/shard_map/ppermute | solution.py:34
  61.8 12.5 %collective-permute-start.16 = (f32[256,512]{1,0:T(8,128)S(1)}, f32[256,512]{1,0:T(8,128)S(1)}, u32[]{:S(2)}, u32[]{:S(2)}) collective-permute-start(f32[256,512]{1,0:T(8,128)S(1)} %get-tuple-element.68), channel_id=1, source_target_pairs={{0,8},{8,0},{32,40},{40,32},{64,72},{72,64},{96,104},{104,96},{1,9... | collective-permute-start | bytes 1572872 | tf_op jit(solution)/shard_map/ppermute | solution.py:34
  65.0 10.1 %collective-permute-start.13 = (f32[192,512]{1,0:T(8,128)S(1)}, f32[192,512]{1,0:T(8,128)S(1)}, u32[]{:S(2)}, u32[]{:S(2)}) collective-permute-start(f32[192,512]{1,0:T(8,128)S(1)} %get-tuple-element.65), channel_id=1, source_target_pairs={{0,32},{8,40},{32,64},{40,72},{64,96},{72,104},{96,0},{104,8},{1,3... | collective-permute-start | bytes 1179656 | tf_op jit(solution)/shard_map/ppermute | solution.py:34
  65.1 10.0 %collective-permute-start.14 = (f32[192,512]{1,0:T(8,128)S(1)}, f32[192,512]{1,0:T(8,128)S(1)}, u32[]{:S(2)}, u32[]{:S(2)}) collective-permute-start(f32[192,512]{1,0:T(8,128)S(1)} %get-tuple-element.66), channel_id=1, source_target_pairs={{0,96},{8,104},{32,0},{40,8},{64,32},{72,40},{96,64},{104,72},{1,9... | collective-permute-start | bytes 1179656 | tf_op jit(solution)/shard_map/ppermute | solution.py:34
  71.3 18.9 %collective-permute-start.12 = (f32[320,512]{1,0:T(8,128)S(1)}, f32[320,512]{1,0:T(8,128)S(1)}, u32[]{:S(2)}, u32[]{:S(2)}) collective-permute-start(f32[320,512]{1,0:T(8,128)S(1)} %get-tuple-element.63), channel_id=1, source_target_pairs={{0,16},{8,24},{32,48},{40,56},{64,80},{72,88},{96,112},{104,120},{... | collective-permute-start | bytes 1966088 | tf_op jit(solution)/shard_map/ppermute | solution.py:34
  76.7 5.7 %collective-permute-start.17 = (f32[8,13,256]{2,1,0:T(8,128)S(1)}, f32[8,13,256]{2,1,0:T(8,128)S(1)}, u32[]{:S(2)}, u32[]{:S(2)}) collective-permute-start(f32[8,13,256]{2,1,0:T(8,128)S(1)} %get-tuple-element.69.refs_0_.refs_5_), channel_id=1, source_target_pairs={{0,4},{8,12},{32,36},{40,44},{64,68},{72,76},{96,100},{104,108},{1... | collective-permute-start | bytes 319496 | tf_op jit(solution)/shard_map/ppermute | solution.py:34
  79.6 4.4 %collective-permute-start.18 = (f32[8,13,256]{2,1,0:T(8,128)S(1)}, f32[8,13,256]{2,1,0:T(8,128)S(1)}, u32[]{:S(2)}, u32[]{:S(2)}) collective-permute-start(f32[8,13,256]{2,1,0:T(8,128)S(1)} %get-tuple-element.69.refs_0_.refs_5_), channel_id=1, source_target_pairs={{0,2},{8,10},{32,34},{40,42},{64,66},{72,74},{96,98},{104,106},{1,... | collective-permute-start | bytes 319496 | tf_op jit(solution)/shard_map/ppermute | solution.py:34
  79.9 6.7 %collective-permute-start.19 = (f32[8,13,256]{2,1,0:T(8,128)S(1)}, f32[8,13,256]{2,1,0:T(8,128)S(1)}, u32[]{:S(2)}, u32[]{:S(2)}) collective-permute-start(f32[8,13,256]{2,1,0:T(8,128)S(1)} %get-tuple-element.69.refs_0_.refs_5_), channel_id=1, source_target_pairs={{0,6},{8,14},{32,38},{40,46},{64,70},{72,78},{96,102},{104,110},{1... | collective-permute-start | bytes 319496 | tf_op jit(solution)/shard_map/ppermute | solution.py:34
  86.6 11.1 %collective-permute-start.21 = (f32[8,13,256]{2,1,0:T(8,128)S(1)}, f32[8,13,256]{2,1,0:T(8,128)S(1)}, u32[]{:S(2)}, u32[]{:S(2)}) collective-permute-start(f32[8,13,256]{2,1,0:T(8,128)S(1)} %get-tuple-element.77.refs_0_), channel_id=1, source_target_pairs={{0,16},{8,24},{32,48},{40,56},{64,80},{72,88},{96,112},{104,120},{... | collective-permute-start | bytes 319496 | tf_op jit(solution)/shard_map/ppermute | solution.py:34
  89.5 8.3 %collective-permute-start.22 = (f32[8,13,256]{2,1,0:T(8,128)S(1)}, f32[8,13,256]{2,1,0:T(8,128)S(1)}, u32[]{:S(2)}, u32[]{:S(2)}) collective-permute-start(f32[8,13,256]{2,1,0:T(8,128)S(1)} %get-tuple-element.77.refs_0_), channel_id=1, source_target_pairs={{0,1},{8,9},{32,33},{40,41},{64,65},{72,73},{96,97},{104,105},{1,0... | collective-permute-start | bytes 319496 | tf_op jit(solution)/shard_map/ppermute | solution.py:34
  90.0 7.7 %collective-permute-start.23 = (f32[8,13,256]{2,1,0:T(8,128)S(1)}, f32[8,13,256]{2,1,0:T(8,128)S(1)}, u32[]{:S(2)}, u32[]{:S(2)}) collective-permute-start(f32[8,13,256]{2,1,0:T(8,128)S(1)} %get-tuple-element.77.refs_0_), channel_id=1, source_target_pairs={{0,17},{8,25},{32,49},{40,57},{64,81},{72,89},{96,113},{104,121},{... | collective-permute-start | bytes 319496 | tf_op jit(solution)/shard_map/ppermute | solution.py:34
  91.7 9.4 %collective-permute-start.20 = (f32[256,512]{1,0:T(8,128)S(1)}, f32[256,512]{1,0:T(8,128)S(1)}, u32[]{:S(2)}, u32[]{:S(2)}) collective-permute-start(f32[256,512]{1,0:T(8,128)S(1)} %get-tuple-element.76), channel_id=1, source_target_pairs={{0,8},{8,0},{32,40},{40,32},{64,72},{72,64},{96,104},{104,96},{1,9... | collective-permute-start | bytes 1572872 | tf_op jit(solution)/shard_map/ppermute | solution.py:34
  (4 other events, 18.8 us)

commit v7 on v6

--- a/solution.py
+++ b/solution.py
@@ -408,16 +408,13 @@
             for k in range(4):
                 n = nblock // len(rows[k])
                 for i, ref in enumerate(rows[k]):
-                    cut = slice(i * n, (i + 1) * n)
-                    field[k, cut, at, out_cols] = ref[:, at, out_cols] - turned[k * nblock + i * n:k * nblock + (i + 1) * n]
+                    to = pl.ds(part * ((odd + i) % 2), part) if k >= 2 else slice(None)
+                    field[k, to, at, out_cols] = ref[:, at, out_cols] - turned[k * nblock + i * n:k * nblock + (i + 1) * n]
         for k in range(4):
-            for i in range(2):
-                to = (part * i if k < 2 else part * ((odd + i) % 2))
-                store = pltpu.make_async_copy(field.at[k, pl.ds(i * part, part), pl.ds(c * step, step), :],
-                                              out_ref.at[dp ^ k, pl.ds(to, part), pl.ds(c * step, step), :],
-                                              sems.at[(c * 4 + k) * 2 + i])
-                store.start()
-                stores.append(store)
+            store = pltpu.make_async_copy(field.at[k, :, pl.ds(c * step, step), :],
+                                          out_ref.at[dp ^ k, :, pl.ds(c * step, step), :], sems.at[c * 4 + k])
+            store.start()
+            stores.append(store)
     for store in stores:
         store.wait()
 
@@ -432,7 +429,7 @@
         scratch_shapes=[
             pltpu.VMEM((NB, 4, OWN // GROUP, BAND), F32),
             pltpu.VMEM((4, OWN // GROUP, GROUP, COLS), F32),
-            pltpu.SemaphoreType.DMA((8 * GROUP // 8,)),
+            pltpu.SemaphoreType.DMA((4 * GROUP // 8,)),
         ],
         compiler_params=pltpu.CompilerParams(vmem_limit_bytes=24 * 2**20),
         name="parameter_update",

time: 105 us -> 105 us (level)
  no operation moved by 1% of the time
where the time goes in v7:
time: 105 us
  waiting for transfers between devices  42 us (40%)
  starting transfers between devices  35.2 us (34%)
  Pallas kernels  25.1 us (24%)
  other arithmetic  1.48 us (1%)
    ppermute x25, waiting for transfers between devices, swap(): return lax.ppermute(value, AXES, pairs)  42 us
    ppermute x25, starting transfers between devices, swap(): return lax.ppermute(value, AXES, pairs)  35.2 us
    pallas_call x14, Pallas kernels, piece_call(): pl.pallas_call(kernel, in_specs=[pl.BlockSpec(memory_space=pltpu.HBM)] +...  21.6 us
    pallas_call x1, Pallas kernels, update_call(): pl.pallas_call(update_kernel, in_specs=[pl.BlockSpec(memory_space=pltpu.V...  3.49 us
  transfers between devices with their start and end apart: 25, of which 10 were waited for; matrix products, arithmetic and copies ran while one was open for 1% of the time, Pallas kernels for 19%

profile of v7, /device:TPU:1, one launch (start us, length us, event | category | flops | bytes accessed | tf_op | source)
XLA Modules:
  0.0 104.8 jit_solution(8716373436471448384)
XLA Ops:
  3.4 2.1 %widen_b.1 = (f32[640,512]{1,0:T(8,128)S(1)}, f32[640,512]{1,0:T(8,128)S(1)}, f32[768,512]{1,0:T(8,128)S(1)}, f32[640,512]{1,0:T(8,128)S(1)}, f32[1088,512]{1,0:T(8,128)S(1)}, /*index=5*/f32[8,128]{1,0:T(8,128)S(1)}) custom-call(bf16[4,2,2,512,512]{4,3,2,1,0:T(8,128)(2,1)} %bitcast.20, f32[512,512]{1,0:T(8,128)S(1)} %copy-done, ...), custom_call_target="tpu_custom_call" | custom-call | flops 100 | bytes 1 | tf_op jit(solution)/shard_map/widen_b/pallas_call | solution.py:99
  7.9 1.8 %collective-permute-start.4 = (f32[640,256]{1,0:T(8,128)S(1)}, f32[640,256]{1,0:T(8,128)S(1)}, u32[]{:S(2)}, u32[]{:S(2)}) collective-permute-start(f32[640,256]{1,0:T(8,128)S(1)} %get-tuple-element.48), channel_id=1, source_target_pairs={{0,32},{8,40},{32,64},{40,72},{64,96},{72,104},{96,0},{104,8},{1,3... | collective-permute-start | bytes 1966088 | tf_op jit(solution)/shard_map/ppermute | solution.py:34
  9.7 2.2 %collective-permute-start.5 = (f32[640,256]{1,0:T(8,128)S(1)}, f32[640,256]{1,0:T(8,128)S(1)}, u32[]{:S(2)}, u32[]{:S(2)}) collective-permute-start(f32[640,256]{1,0:T(8,128)S(1)} %get-tuple-element.49), channel_id=1, source_target_pairs={{0,96},{8,104},{32,0},{40,8},{64,32},{72,40},{96,64},{104,72},{1,9... | collective-permute-start | bytes 1966088 | tf_op jit(solution)/shard_map/ppermute | solution.py:34
  11.9 2.9 %collective-permute-start.7 = (f32[224,512]{1,0:T(8,128)S(1)}, f32[224,512]{1,0:T(8,128)S(1)}, u32[]{:S(2)}, u32[]{:S(2)}) collective-permute-start(f32[224,512]{1,0:T(8,128)S(1)} %get-tuple-element.51), channel_id=1, source_target_pairs={{0,16},{8,24},{32,48},{40,56},{64,80},{72,88},{96,112},{104,120},{... | collective-permute-start | bytes 1376264 | tf_op jit(solution)/shard_map/ppermute | solution.py:34
  15.8 2.4 %band_table.1 = (bf16[256,4096]{1,0:T(8,128)(2,1)S(1)}, bf16[256,4096]{1,0:T(8,128)(2,1)S(1)}, f32[8,128]{1,0:T(8,128)S(1)}) custom-call(bf16[4,2,2,512,512]{4,3,2,1,0:T(8,128)(2,1)} %bitcast.22, f32[256,64]{1,0:T(8,128)S(1)} %get-tuple-element.91.refs_0_, f32[256,64]{1,0:T(8,128)S(1)} %get-tuple-element.90.refs_1_.refs_4_, ...), custom_call_target="tpu_custom_call" | custom-call | flops 100 | bytes 1 | tf_op jit(solution)/shard_map/band_table/pallas_call | solution.py:99
  18.3 1.8 %crossing.1 = (f32[800,512]{1,0:T(8,128)S(1)}, f32[8,128]{1,0:T(8,128)}) custom-call(bf16[4,2,2,512,512]{4,3,2,1,0:T(8,128)(2,1)} %bitcast.23, f32[768,512]{1,0:T(8,128)S(1)} %collective-permute-done.6.refs_4_.refs_0_, f32[512,512]{1,0:T(8,128)S(1)} %copy-done, f32[8,128]{1,0:T(8,128)S(1)} %get-tuple-element.52.refs_2_), custom_call_target="tpu_custom_call" | custom-call | flops 100 | bytes 1 | tf_op jit(solution)/shard_map/crossing/pallas_call | solution.py:99
  21.2 3.7 %collective-permute-done.7.refs_5_.refs_0_ = f32[224,512]{1,0:T(8,128)S(1)} collective-permute-done((f32[224,512]{1,0:T(8,128)S(1)}, f32[224,512]{1,0:T(8,128)S(1)}, u32[]{:S(2)}, u32[]{:S(2)}) %collective-permute-start.7) | collective-permute-done | bytes 458784 | tf_op jit(solution)/shard_map/ppermute | solution.py:34
  24.9 1.8 %collective-permute-done.4.refs_2_ = f32[640,256]{1,0:T(8,128)S(1)} collective-permute-done((f32[640,256]{1,0:T(8,128)S(1)}, f32[640,256]{1,0:T(8,128)S(1)}, u32[]{:S(2)}, u32[]{:S(2)}) %collective-permute-start.4) | collective-permute-done | bytes 655392 | tf_op jit(solution)/shard_map/ppermute | solution.py:34
  26.7 1.6 %sides.1 = (f32[736,512]{1,0:T(8,128)S(1)}, f32[736,512]{1,0:T(8,128)S(1)}, f32[8,128]{1,0:T(8,128)S(1)}) custom-call(bf16[4,2,2,512,512]{4,3,2,1,0:T(8,128)(2,1)} %bitcast.24, f32[640,512]{1,0:T(8,128)S(1)} %collective-permute-done.1.refs_0_, f32[640,512]{1,0:T(8,128)S(1)} %collective-permute-done.2.refs_1_, f32[640,256]{1,0:T(8,128)S(1)} %collective-permute-done.4.refs_2_, ...), custom_call_target="tpu_custom_call" | custom-call | flops 10000000000 | bytes 100000000 | tf_op jit(solution)/shard_map/sides/pallas_call | solution.py:99
  28.7 2.3 %collective-permute-start.9 = (f32[736,512]{1,0:T(8,128)S(1)}, f32[736,512]{1,0:T(8,128)S(1)}, u32[]{:S(2)}, u32[]{:S(2)}) collective-permute-start(f32[736,512]{1,0:T(8,128)S(1)} %get-tuple-element.55), channel_id=1, source_target_pairs={{0,96},{8,104},{32,0},{40,8},{64,32},{72,40},{96,64},{104,72},{1,9... | collective-permute-start | bytes 4521992 | tf_op jit(solution)/shard_map/ppermute | solution.py:34
  32.5 28.0 %collective-permute-done.10.refs_1_.refs_3_ = f32[800,512]{1,0:T(8,128)S(1)} collective-permute-done((f32[800,512]{1,0:T(8,128)S(1)}, f32[800,512]{1,0:T(8,128)S(1)}, u32[]{:S(2)}, u32[]{:S(2)}) %collective-permute-start.10) | collective-permute-done | bytes 1638432 | tf_op jit(solution)/shard_map/ppermute | solution.py:34
  63.2 1.8 %own.1 = (f32[320,512]{1,0:T(8,128)S(1)}, f32[192,512]{1,0:T(8,128)S(1)}, f32[192,512]{1,0:T(8,128)S(1)}, f32[320,512]{1,0:T(8,128)S(1)}, f32[192,512]{1,0:T(8,128)S(1)}, /*index=5*/f32[8,128]{1,0:T(8,128)S(1)}) custom-call(bf16[4,2,2,512,512]{4,3,2,1,0:T(8,128)(2,1)} %bitcast.26, f32[640,512]{1,0:T(8,128)S(1)} %collective-permute-done.refs_0_, ...), custom_call_target="tpu_custom_call" | custom-call | flops 100 | bytes 1 | tf_op jit(solution)/shard_map/own/pallas_call | solution.py:99
  65.1 2.7 %collective-permute-start.14 = (f32[192,512]{1,0:T(8,128)S(1)}, f32[192,512]{1,0:T(8,128)S(1)}, u32[]{:S(2)}, u32[]{:S(2)}) collective-permute-start(f32[192,512]{1,0:T(8,128)S(1)} %get-tuple-element.66), channel_id=1, source_target_pairs={{0,96},{8,104},{32,0},{40,8},{64,32},{72,40},{96,64},{104,72},{1,9... | collective-permute-start | bytes 1179656 | tf_op jit(solution)/shard_map/ppermute | solution.py:34
  68.3 3.0 %partial_encode.1 = (f32[8,10,256]{2,1,0:T(8,128)S(1)}, f32[320,512]{1,0:T(8,128)S(1)}, f32[8,128]{1,0:T(8,128)}) custom-call(bf16[4,2,2,512,512]{4,3,2,1,0:T(8,128)(2,1)} %bitcast.27, f32[320,512]{1,0:T(8,128)S(1)} %get-tuple-element.60.refs_0_, f32[320,512]{1,0:T(8,128)S(1)} %get-tuple-element.61.refs_1_, f32[512,512]{1,0:T(8,128)S(1)} %bitcast.11, ...), custom_call_target="tpu_custom_call" | custom-call | flops 100 | bytes 1 | tf_op jit(solution)/shard_map/partial_encode/pallas_call | solution.py:99
  71.3 3.0 %collective-permute-start.12 = (f32[320,512]{1,0:T(8,128)S(1)}, f32[320,512]{1,0:T(8,128)S(1)}, u32[]{:S(2)}, u32[]{:S(2)}) collective-permute-start(f32[320,512]{1,0:T(8,128)S(1)} %get-tuple-element.63), channel_id=1, source_target_pairs={{0,16},{8,24},{32,48},{40,56},{64,80},{72,88},{96,112},{104,120},{... | collective-permute-start | bytes 1966088 | tf_op jit(solution)/shard_map/ppermute | solution.py:34
  75.1 1.6 %last_momentum.1 = (f32[192,512]{1,0:T(8,128)S(1)}, f32[8,13,256]{2,1,0:T(8,128)S(1)}, f32[8,128]{1,0:T(8,128)}) custom-call(bf16[4,2,2,512,512]{4,3,2,1,0:T(8,128)(2,1)} %bitcast.28, f32[192,512]{1,0:T(8,128)S(1)} %get-tuple-element.64.refs_0_, f32[192,512]{1,0:T(8,128)S(1)} %collective-permute-done.13.refs_1_, ...), custom_call_target="tpu_custom_call" | custom-call | flops 400000000 | bytes 4000000 | tf_op jit(solution)/shard_map/last_momentum/pallas_call | solution.py:99
  76.7 2.8 %collective-permute-start.17 = (f32[8,13,256]{2,1,0:T(8,128)S(1)}, f32[8,13,256]{2,1,0:T(8,128)S(1)}, u32[]{:S(2)}, u32[]{:S(2)}) collective-permute-start(f32[8,13,256]{2,1,0:T(8,128)S(1)} %get-tuple-element.69.refs_0_.refs_5_), channel_id=1, source_target_pairs={{0,4},{8,12},{32,36},{40,44},{64,68},{72,76},{96,100},{104,108},{1... | collective-permute-start | bytes 319496 | tf_op jit(solution)/shard_map/ppermute | solution.py:34
  80.4 2.0 %collective-permute-done.17.refs_1_ = f32[8,13,256]{2,1,0:T(8,128)S(1)} collective-permute-done((f32[8,13,256]{2,1,0:T(8,128)S(1)}, f32[8,13,256]{2,1,0:T(8,128)S(1)}, u32[]{:S(2)}, u32[]{:S(2)}) %collective-permute-start.17) | collective-permute-done | bytes 106528 | tf_op jit(solution)/shard_map/ppermute | solution.py:34
  83.9 2.7 %collective-permute-done.19.refs_3_ = f32[8,13,256]{2,1,0:T(8,128)S(1)} collective-permute-done((f32[8,13,256]{2,1,0:T(8,128)S(1)}, f32[8,13,256]{2,1,0:T(8,128)S(1)}, u32[]{:S(2)}, u32[]{:S(2)}) %collective-permute-start.19) | collective-permute-done | bytes 106528 | tf_op jit(solution)/shard_map/ppermute | solution.py:34
  86.6 2.8 %collective-permute-start.21 = (f32[8,13,256]{2,1,0:T(8,128)S(1)}, f32[8,13,256]{2,1,0:T(8,128)S(1)}, u32[]{:S(2)}, u32[]{:S(2)}) collective-permute-start(f32[8,13,256]{2,1,0:T(8,128)S(1)} %get-tuple-element.77.refs_0_), channel_id=1, source_target_pairs={{0,16},{8,24},{32,48},{40,56},{64,80},{72,88},{96,112},{104,120},{... | collective-permute-start | bytes 319496 | tf_op jit(solution)/shard_map/ppermute | solution.py:34
  91.7 3.5 %collective-permute-start.20 = (f32[256,512]{1,0:T(8,128)S(1)}, f32[256,512]{1,0:T(8,128)S(1)}, u32[]{:S(2)}, u32[]{:S(2)}) collective-permute-start(f32[256,512]{1,0:T(8,128)S(1)} %get-tuple-element.76), channel_id=1, source_target_pairs={{0,8},{8,0},{32,40},{40,32},{64,72},{72,64},{96,104},{104,96},{1,9... | collective-permute-start | bytes 1572872 | tf_op jit(solution)/shard_map/ppermute | solution.py:34
  95.3 2.5 %momentum_residual.1 = (f32[512,512]{1,0:T(8,128)}, f32[8,128]{1,0:T(8,128)S(1)}) custom-call(bf16[4,2,2,512,512]{4,3,2,1,0:T(8,128)(2,1)} %bitcast.31, f32[320,512]{1,0:T(8,128)S(1)} %get-tuple-element.71.refs_0_, f32[192,512]{1,0:T(8,128)S(1)} %get-tuple-element.72.refs_1_, f32[8,8,256]{2,1,0:T(8,128)S(1)} %get-tuple-element.73.refs_2_, ...), custom_call_target="tpu_custom_call" | custom-call | flops 900000000 | bytes 9000000 | tf_op jit(solution)/shard_map/momentum_residual/pallas_call | solution.py:99
  98.4 1.7 %collective-permute-start.24 = (f32[2,8,8,256]{3,2,1,0:T(8,128)S(1)}, f32[2,8,8,256]{3,2,1,0:T(8,128)S(1)}, u32[]{:S(2)}, u32[]{:S(2)}) collective-permute-start(f32[2,8,8,256]{3,2,1,0:T(8,128)S(1)} %get-tuple-element.79.pair_ref), channel_id=1, source_target_pairs={{0,8},{8,0},{32,40},{40,32},{64,72},{72,64},{96,104},{104,96},{1,9... | collective-permute-start | bytes 393224 | tf_op jit(solution)/shard_map/ppermute | solution.py:34
  101.1 3.5 %parameter_update.1 = f32[4,8,64,512]{3,2,1,0:T(8,128)} custom-call(f32[8,64,512]{2,1,0:T(8,128)S(1)} %bitcast.10, f32[4,64,512]{2,1,0:T(8,128)S(1)} %bitcast.17, f32[4,64,512]{2,1,0:T(8,128)S(1)} %bitcast.15, f32[17,64,512]{2,1,0:T(8,128)S(1)} %bitcast.14, f32[4,64,512]{2,1,0:T(8,128)S(1)} %bitcast.16, f32[4,64,512]{2,1,0:T(8,128)S(1)} %bitcast.18, ...), custom_call_target="tpu_custom_call" | custom-call | tf_op jit(solution)/shard_map/parameter_update/pallas_call | solution.py:424
  (51 shorter events, 19.5 us)
Async XLA Ops:
  1.9 4.7 %collective-permute-start.3 = (f32[832,512]{1,0:T(8,128)S(1)}, f32[832,512]{1,0:T(8,128)S(1)}, u32[]{:S(2)}, u32[]{:S(2)}) collective-permute-start(f32[832,512]{1,0:T(8,128)S(1)} %get-tuple-element.46), channel_id=1, source_target_pairs={{0,8},{8,0},{32,40},{40,32},{64,72},{72,64},{96,104},{104,96},{1,9... | collective-permute-start | bytes 5111816 | tf_op jit(solution)/shard_map/ppermute | solution.py:34
  5.5 6.4 %collective-permute-start.6 = (f32[768,512]{1,0:T(8,128)S(1)}, f32[768,512]{1,0:T(8,128)S(1)}, u32[]{:S(2)}, u32[]{:S(2)}) collective-permute-start(f32[768,512]{1,0:T(8,128)S(1)} %get-tuple-element.50), channel_id=1, source_target_pairs={{0,8},{8,0},{32,40},{40,32},{64,72},{72,64},{96,104},{104,96},{1,9... | collective-permute-start | bytes 4718600 | tf_op jit(solution)/shard_map/ppermute | solution.py:34
  5.7 14.4 %collective-permute-start.1 = (f32[640,512]{1,0:T(8,128)S(1)}, f32[640,512]{1,0:T(8,128)S(1)}, u32[]{:S(2)}, u32[]{:S(2)}) collective-permute-start(f32[640,512]{1,0:T(8,128)S(1)} %get-tuple-element.44), channel_id=1, source_target_pairs={{0,8},{8,0},{32,40},{40,32},{64,72},{72,64},{96,104},{104,96},{1,9... | collective-permute-start | bytes 3932168 | tf_op jit(solution)/shard_map/ppermute | solution.py:34
  6.1 15.0 %collective-permute-start.2 = (f32[640,512]{1,0:T(8,128)S(1)}, f32[640,512]{1,0:T(8,128)S(1)}, u32[]{:S(2)}, u32[]{:S(2)}) collective-permute-start(f32[640,512]{1,0:T(8,128)S(1)} %get-tuple-element.45), channel_id=1, source_target_pairs={{0,8},{8,0},{32,40},{40,32},{64,72},{72,64},{96,104},{104,96},{1,9... | collective-permute-start | bytes 3932168 | tf_op jit(solution)/shard_map/ppermute | solution.py:34
  7.9 18.7 %collective-permute-start.4 = (f32[640,256]{1,0:T(8,128)S(1)}, f32[640,256]{1,0:T(8,128)S(1)}, u32[]{:S(2)}, u32[]{:S(2)}) collective-permute-start(f32[640,256]{1,0:T(8,128)S(1)} %get-tuple-element.48), channel_id=1, source_target_pairs={{0,32},{8,40},{32,64},{40,72},{64,96},{72,104},{96,0},{104,8},{1,3... | collective-permute-start | bytes 1966088 | tf_op jit(solution)/shard_map/ppermute | solution.py:34
  9.7 16.9 %collective-permute-start.5 = (f32[640,256]{1,0:T(8,128)S(1)}, f32[640,256]{1,0:T(8,128)S(1)}, u32[]{:S(2)}, u32[]{:S(2)}) collective-permute-start(f32[640,256]{1,0:T(8,128)S(1)} %get-tuple-element.49), channel_id=1, source_target_pairs={{0,96},{8,104},{32,0},{40,8},{64,32},{72,40},{96,64},{104,72},{1,9... | collective-permute-start | bytes 1966088 | tf_op jit(solution)/shard_map/ppermute | solution.py:34
  11.9 12.9 %collective-permute-start.7 = (f32[224,512]{1,0:T(8,128)S(1)}, f32[224,512]{1,0:T(8,128)S(1)}, u32[]{:S(2)}, u32[]{:S(2)}) collective-permute-start(f32[224,512]{1,0:T(8,128)S(1)} %get-tuple-element.51), channel_id=1, source_target_pairs={{0,16},{8,24},{32,48},{40,56},{64,80},{72,88},{96,112},{104,120},{... | collective-permute-start | bytes 1376264 | tf_op jit(solution)/shard_map/ppermute | solution.py:34
  20.1 43.0 %collective-permute-start.11 = (f32[1088,512]{1,0:T(8,128)S(1)}, f32[1088,512]{1,0:T(8,128)S(1)}, u32[]{:S(2)}, u32[]{:S(2)}) collective-permute-start(f32[1088,512]{1,0:T(8,128)S(1)} %get-tuple-element.57), channel_id=1, source_target_pairs={{0,8},{8,0},{32,40},{40,32},{64,72},{72,64},{96,104},{104,96},{1,9... | collective-permute-start | bytes 6684680 | tf_op jit(solution)/shard_map/ppermute | solution.py:34
  21.1 39.4 %collective-permute-start.10 = (f32[800,512]{1,0:T(8,128)S(1)}, f32[800,512]{1,0:T(8,128)S(1)}, u32[]{:S(2)}, u32[]{:S(2)}) collective-permute-start(f32[800,512]{1,0:T(8,128)S(1)} %get-tuple-element.56), channel_id=1, source_target_pairs={{0,16},{8,24},{32,48},{40,56},{64,80},{72,88},{96,112},{104,120},{... | collective-permute-start | bytes 4915208 | tf_op jit(solution)/shard_map/ppermute | solution.py:34
  28.3 34.9 %collective-permute-start.8 = (f32[736,512]{1,0:T(8,128)S(1)}, f32[736,512]{1,0:T(8,128)S(1)}, u32[]{:S(2)}, u32[]{:S(2)}) collective-permute-start(f32[736,512]{1,0:T(8,128)S(1)} %get-tuple-element.54), channel_id=1, source_target_pairs={{0,32},{8,40},{32,64},{40,72},{64,96},{72,104},{96,0},{104,8},{1,3... | collective-permute-start | bytes 4521992 | tf_op jit(solution)/shard_map/ppermute | solution.py:34
  28.7 34.5 %collective-permute-start.9 = (f32[736,512]{1,0:T(8,128)S(1)}, f32[736,512]{1,0:T(8,128)S(1)}, u32[]{:S(2)}, u32[]{:S(2)}) collective-permute-start(f32[736,512]{1,0:T(8,128)S(1)} %get-tuple-element.55), channel_id=1, source_target_pairs={{0,96},{8,104},{32,0},{40,8},{64,32},{72,40},{96,64},{104,72},{1,9... | collective-permute-start | bytes 4521992 | tf_op jit(solution)/shard_map/ppermute | solution.py:34
  31.0 30.8 %collective-permute-start = (f32[640,512]{1,0:T(8,128)S(1)}, f32[640,512]{1,0:T(8,128)S(1)}, u32[]{:S(2)}, u32[]{:S(2)}) collective-permute-start(f32[640,512]{1,0:T(8,128)S(1)} %get-tuple-element.43), channel_id=1, source_target_pairs={{0,8},{8,0},{32,40},{40,32},{64,72},{72,64},{96,104},{104,96},{1,9... | collective-permute-start | bytes 3932168 | tf_op jit(solution)/shard_map/ppermute | solution.py:34
  60.5 13.8 %collective-permute-start.15 = (f32[256,512]{1,0:T(8,128)S(1)}, f32[256,512]{1,0:T(8,128)S(1)}, u32[]{:S(2)}, u32[]{:S(2)}) collective-permute-start(f32[256,512]{1,0:T(8,128)S(1)} %get-tuple-element.68), channel_id=1, source_target_pairs={{0,2},{8,10},{32,34},{40,42},{64,66},{72,74},{96,98},{104,106},{1,... | collective-permute-start | bytes 1572872 | tf_op jit(solution)/shard_map/ppermute | solution.py:34
  61.8 12.5 %collective-permute-start.16 = (f32[256,512]{1,0:T(8,128)S(1)}, f32[256,512]{1,0:T(8,128)S(1)}, u32[]{:S(2)}, u32[]{:S(2)}) collective-permute-start(f32[256,512]{1,0:T(8,128)S(1)} %get-tuple-element.68), channel_id=1, source_target_pairs={{0,8},{8,0},{32,40},{40,32},{64,72},{72,64},{96,104},{104,96},{1,9... | collective-permute-start | bytes 1572872 | tf_op jit(solution)/shard_map/ppermute | solution.py:34
  65.0 10.1 %collective-permute-start.13 = (f32[192,512]{1,0:T(8,128)S(1)}, f32[192,512]{1,0:T(8,128)S(1)}, u32[]{:S(2)}, u32[]{:S(2)}) collective-permute-start(f32[192,512]{1,0:T(8,128)S(1)} %get-tuple-element.65), channel_id=1, source_target_pairs={{0,32},{8,40},{32,64},{40,72},{64,96},{72,104},{96,0},{104,8},{1,3... | collective-permute-start | bytes 1179656 | tf_op jit(solution)/shard_map/ppermute | solution.py:34
  65.1 10.0 %collective-permute-start.14 = (f32[192,512]{1,0:T(8,128)S(1)}, f32[192,512]{1,0:T(8,128)S(1)}, u32[]{:S(2)}, u32[]{:S(2)}) collective-permute-start(f32[192,512]{1,0:T(8,128)S(1)} %get-tuple-element.66), channel_id=1, source_target_pairs={{0,96},{8,104},{32,0},{40,8},{64,32},{72,40},{96,64},{104,72},{1,9... | collective-permute-start | bytes 1179656 | tf_op jit(solution)/shard_map/ppermute | solution.py:34
  71.3 18.9 %collective-permute-start.12 = (f32[320,512]{1,0:T(8,128)S(1)}, f32[320,512]{1,0:T(8,128)S(1)}, u32[]{:S(2)}, u32[]{:S(2)}) collective-permute-start(f32[320,512]{1,0:T(8,128)S(1)} %get-tuple-element.63), channel_id=1, source_target_pairs={{0,16},{8,24},{32,48},{40,56},{64,80},{72,88},{96,112},{104,120},{... | collective-permute-start | bytes 1966088 | tf_op jit(solution)/shard_map/ppermute | solution.py:34
  76.7 5.7 %collective-permute-start.17 = (f32[8,13,256]{2,1,0:T(8,128)S(1)}, f32[8,13,256]{2,1,0:T(8,128)S(1)}, u32[]{:S(2)}, u32[]{:S(2)}) collective-permute-start(f32[8,13,256]{2,1,0:T(8,128)S(1)} %get-tuple-element.69.refs_0_.refs_5_), channel_id=1, source_target_pairs={{0,4},{8,12},{32,36},{40,44},{64,68},{72,76},{96,100},{104,108},{1... | collective-permute-start | bytes 319496 | tf_op jit(solution)/shard_map/ppermute | solution.py:34
  79.6 4.4 %collective-permute-start.18 = (f32[8,13,256]{2,1,0:T(8,128)S(1)}, f32[8,13,256]{2,1,0:T(8,128)S(1)}, u32[]{:S(2)}, u32[]{:S(2)}) collective-permute-start(f32[8,13,256]{2,1,0:T(8,128)S(1)} %get-tuple-element.69.refs_0_.refs_5_), channel_id=1, source_target_pairs={{0,2},{8,10},{32,34},{40,42},{64,66},{72,74},{96,98},{104,106},{1,... | collective-permute-start | bytes 319496 | tf_op jit(solution)/shard_map/ppermute | solution.py:34
  79.9 6.7 %collective-permute-start.19 = (f32[8,13,256]{2,1,0:T(8,128)S(1)}, f32[8,13,256]{2,1,0:T(8,128)S(1)}, u32[]{:S(2)}, u32[]{:S(2)}) collective-permute-start(f32[8,13,256]{2,1,0:T(8,128)S(1)} %get-tuple-element.69.refs_0_.refs_5_), channel_id=1, source_target_pairs={{0,6},{8,14},{32,38},{40,46},{64,70},{72,78},{96,102},{104,110},{1... | collective-permute-start | bytes 319496 | tf_op jit(solution)/shard_map/ppermute | solution.py:34
  86.6 11.1 %collective-permute-start.21 = (f32[8,13,256]{2,1,0:T(8,128)S(1)}, f32[8,13,256]{2,1,0:T(8,128)S(1)}, u32[]{:S(2)}, u32[]{:S(2)}) collective-permute-start(f32[8,13,256]{2,1,0:T(8,128)S(1)} %get-tuple-element.77.refs_0_), channel_id=1, source_target_pairs={{0,16},{8,24},{32,48},{40,56},{64,80},{72,88},{96,112},{104,120},{... | collective-permute-start | bytes 319496 | tf_op jit(solution)/shard_map/ppermute | solution.py:34
  89.5 8.3 %collective-permute-start.22 = (f32[8,13,256]{2,1,0:T(8,128)S(1)}, f32[8,13,256]{2,1,0:T(8,128)S(1)}, u32[]{:S(2)}, u32[]{:S(2)}) collective-permute-start(f32[8,13,256]{2,1,0:T(8,128)S(1)} %get-tuple-element.77.refs_0_), channel_id=1, source_target_pairs={{0,1},{8,9},{32,33},{40,41},{64,65},{72,73},{96,97},{104,105},{1,0... | collective-permute-start | bytes 319496 | tf_op jit(solution)/shard_map/ppermute | solution.py:34
  90.0 7.7 %collective-permute-start.23 = (f32[8,13,256]{2,1,0:T(8,128)S(1)}, f32[8,13,256]{2,1,0:T(8,128)S(1)}, u32[]{:S(2)}, u32[]{:S(2)}) collective-permute-start(f32[8,13,256]{2,1,0:T(8,128)S(1)} %get-tuple-element.77.refs_0_), channel_id=1, source_target_pairs={{0,17},{8,25},{32,49},{40,57},{64,81},{72,89},{96,113},{104,121},{... | collective-permute-start | bytes 319496 | tf_op jit(solution)/shard_map/ppermute | solution.py:34
  91.7 9.4 %collective-permute-start.20 = (f32[256,512]{1,0:T(8,128)S(1)}, f32[256,512]{1,0:T(8,128)S(1)}, u32[]{:S(2)}, u32[]{:S(2)}) collective-permute-start(f32[256,512]{1,0:T(8,128)S(1)} %get-tuple-element.76), channel_id=1, source_target_pairs={{0,8},{8,0},{32,40},{40,32},{64,72},{72,64},{96,104},{104,96},{1,9... | collective-permute-start | bytes 1572872 | tf_op jit(solution)/shard_map/ppermute | solution.py:34
  (4 other events, 18.8 us)
